TPU v7x, 32 devices: a whole 2x2x4 slice. The times are simulated.
32 devices in a mesh: ctx: 8 (over y, x, core), seq: 4 (over z).
Axes of the slice: x: 2, y: 2, z: 4, core: 2. Of those that a mesh axis runs over, the one named last changes fastest.
Arguments:
- layer_input: bfloat16 [16, 2208, 256], P('ctx', 'seq'), may hold values from -6 to 6
- gene_kept: int32 [16, 2208], P('ctx'), may hold values 0 or 1
- attn_gain: bfloat16 [256], replicated, may hold values from 0.5 to 1.5
- attn_shift: bfloat16 [256], replicated, may hold values from -1.5 to 1.5
- w_query: bfloat16 [256, 256], replicated, may hold values from -0.5 to 0.5
- w_key: bfloat16 [256, 256], replicated, may hold values from -0.5 to 0.5
- w_value: bfloat16 [256, 256], replicated, may hold values from -0.375 to 0.375
- w_out: bfloat16 [256, 256], replicated, may hold values from -2 to 2
- out_bias: bfloat16 [256], replicated, may hold values from -1.5 to 1.5
- mlp_gain: bfloat16 [256], replicated, may hold values from 0.5 to 1.5
- mlp_shift: bfloat16 [256], replicated, may hold values from -1.5 to 1.5
- w_up: bfloat16 [256, 1024], replicated, may hold values from -0.375 to 0.375
- up_bias: bfloat16 [1024], replicated, may hold values from -2.5 to 2.5
- w_down: bfloat16 [1024, 256], replicated, may hold values from -0.25 to 0.25
- down_bias: bfloat16 [256], replicated, may hold values from -1.5 to 1.5
- cotangent: float32 [16, 2208, 256], P('ctx', 'seq'), may hold values from -16 to 16
Outputs:
- block_output: bfloat16 [16, 2208, 256], P('ctx', 'seq')
- input_grad: float32 [16, 2208, 256], P('ctx', 'seq')
- grad_attn_gain: float32 [256], replicated
- grad_attn_shift: float32 [256], replicated
- grad_w_query: float32 [256, 256], replicated
- grad_w_key: float32 [256, 256], replicated
- grad_w_value: float32 [256, 256], replicated
- grad_w_out: float32 [256, 256], replicated
- grad_out_bias: float32 [256], replicated
- grad_mlp_gain: float32 [256], replicated
- grad_mlp_shift: float32 [256], replicated
- grad_w_up: float32 [256, 1024], replicated
- grad_up_bias: float32 [1024], replicated
- grad_w_down: float32 [1024, 256], replicated
- grad_down_bias: float32 [256], replicated
All inputs are finite; a program needn't handle non-finite values. No bound on the sum of `gene_kept` on one device may be relied on, other than what follows from the above.
Results may differ from a plain program's by a relative error of at most 0.014.
The roundings to bfloat16 on the way count: a program that leaves them out, or rounds other values in their place, can miss the bound.
Values may be sent and summed in bfloat16 or wider, within the bound.
A program may use at most 128 MiB of HBM per device.

v0:
```python
from functools import partial
import math

import jax
import jax.numpy as jnp
from jax import lax
from jax.sharding import PartitionSpec as P

HEADS = 4
CLS = 8


def layer_norm(rows_in, gain_vec, shift_vec):
    average = jnp.mean(rows_in, axis=-1, keepdims=True)
    centred = rows_in - average
    spread = jnp.mean(centred * centred, axis=-1, keepdims=True)
    return centred * lax.rsqrt(spread + 1e-05) * gain_vec + shift_vec


def exact_gelu(values_in):
    return jax.nn.gelu(values_in, approximate=False)


def to_items(array_in, head_count):
    copy_count, row_count, model_width = array_in.shape
    head_dim = model_width // head_count
    split_heads = array_in.reshape(copy_count, row_count, head_count, head_dim)
    return jnp.transpose(split_heads, (0, 2, 1, 3)).reshape(
        copy_count * head_count, row_count, head_dim
    )


def from_items(items_in, copy_count):
    item_count, row_count, head_dim = items_in.shape
    head_count = item_count // copy_count
    split_heads = items_in.reshape(copy_count, head_count, row_count, head_dim)
    return jnp.transpose(split_heads, (0, 2, 1, 3)).reshape(
        copy_count * row_count, head_count * head_dim
    )


def masked_scores(query_rows, key_rows, usable_keys, score_scale):
    scores = (
        jnp.einsum("qd,kd->qk", query_rows, key_rows, preferred_element_type=jnp.float32)
        * score_scale
    )
    return jnp.where(usable_keys[None, :], scores, -1000000000.0)


def forward_item(operands, score_scale):
    query_rows, key_rows, value_rows, usable_keys = operands
    scores = masked_scores(query_rows, key_rows, usable_keys, score_scale)
    row_max = jnp.max(scores, axis=1, keepdims=True)
    exp_scores = jnp.exp(scores - row_max)
    row_total = jnp.sum(exp_scores, axis=1, keepdims=True)
    probs_low = (exp_scores / row_total).astype(jnp.bfloat16)
    attended = jnp.dot(probs_low, value_rows, preferred_element_type=jnp.float32).astype(
        jnp.bfloat16
    )
    return (attended, (row_max + jnp.log(row_total))[:, 0])


def query_side(operands, score_scale, with_keys):
    query_rows, key_rows, value_rows, usable_keys, grad_rows, log_total = operands
    scores = masked_scores(query_rows, key_rows, usable_keys, score_scale)
    probs = jnp.exp(scores - log_total[:, None])
    grad_probs = jnp.einsum("qd,kd->qk", grad_rows, value_rows, preferred_element_type=jnp.float32)
    delta = jnp.sum(probs * grad_probs, axis=1)
    grad_scores = (probs * (grad_probs - delta[:, None])).astype(jnp.bfloat16)
    grad_query = jnp.dot(grad_scores, key_rows, preferred_element_type=jnp.float32) * score_scale
    grad_keys = (
        jnp.einsum("qk,qd->kd", grad_scores, query_rows, preferred_element_type=jnp.float32)
        * score_scale
    )
    grad_values = jnp.einsum(
        "qk,qd->kd", probs.astype(jnp.bfloat16), grad_rows, preferred_element_type=jnp.float32
    )
    return (grad_query, delta, grad_keys, grad_values)


def body(
    layer_input,
    gene_kept,
    attn_gain,
    attn_shift,
    w_query,
    w_key,
    w_value,
    w_out,
    out_bias,
    mlp_gain,
    mlp_shift,
    w_up,
    up_bias,
    w_down,
    down_bias,
    cotangent,
):
    copy_count, tok_rows, model_width = layer_input.shape
    head_count = HEADS
    seq_count = lax.axis_size("seq")
    ctx_length = tok_rows * seq_count
    row_count = copy_count * tok_rows
    score_scale = 1.0 / math.sqrt(model_width // head_count)
    positions = jnp.arange(ctx_length)
    usable = (gene_kept == 1) | (positions[None, :] < CLS)
    usable_items = jnp.repeat(usable, head_count, axis=0)
    gain_one = attn_gain.astype(jnp.float32)
    shift_one = attn_shift.astype(jnp.float32)
    gain_two = mlp_gain.astype(jnp.float32)
    shift_two = mlp_shift.astype(jnp.float32)
    inputs = layer_input.astype(jnp.float32).reshape(row_count, model_width)
    normed_one, norm_one_back = jax.vjp(layer_norm, inputs, gain_one, shift_one)
    low_one = normed_one.astype(jnp.bfloat16)
    query_low = jnp.dot(low_one, w_query, preferred_element_type=jnp.float32).astype(jnp.bfloat16)
    key_low = jnp.dot(low_one, w_key, preferred_element_type=jnp.float32).astype(jnp.bfloat16)
    value_low = jnp.dot(low_one, w_value, preferred_element_type=jnp.float32).astype(jnp.bfloat16)
    query_shaped = query_low.reshape(copy_count, tok_rows, model_width)
    key_shaped = key_low.reshape(copy_count, tok_rows, model_width)
    value_shaped = value_low.reshape(copy_count, tok_rows, model_width)
    key_all, value_all = (
        lax.all_gather(key_shaped, "seq", axis=1, tiled=True),
        lax.all_gather(value_shaped, "seq", axis=1, tiled=True),
    )
    query_items = to_items(query_shaped, head_count)
    key_items = to_items(key_all, head_count)
    value_items = to_items(value_all, head_count)
    attended_items, log_totals = lax.map(
        partial(forward_item, score_scale=score_scale),
        (query_items, key_items, value_items, usable_items),
    )
    attended_low = from_items(attended_items, copy_count)
    branch = jnp.dot(attended_low, w_out, preferred_element_type=jnp.float32) + out_bias.astype(
        jnp.float32
    )
    middle = inputs + branch
    normed_two, norm_two_back = jax.vjp(layer_norm, middle, gain_two, shift_two)
    low_two = normed_two.astype(jnp.bfloat16)
    hidden = jnp.dot(low_two, w_up, preferred_element_type=jnp.float32) + up_bias.astype(
        jnp.float32
    )
    activated, gelu_back = jax.vjp(exact_gelu, hidden)
    act_low = activated.astype(jnp.bfloat16)
    output = middle + (
        jnp.dot(act_low, w_down, preferred_element_type=jnp.float32) + down_bias.astype(jnp.float32)
    )
    result = output.astype(jnp.bfloat16).reshape(copy_count, tok_rows, model_width)
    grad_output = cotangent.reshape(row_count, model_width)
    grad_low = grad_output.astype(jnp.bfloat16)
    grad_w_down = jnp.einsum("rf,rd->fd", act_low, grad_low, preferred_element_type=jnp.float32)
    grad_down_bias = jnp.sum(grad_low.astype(jnp.float32), axis=0)
    grad_act = jnp.einsum("rd,fd->rf", grad_low, w_down, preferred_element_type=jnp.float32)
    (grad_hidden,) = gelu_back(grad_act)
    hidden_low = grad_hidden.astype(jnp.bfloat16)
    grad_w_up = jnp.einsum("rd,rf->df", low_two, hidden_low, preferred_element_type=jnp.float32)
    grad_up_bias = jnp.sum(hidden_low.astype(jnp.float32), axis=0)
    grad_norm_two = jnp.einsum("rf,df->rd", hidden_low, w_up, preferred_element_type=jnp.float32)
    grad_mid_norm, grad_mlp_gain, grad_mlp_shift = norm_two_back(grad_norm_two)
    grad_middle = grad_output + grad_mid_norm
    middle_low = grad_middle.astype(jnp.bfloat16)
    grad_w_out = jnp.einsum(
        "rd,re->de", attended_low, middle_low, preferred_element_type=jnp.float32
    )
    grad_out_bias = jnp.sum(middle_low.astype(jnp.float32), axis=0)
    grad_att_low = jnp.einsum(
        "re,de->rd", middle_low, w_out, preferred_element_type=jnp.float32
    ).astype(jnp.bfloat16)
    grad_att_shaped = grad_att_low.reshape(copy_count, tok_rows, model_width)
    grad_items = to_items(grad_att_shaped, head_count)
    key_again, value_again = (
        lax.all_gather(key_shaped, "seq", axis=1, tiled=True),
        lax.all_gather(value_shaped, "seq", axis=1, tiled=True),
    )
    key_back_items = to_items(key_again, head_count)
    value_back_items = to_items(value_again, head_count)
    grad_q_items, deltas, grad_k_items, grad_v_items = lax.map(
        partial(query_side, score_scale=score_scale, with_keys=True),
        (query_items, key_back_items, value_back_items, usable_items, grad_items, log_totals),
    )
    key_terms = from_items(grad_k_items, copy_count).reshape(copy_count, ctx_length, model_width)
    value_terms = from_items(grad_v_items, copy_count).reshape(copy_count, ctx_length, model_width)
    summed = lax.psum_scatter(
        jnp.concatenate((key_terms, value_terms), axis=2).astype(jnp.bfloat16),
        "seq",
        scatter_dimension=1,
        tiled=True,
    ).astype(jnp.float32)
    grad_key_low = summed[:, :, :model_width].reshape(row_count, model_width).astype(jnp.bfloat16)
    grad_value_low = summed[:, :, model_width:].reshape(row_count, model_width).astype(jnp.bfloat16)
    grad_query_low = from_items(grad_q_items, copy_count).astype(jnp.bfloat16)
    grad_w_query = jnp.einsum(
        "rd,re->de", low_one, grad_query_low, preferred_element_type=jnp.float32
    )
    grad_w_key = jnp.einsum("rd,re->de", low_one, grad_key_low, preferred_element_type=jnp.float32)
    grad_w_value = jnp.einsum(
        "rd,re->de", low_one, grad_value_low, preferred_element_type=jnp.float32
    )
    grad_norm_one = jnp.einsum(
        "re,de->rd", grad_query_low, w_query, preferred_element_type=jnp.float32
    )
    grad_norm_one = grad_norm_one + jnp.einsum(
        "re,de->rd", grad_key_low, w_key, preferred_element_type=jnp.float32
    )
    grad_norm_one = grad_norm_one + jnp.einsum(
        "re,de->rd", grad_value_low, w_value, preferred_element_type=jnp.float32
    )
    grad_in_norm, grad_attn_gain, grad_attn_shift = norm_one_back(grad_norm_one)
    input_grad = (grad_middle + grad_in_norm).reshape(copy_count, tok_rows, model_width)
    summed_grads = lax.psum(
        (
            grad_attn_gain,
            grad_attn_shift,
            grad_w_query,
            grad_w_key,
            grad_w_value,
            grad_w_out,
            grad_out_bias,
            grad_mlp_gain,
            grad_mlp_shift,
            grad_w_up,
            grad_up_bias,
            grad_w_down,
            grad_down_bias,
        ),
        ("ctx", "seq"),
    )
    return (result, input_grad) + tuple(summed_grads)


def solution(mesh):
    return jax.shard_map(
        body,
        mesh=mesh,
        in_specs=(
            P("ctx", "seq", None),
            P("ctx", None),
            P(),
            P(),
            P(),
            P(),
            P(),
            P(),
            P(),
            P(),
            P(),
            P(),
            P(),
            P(),
            P(),
            P("ctx", "seq", None),
        ),
        out_specs=(
            P("ctx", "seq", None),
            P("ctx", "seq", None),
            P(),
            P(),
            P(),
            P(),
            P(),
            P(),
            P(),
            P(),
            P(),
            P(),
            P(),
            P(),
            P(),
        ),
        check_vma=False,
    )
```

profile of v0, /device:TPU:0, one launch (start us, length us, event | category | flops | bytes accessed | tf_op | source)
XLA Modules:
  0.0 584.5 jit_solution(3380945880968504732)
XLA Ops:
  24.0 43.3 %all-gather.3.cloned.1.call-done = bf16[2,2208,256]{2,1,0:T(8,128)(2,1)} async-done(((bf16[2,552,256]{2,1,0:T(8,128)(2,1)}), bf16[2,2208,256]{2,1,0:T(8,128)(2,1)}) %all-gather.3.cloned.1.call-update) | async-done | bytes 2261008 | tf_op jit(solution)/shard_map/all_gather | solution.py:122
  67.3 3.1 fusion.61
  70.3 13.9 %pad_maximum_fusion.1 = bf16[2,8832,64]{2,1,0:T(8,128)(2,1)} fusion(bf16[2,2208,64]{2,1,0:T(8,128)(2,1)S(1)} %get-tuple-element.214, bf16[2,2208,64]{2,1,0:T(8,128)(2,1)S(1)} %get-tuple-element.215, bf16[2,2208,64]{2,1,0:T(8,128)(2,1)S(1)} %get-tuple-element.216, bf16[2,2208,64]{2,1,0:T(8,128)(2,1)S(1)} %get-tuple-element.213), kind=kLoop, calls=%fused_computation.60 | loop fusion | flops 9043968 | bytes 4521984 | tf_op jit(solution)/shard_map/concatenate
  84.2 32.3 %all-gather.5.cloned.1.call-done = bf16[2,2208,256]{2,1,0:T(8,128)(2,1)} async-done(((bf16[2,552,256]{2,1,0:T(8,128)(2,1)}), bf16[2,2208,256]{2,1,0:T(8,128)(2,1)}) %all-gather.5.cloned.1.call-update) | async-done | bytes 2261008 | tf_op jit(solution)/shard_map/all_gather | solution.py:123
  116.6 3.1 fusion.60
  119.6 14.2 %pad_maximum_fusion.2 = bf16[2,8832,64]{2,1,0:T(8,128)(2,1)} fusion(bf16[2,2208,64]{2,1,0:T(8,128)(2,1)S(1)} %get-tuple-element.210, bf16[2,2208,64]{2,1,0:T(8,128)(2,1)S(1)} %get-tuple-element.211, bf16[2,2208,64]{2,1,0:T(8,128)(2,1)S(1)} %get-tuple-element.212, bf16[2,2208,64]{2,1,0:T(8,128)(2,1)S(1)} %get-tuple-element.209), kind=kLoop, calls=%fused_computation.61 | loop fusion | flops 9043968 | bytes 4521984 | tf_op jit(solution)/shard_map/concatenate.2
  133.8 43.5 %while.26 = (s32[]{:T(128)}, bf16[8,552,64]{1,2,0:T(8,128)(2,1)S(1)}, f32[8,552]{1,0:T(8,128)S(1)}, pred[8,2208]{1,0:T(8,128)(4,1)S(1)}, bf16[8,552,64]{2,1,0:T(...) while((s32[]{:T(128)}, ...), condition=%wide.region_5.6_spmd, body=%wide.region_2.5_spmd.sunk | while | flops 321802208 | bytes 16230541 | solution.py:128
  183.2 12.1 %multiply_convert_fusion.1 = (bf16[1104,1024]{1,0:T(8,128)(2,1)}, f32[1104,1024]{1,0:T(8,128)S(1)}, f32[1104,1024]{1,0:T(8,128)S(1)}) fusion(f32[1024]{0:T(1024)S(1)} %convert_element_type.133, bf16[256,1024]{1,0:T(8,128)(2,1)S(1)} %copy-done, f32[1104,256]{1,0:T(8,128)S(1)} %get-tuple-element.224, f32[256]{0:T(256)S(1)} %convert_element_type.131, ...), kind=kOutput, calls=%fused_computation.64 | convolution fusion | flops 654839808 | bytes 12974720 | tf_op jit(solution)/shard_map/dot_general | solution.py:139
  205.4 2.8 reshape_reshape.15
  208.3 3.1 copy.64
  211.4 99.8 %while.27 = (s32[]{:T(128)}, bf16[8,552,64]{1,2,0:T(8,128)(2,1)}, bf16[8,2208,64]{1,2,0:T(8,128)(2,1)}, bf16[8,2208,64]{1,2,0:T(8,128)(2,1)}, pred[8,2208]{1,0:T...) while((s32[]{:T(128)}, bf16[8,552,64]{1,2,0:T(8,128)(2,1)}, ...), condition=%wide.region_12.13_spmd, body=%wide.region_10.12_spmd.sunk | while | flops 791187712 | bytes 40191868 | solution.py:176
  213.4 2.7 multiply_reduce_fusion.8
  225.9 2.7 multiply_reduce_fusion.8
  238.4 2.7 multiply_reduce_fusion.8
  250.8 2.7 multiply_reduce_fusion.8
  311.2 4.9 pad_maximum_fusion
  316.1 12.5 %copy.65 = bf16[2,2208,512]{2,0,1:T(2,128)(2,1)} copy(bf16[2,2208,512]{1,2,0:T(8,128)(2,1)} %pad_maximum_fusion) | data formatting | bytes 9043968
  328.6 5.8 copy.68
  339.0 2.8 convert_element_type.144
  353.5 62.0 %reduce-scatter.4.cloned.1.call-done = bf16[552,1024]{1,0:T(8,128)(2,1)} async-done(((bf16[2208,1024]{1,0:T(8,128)(2,1)}), bf16[552,1024]{1,0:T(8,128)(2,1)}) %reduce-scatter.4.cloned.1.call-update) | async-done | bytes 1130512
  415.6 3.9 reshape.287
  427.7 2.8 add_add_fusion
  432.0 41.2 %all-reduce = (f32[256]{0:T(256)}, f32[256]{0:T(256)}, f32[256]{0:T(256)}, f32[256]{0:T(256)}, f32[256]{0:T(256)}, /*index=5*/f32[1024]{0:T(1024)}, f32[256]{0:T(256)}) all-reduce(f32[256]{0:T(256)S(1)} %get-tuple-element.148, f32[256]{0:T(256)S(1)} %get-tuple-element.151, ...), channel_id=1, replica_groups=mesh['ctx'=8,'seq'=4] {'ctx','seq'}, use_global_device_ids=true, to_apply=%region_17.18 | all-reduce | flops 2560 | bytes 20480 | tf_op jit(solution)/shard_map/psum | solution.py:209
  475.9 92.8 %all-reduce.4.cloned.1.call-done = (f32[256,256]{1,0:T(8,128)}, f32[256,256]{1,0:T(8,128)}, f32[256,256]{1,0:T(8,128)}, f32[256,256]{1,0:T(8,128)}, f32[256,1024]{1,0:T(8,128)}, /*index=5*/f32[1024,256]{1,0:T(8,128)}) async-done(((f32[256,256]{1,0:T(8,128)}, f32[256,256]{1,0:T(8,128)}, f32[256,256]{1,0:T(8,128)}, f32[256,256]{1,0:T(8,128)}, f32[256,1024]{1,0:T(8,128)}, /*index=5*/f32[1024,256]{1,0:T(8,128)}), ...) | async-done | bytes 3145744 | tf_op jit(solution)/shard_map/psum | solution.py:209
  (297 shorter events, 201.7 us)
Async XLA Ops:
  7.2 176.0 %copy-start = (bf16[256,1024]{1,0:T(8,128)(2,1)S(1)}, bf16[256,1024]{1,0:T(8,128)(2,1)}, u32[]{:S(2)}) copy-start(bf16[256,1024]{1,0:T(8,128)(2,1)} %param.31) | copy-start | bytes 1572868
  7.2 7.2 %copy-start.24 = (bf16[256,256]{1,0:T(8,128)(2,1)S(1)}, bf16[256,256]{1,0:T(8,128)(2,1)}, u32[]{:S(2)}) copy-start(bf16[256,256]{1,0:T(8,128)(2,1)} %param.25) | copy-start | bytes 393220
  7.2 8.4 %copy-start.26 = (bf16[256,256]{1,0:T(8,128)(2,1)S(1)}, bf16[256,256]{1,0:T(8,128)(2,1)}, u32[]{:S(2)}) copy-start(bf16[256,256]{1,0:T(8,128)(2,1)} %param.26) | copy-start | bytes 393220
  7.2 60.0 %all-gather.3.cloned.1.call-start = ((), (), s32[]{:S(2)}) async-start(), calls=%async_computation.1 | async-start | bytes 2826240 | tf_op jit(solution)/shard_map/all_gather | solution.py:122
  10.2 6.5 %copy-start.28 = (f32[1104]{0:T(1024)}, f32[1104]{0:T(1024)S(1)}, u32[]{:S(2)}) copy-start(f32[1104]{0:T(1024)S(1)} %div.47) | copy-start | bytes 13252
  10.9 5.9 %copy-start.38 = (f32[256]{0:T(256)}, f32[256]{0:T(256)S(1)}, u32[]{:S(2)}) copy-start(f32[256]{0:T(256)S(1)} %convert_element_type.123) | copy-start | bytes 3076
  11.6 5.2 copy-start.40
  15.5 101.0 %all-gather.5.cloned.1.call-start = ((), (), s32[]{:S(2)}) async-start(), calls=%async_computation.2 | async-start | bytes 2826240 | tf_op jit(solution)/shard_map/all_gather | solution.py:123
  16.8 398.8 %reduce-scatter.4.cloned.1.call-start = ((), (), s32[]{:S(2)}) async-start(), calls=%async_computation.3 | async-start | bytes 5652480
  18.2 4.3 copy-start.3
  119.6 14.2 %copy-start.17 = (bf16[8,552,64]{1,2,0:T(8,128)(2,1)S(1)}, bf16[8,552,64]{1,2,0:T(8,128)(2,1)}, u32[]{:S(2)}) copy-start(bf16[8,552,64]{1,2,0:T(8,128)(2,1)} %custom-call) | copy-start | bytes 1695748
  183.2 12.2 %copy-start.19 = (bf16[1104,256]{1,0:T(8,128)(2,1)S(1)}, bf16[1104,256]{1,0:T(8,128)(2,1)}, u32[]{:S(2)}) copy-start(bf16[1104,256]{1,0:T(8,128)(2,1)} %get-tuple-element.218) | copy-start | bytes 1695748
  183.2 12.2 %copy-start.45 = (bf16[1024,256]{1,0:T(8,128)(2,1)S(1)}, bf16[1024,256]{1,0:T(8,128)(2,1)}, u32[]{:S(2)}) copy-start(bf16[1024,256]{1,0:T(8,128)(2,1)} %param.33) | copy-start | bytes 1572868
  334.5 234.2 %all-reduce.4.cloned.1.call-start = ((), (), s32[]{:S(2)}) async-start(), calls=%async_computation.4 | async-start | bytes 6291456 | tf_op jit(solution)/shard_map/psum | solution.py:209
  339.0 7.6 %copy-start.22 = (bf16[256,256]{1,0:T(8,128)(2,1)S(1)}, bf16[256,256]{1,0:T(8,128)(2,1)}, u32[]{:S(2)}) copy-start(bf16[256,256]{1,0:T(8,128)(2,1)} %param.24) | copy-start | bytes 393220
  341.8 4.8 copy-start.6
  341.8 6.1 %copy-start.20 = (bf16[1104,256]{1,0:T(8,128)(2,1)S(1)}, bf16[1104,256]{1,0:T(8,128)(2,1)}, u32[]{:S(2)}) copy-start(bf16[1104,256]{1,0:T(8,128)(2,1)} %get-tuple-element.218) | copy-start | bytes 1695748
  341.8 6.1 %copy-start.51 = (bf16[1104,1024]{1,0:T(8,128)(2,1)S(1)}, bf16[1104,1024]{1,0:T(8,128)(2,1)}, u32[]{:S(2)}) copy-start(bf16[1104,1024]{1,0:T(8,128)(2,1)} %get-tuple-element.203) | copy-start | bytes 6782980
  427.1 4.9 copy-start.42
  427.1 4.9 copy-start.44
  427.1 46.2 %copy-start.5 = (f32[1104,256]{1,0:T(8,128)S(1)}, f32[1104,256]{1,0:T(8,128)}, u32[]{:S(2)}) copy-start(f32[1104,256]{1,0:T(8,128)} %copy-done.4) | copy-start | bytes 3391492
  568.7 6.9 %copy-start.16 = (f32[256,1024]{1,0:T(8,128)S(1)}, f32[256,1024]{1,0:T(8,128)}, u32[]{:S(2)}) copy-start(f32[256,1024]{1,0:T(8,128)} %get-tuple-element.413) | copy-start | bytes 3145732
  568.7 7.9 %copy-start.15 = (f32[1024,256]{1,0:T(8,128)S(1)}, f32[1024,256]{1,0:T(8,128)}, u32[]{:S(2)}) copy-start(f32[1024,256]{1,0:T(8,128)} %get-tuple-element.415) | copy-start | bytes 3145732
  572.2 5.3 copy-start.1
  (32 other events, 71.9 us)
Sparse Core Ops, SparseCore 0:
  15.7 51.5 all-gather.2
  68.8 47.7 all-gather.4
  334.6 80.8 reduce-scatter.3
  427.2 141.4 all-reduce.3
where the time goes:
time: 596 us; the launch traced here: 584 us
  waiting for transfers between devices  230 us (39%)
  matrix products  170 us (29%)
  local copies, waits for them, and re-layouts  66.6 us (11%)
  other arithmetic  61.1 us (10%)
  blocking collectives  41.2 us (7%)
  between operations  14.8 us (2%)
    psum x1, waiting for transfers between devices, body(): lax.psum((grad_attn_gain, grad_attn_shift, grad_w_query, grad_w_key, grad...  92.8 us
    unnamed x5, waiting for transfers between devices  62.1 us
    all_gather x1, waiting for transfers between devices, body(): lax.all_gather(key_shaped, 'seq', axis=1, tiled=True)  43.3 us
    psum x1, blocking collectives, body(): lax.psum((grad_attn_gain, grad_attn_shift, grad_w_query, grad_w_key, grad...  41.2 us
    dot_general x16, matrix products, masked_scores(): jnp.einsum('qd,kd->qk', query_rows, key_rows, preferred_element_type=jnp....  39.1 us
    unnamed x114, local copies, waits for them, and re-layouts  38 us
    all_gather x1, waiting for transfers between devices, body(): lax.all_gather(value_shaped, 'seq', axis=1, tiled=True)  32.3 us
    dot_general x8, matrix products, query_side(): jnp.dot(grad_scores, key_rows, preferred_element_type=jnp.float32)  20.9 us
  transfers between devices with their start and end apart: 4, of which 4 were waited for; matrix products, arithmetic and copies ran while one was open for 9% of the time, Pallas kernels for 0%

commit v1 on v0

v1 whole, which is shorter than its diff:
```python
import math
from functools import partial

import jax
import jax.numpy as jnp
from jax import lax
from jax.experimental import pallas as pl
from jax.experimental.pallas import tpu as pltpu
from jax.sharding import PartitionSpec as P

bf16 = jnp.bfloat16
f32 = jnp.float32
HEADS = 4
CLS = 8
TILE = 256
MASKED = -8.0e9
NN = (((1,), (0,)), ((), ()))
NT = (((1,), (1,)), ((), ()))
TN = (((0,), (0,)), ((), ()))
TT = (((0,), (1,)), ((), ()))
MESH = pl.DeviceIdType.MESH


def mm(a, b, dims=NN):
    return lax.dot_general(a, b, dims, preferred_element_type=f32)


def norm_parts(z):
    average = jnp.mean(z, axis=-1, keepdims=True)
    centred = z - average
    spread = jnp.mean(centred * centred, axis=-1, keepdims=True)
    rstd = lax.rsqrt(spread + 1e-05)
    return centred * rstd, rstd


def norm_back(f, n, rstd):
    mean_f = jnp.mean(f, axis=-1, keepdims=True)
    mean_fn = jnp.mean(f * n, axis=-1, keepdims=True)
    return rstd * (f - mean_f - n * mean_fn)


def normal_parts(u):
    bell = jnp.exp2(u * u * (-0.5 * math.log2(math.e)))
    t = 1.0 / (1.0 + (0.3275911 / math.sqrt(2.0)) * jnp.abs(u))
    poly = 1.061405429 * t - 1.453152027
    poly = poly * t + 1.421413741
    poly = poly * t - 0.284496736
    poly = (poly * t + 0.254829592) * t
    tail = 0.5 * poly * bell
    return jnp.where(u < 0, tail, 1.0 - tail), bell * (1.0 / math.sqrt(2.0 * math.pi))


def colsum(z):
    return jnp.sum(z, axis=0, keepdims=True)


def layer_kernel(
    x_ref, keep_ref, cot_ref,
    ag_ref, as_ref, wq_ref, wk_ref, wv_ref, wo_ref, ob_ref,
    mg_ref, ms_ref, wu_ref, ub_ref, wd_ref, db_ref,
    out_ref, dmid_ref, esib_ref, eown_ref, grads_ref, small_ref,
    n_ref, qaug, kaug, vaug, kt, vtaug, prob, s_ref, ot_ref, rl_ref,
    att_t, att, nt_ref, act_ref, gh_ref, gml_ref, gaug, gatt_t, dk_ref, dv_ref,
):
    rows, width = x_ref.shape
    own = rows // 2
    hd = width // HEADS
    pairs = HEADS // 2
    pw = 2 * hd
    head_cols = qaug.shape[2] // 2
    cols = 2 * head_cols
    tiles = cols // TILE
    scale = 1.0 / math.sqrt(hd)
    expo = scale * math.log2(math.e)
    ff = wu_ref.shape[1]
    chunk = own // 3

    gain = ag_ref[...].astype(f32)
    shift = as_ref[...].astype(f32)

    def norm_rows(i, carry):
        at = pl.ds(pl.multiple_of(i * chunk, 16), chunk)
        n, _ = norm_parts(x_ref[at, :].astype(f32))
        low = (n * gain + shift).astype(bf16)
        n_ref[at, :] = low
        k = mm(low, wk_ref[...]).astype(bf16)
        v = mm(low, wv_ref[...]).astype(bf16)
        for p in range(pairs):
            kaug[p, at, 0:pw] = k[:, p * pw:(p + 1) * pw]
            vaug[p, at, 0:pw] = v[:, p * pw:(p + 1) * pw]
        return carry

    lax.fori_loop(0, rows // chunk, norm_rows, 0)
    lane = lax.broadcasted_iota(jnp.int32, (rows, pw), 1)
    bias = jnp.where(lane == 0, keep_ref[...], 0.0).astype(bf16)
    ones = jnp.where(lane < 2, 1.0, 0.0).astype(bf16)
    for p in range(pairs):
        kaug[p, :, pw:2 * pw] = bias
        vaug[p, :, pw:2 * pw] = ones
    sub = lax.broadcasted_iota(jnp.int32, (16, rows), 0)
    kt[...] = mm(wk_ref[...], n_ref[...], TT).astype(bf16)
    vt = mm(wv_ref[...], n_ref[...], TT).astype(bf16)
    for p in range(pairs):
        vtaug[p, 0:pw, :] = vt[p * pw:(p + 1) * pw, :]
        vtaug[p, pw:pw + 16, :] = jnp.where(sub == 0, 1.0, 0.0).astype(bf16)
    qt = mm(wq_ref[...], n_ref[0:own, :], TT).astype(bf16)
    qaug[...] = jnp.zeros_like(qaug)
    gaug[...] = jnp.zeros_like(gaug)
    sub = lax.broadcasted_iota(jnp.int32, (16, cols), 0)
    for p in range(pairs):
        for h in range(2):
            qaug[p, h * hd:(h + 1) * hd, h * head_cols:h * head_cols + own] = qt[p * pw + h * hd:p * pw + (h + 1) * hd, :]
        qaug[p, pw:pw + 16, :] = jnp.where(sub == 0, 1.0, 0.0).astype(bf16)

    def forward(i, carry):
        p = i // tiles
        at = pl.ds(pl.multiple_of((i % tiles) * TILE, TILE), TILE)
        s_ref[...] = mm(kaug[p], qaug[p, :, at])
        top = jnp.max(s_ref[...], axis=0, keepdims=True)
        prob[p, :, at] = jnp.exp2((s_ref[...] - top) * expo).astype(bf16)
        o = mm(vtaug[p], prob[p, :, at])
        rl = 1.0 / o[pw:pw + 1]
        ot_ref[p, :, at] = o[0:pw] * rl
        rl_ref[p, :, at] = rl
        return carry

    lax.fori_loop(0, pairs * tiles, forward, 0)
    for p in range(pairs):
        for h in range(2):
            att_t[p * pw + h * hd:p * pw + (h + 1) * hd, :] = ot_ref[
                p, h * hd:(h + 1) * hd, h * head_cols:h * head_cols + own
            ].astype(bf16)
    att[...] = jnp.transpose(att_t[...])

    gain2 = mg_ref[...].astype(f32)
    shift2 = ms_ref[...].astype(f32)
    out_bias = ob_ref[...].astype(f32)
    up_bias = ub_ref[...].astype(f32)
    down_bias = db_ref[...].astype(f32)

    def mlp(i, carry):
        g_up, g_down, g_out, g_gain, g_shift = carry
        at = pl.ds(pl.multiple_of(i * chunk, 16), chunk)
        middle = x_ref[at, :].astype(f32) + (mm(att[at, :], wo_ref[...]) + out_bias)
        n, rstd = norm_parts(middle)
        low = (n * gain2 + shift2).astype(bf16)
        nt_ref[at, :] = low
        hidden = mm(low, wu_ref[...]) + up_bias
        dist, dens = normal_parts(hidden)
        act = (hidden * dist).astype(bf16)
        act_ref[at, :] = act
        out_ref[at, :] = (middle + (mm(act, wd_ref[...]) + down_bias)).astype(bf16)
        cot = cot_ref[at, :]
        gh = ((dist + hidden * dens) * mm(cot, wd_ref[...], NT)).astype(bf16)
        gh_ref[at, :] = gh
        e = mm(gh, wu_ref[...], NT)
        back = norm_back(e * gain2, n, rstd)
        dmid_ref[at, :] = back
        cot = cot.astype(f32)
        gml = (cot + back).astype(bf16)
        gml_ref[at, :] = gml
        return (
            g_up + colsum(gh.astype(f32)), g_down + colsum(cot), g_out + colsum(gml.astype(f32)),
            g_gain + colsum(e * n), g_shift + colsum(e),
        )

    zero = jnp.zeros((1, width), f32)
    sums = lax.fori_loop(0, 3, mlp, (jnp.zeros((1, ff), f32), zero, zero, zero, zero))
    small_ref[0:1, :] = sums[1]
    small_ref[1:2, :] = sums[2]
    small_ref[2:3, :] = sums[3]
    small_ref[3:4, :] = sums[4]
    for j in range(ff // width):
        small_ref[4 + j:5 + j, :] = sums[0][:, j * width:(j + 1) * width]
    grads_ref[0:ff, :] = mm(act_ref[...], cot_ref[...], TN)
    grads_ref[ff:2 * ff, :] = mm(gh_ref[...], nt_ref[...], TN)
    grads_ref[2 * ff:2 * ff + width, :] = mm(att_t[...], gml_ref[...])

    gatt_t[...] = mm(wo_ref[...], gml_ref[...], NT).astype(bf16)
    sub = lax.broadcasted_iota(jnp.int32, (16, own), 0)
    for p in range(pairs):
        for h in range(2):
            lanes = slice(h * head_cols, h * head_cols + own)
            g = gatt_t[p * pw + h * hd:p * pw + (h + 1) * hd, :].astype(f32)
            g = (g * rl_ref[p, :, lanes]).astype(bf16)
            gaug[p, h * hd:(h + 1) * hd, lanes] = g
            delta = -colsum(g.astype(f32) * ot_ref[p, h * hd:(h + 1) * hd, lanes])
            coarse = delta.astype(bf16).astype(f32)
            fine = delta - coarse
            gaug[p, pw:pw + 16, lanes] = jnp.where(sub == 0, coarse, jnp.where(sub == 1, fine, 0.0)).astype(bf16)

    for p in range(pairs):
        dv_ref[:, p * pw:(p + 1) * pw] = mm(prob[p], gaug[p, 0:pw, :], NT).astype(bf16)

    def backward(i, carry):
        p = i // tiles
        at = pl.ds(pl.multiple_of((i % tiles) * TILE, TILE), TILE)
        ds = prob[p, :, at] * mm(vaug[p], gaug[p, :, at]).astype(bf16)
        prob[p, :, at] = ds
        dq = mm(kt[pl.ds(pl.multiple_of(p * pw, pw), pw), :], ds)
        ot_ref[p, :, at] = dq * scale
        return carry

    lax.fori_loop(0, pairs * tiles, backward, 0)
    for p in range(pairs):
        dk_ref[:, p * pw:(p + 1) * pw] = (mm(prob[p], qaug[p, 0:pw, :], NT) * scale).astype(bf16)

    for p in range(pairs):
        for h in range(2):
            att_t[p * pw + h * hd:p * pw + (h + 1) * hd, :] = ot_ref[
                p, h * hd:(h + 1) * hd, h * head_cols:h * head_cols + own
            ].astype(bf16)
    dq = jnp.transpose(att_t[...])
    base = 2 * ff + width
    grads_ref[base:base + width, :] = mm(n_ref[0:own, :], dq, TN)
    grads_ref[base + width:base + 2 * width, :] = mm(n_ref[...], dk_ref[...], TN)
    grads_ref[base + 2 * width:base + 3 * width, :] = mm(n_ref[...], dv_ref[...], TN)
    esib_ref[...] = (mm(dk_ref[own:rows, :], wk_ref[...], NT) + mm(dv_ref[own:rows, :], wv_ref[...], NT)).astype(bf16)
    eown_ref[...] = (
        mm(dq, wq_ref[...], NT) + mm(dk_ref[0:own, :], wk_ref[...], NT) + mm(dv_ref[0:own, :], wv_ref[...], NT)
    )


def final_kernel(x_ref, eown_ref, esib_ref, dmid_ref, ag_ref, res_ref, small_ref):
    n, rstd = norm_parts(x_ref[...].astype(f32))
    e = eown_ref[...] + esib_ref[...].astype(f32)
    small_ref[0:1, :] = colsum(e * n)
    small_ref[1:2, :] = colsum(e)
    res_ref[...] = (dmid_ref[...] + norm_back(e * ag_ref[...].astype(f32), n, rstd)).astype(bf16)


def reduce_kernel(nbits, seqs, g_ref, small_ref, res_ref, sres_ref, acc, send, recv, gat, ssend, srecv, ssem, rsem):
    c = lax.axis_index("ctx")
    s = lax.axis_index("seq")
    rows = g_ref.shape[0]
    bar = pltpu.get_barrier_semaphore()
    for b in range(nbits):
        pl.semaphore_signal(bar, inc=1, device_id=(c ^ (1 << b), s), device_id_type=MESH)
    for d in range(1, seqs):
        pl.semaphore_signal(bar, inc=1, device_id=(c, lax.rem(s + d, seqs)), device_id_type=MESH)
    pl.semaphore_wait(bar, nbits + seqs - 1)
    off = jnp.int32(0)
    size = rows
    roff = 0
    offs = []
    for b in range(nbits):
        half = size // 2
        mine = lax.rem(c // (1 << b), 2)
        peer = (c ^ (1 << b), s)
        src = acc if b else g_ref
        away = pl.multiple_of(off + (1 - mine) * half, 16)
        keep = pl.multiple_of(off + mine * half, 16)
        send[pl.ds(roff, half), :] = src[pl.ds(away, half), :].astype(bf16)
        ssend[b] = (sres_ref if b else small_ref)[...].astype(bf16)
        cp = pltpu.make_async_remote_copy(
            src_ref=send.at[pl.ds(roff, half)], dst_ref=recv.at[pl.ds(roff, half)],
            send_sem=ssem.at[2 * b], recv_sem=rsem.at[2 * b], device_id=peer, device_id_type=MESH)
        cs = pltpu.make_async_remote_copy(
            src_ref=ssend.at[b], dst_ref=srecv.at[b],
            send_sem=ssem.at[2 * b + 1], recv_sem=rsem.at[2 * b + 1], device_id=peer, device_id_type=MESH)
        cp.start()
        cs.start()
        cp.wait()
        cs.wait()
        acc[pl.ds(keep, half), :] = src[pl.ds(keep, half), :] + recv[pl.ds(roff, half), :].astype(f32)
        sres_ref[...] = ssend[b].astype(f32) + srecv[b].astype(f32)
        offs.append((off, half, mine))
        off = keep
        roff += half
        size = half
    piece = size // seqs
    k = 2 * nbits
    send[pl.ds(roff, size), :] = acc[pl.ds(off, size), :].astype(bf16)
    ssend[nbits] = sres_ref[...].astype(bf16)
    cps = []
    for d in range(1, seqs):
        t = lax.rem(s + d, seqs)
        cps.append(pltpu.make_async_remote_copy(
            src_ref=send.at[pl.ds(pl.multiple_of(roff + t * piece, 16), piece)],
            dst_ref=recv.at[pl.ds(roff + (d - 1) * piece, piece)],
            send_sem=ssem.at[k], recv_sem=rsem.at[k], device_id=(c, t), device_id_type=MESH))
        cps.append(pltpu.make_async_remote_copy(
            src_ref=ssend.at[nbits], dst_ref=srecv.at[nbits + d - 1],
            send_sem=ssem.at[k + 1], recv_sem=rsem.at[k + 1], device_id=(c, t), device_id_type=MESH))
        k += 2
    for cp in cps:
        cp.start()
    for cp in cps:
        cp.wait()
    mine_at = pl.multiple_of(off + s * piece, 16)
    total = acc[pl.ds(mine_at, piece), :]
    for d in range(1, seqs):
        total += recv[pl.ds(roff + (d - 1) * piece, piece), :].astype(f32)
    gat[pl.ds(mine_at, piece), :] = total.astype(bf16)
    shares = [ssend[nbits].astype(f32)] + [srecv[nbits + d - 1].astype(f32) for d in range(1, seqs)]
    stotal = jnp.zeros_like(shares[0])
    for o in range(seqs):
        which = lax.rem(s - o + seqs, seqs)
        for d in range(seqs):
            stotal += jnp.where(which == d, shares[d], 0.0)
    sres_ref[...] = stotal
    cps = []
    for d in range(1, seqs):
        t = lax.rem(s + d, seqs)
        cps.append(pltpu.make_async_remote_copy(
            src_ref=gat.at[pl.ds(mine_at, piece)], dst_ref=gat.at[pl.ds(mine_at, piece)],
            send_sem=ssem.at[k], recv_sem=rsem.at[k], device_id=(c, t), device_id_type=MESH))
        k += 1
    for cp in cps:
        cp.start()
    for cp in cps:
        cp.wait()
    for b in reversed(range(nbits)):
        start, half, mine = offs[b]
        keep = pl.ds(pl.multiple_of(start + mine * half, 16), half)
        cp = pltpu.make_async_remote_copy(
            src_ref=gat.at[keep], dst_ref=gat.at[keep],
            send_sem=ssem.at[k], recv_sem=rsem.at[k], device_id=(c ^ (1 << b), s), device_id_type=MESH)
        cp.start()
        cp.wait()
        k += 1
    res_ref[...] = gat[...].astype(f32)


def all_sum(grads, small, nctx, seqs):
    nbits = nctx.bit_length() - 1
    step = 16 * nctx * seqs
    grads = jnp.pad(grads, ((0, -grads.shape[0] % step), (0, 0)))
    rows, width = grads.shape
    nsem = 2 * nbits + 3 * (seqs - 1) + nbits
    vmem = pl.BlockSpec(memory_space=pltpu.VMEM)
    return pl.pallas_call(
        partial(reduce_kernel, nbits, seqs),
        out_shape=(jax.ShapeDtypeStruct(grads.shape, f32), jax.ShapeDtypeStruct(small.shape, f32)),
        in_specs=[vmem, vmem],
        out_specs=(vmem, vmem),
        scratch_shapes=[
            pltpu.VMEM((rows, width), f32), pltpu.VMEM((rows, width), bf16), pltpu.VMEM((rows, width), bf16),
            pltpu.VMEM((rows, width), bf16), pltpu.VMEM((nbits + 1,) + small.shape, bf16),
            pltpu.VMEM((nbits + seqs,) + small.shape, bf16),
            pltpu.SemaphoreType.DMA((nsem,)), pltpu.SemaphoreType.DMA((nsem,)),
        ],
        compiler_params=pltpu.CompilerParams(collective_id=1, has_side_effects=True, vmem_limit_bytes=40 * 2**20),
        name="sum_grads",
    )(grads, small)


def body(nctx, seqs, layer_input, gene_kept, attn_gain, attn_shift, w_query, w_key, w_value, w_out, out_bias,
         mlp_gain, mlp_shift, w_up, up_bias, w_down, down_bias, cotangent):
    copies, tok, width = layer_input.shape
    own = 2 * tok
    rows = 2 * own
    ff = w_up.shape[1]
    c = lax.axis_index("ctx")
    s = lax.axis_index("seq")
    cc = c % 2

    def go(k):
        return [
            (ci * seqs + si, (ci - ci % 2 + si // 2) * seqs + 2 * (ci % 2) + (si + k) % 2)
            for ci in range(nctx) for si in range(seqs)
        ]

    siblings = [(ci, ci ^ 1) for ci in range(nctx)]

    def scatter(local):
        parts = []
        for k in range(2):
            block = lax.dynamic_index_in_dim(local, (s + k) % 2, 0, keepdims=False)
            parts.append(lax.ppermute(block, ("ctx", "seq"), go(k)))
        return jnp.concatenate(parts)

    def gather(held):
        parts = []
        for k in range(2):
            back = [(b, a) for a, b in go(k)]
            parts.append(lax.ppermute(held[k * tok:(k + 1) * tok], ("ctx", "seq"), back))
        return jnp.where(s % 2 == 0, jnp.stack(parts), jnp.stack(parts[::-1]))

    x_own = scatter(layer_input)
    kept_sib = lax.ppermute(gene_kept, "ctx", siblings)
    x_all = jnp.concatenate([x_own, lax.ppermute(x_own, "ctx", siblings)])
    cot_own = scatter(cotangent.astype(bf16))
    usable = (jnp.stack([gene_kept, kept_sib]) == 1) | (jnp.arange(seqs * tok) < CLS)
    row = jnp.where(s // 2 == cc, usable[0], usable[1])
    row = lax.dynamic_index_in_dim(row, s % 2, 0, keepdims=False).reshape(seqs, tok)
    first = s % 2
    order = jnp.stack([2 * cc + first, 2 * cc + 1 - first, 2 * (1 - cc) + first, 2 * (1 - cc) + 1 - first])
    keep = jnp.where(row[order].reshape(rows, 1), 0.0, MASKED).astype(f32)

    vec = lambda v: v.reshape(1, -1)
    vmem = pl.BlockSpec(memory_space=pltpu.VMEM)
    head_cols = -(-own // 128) * 128
    cols = 2 * head_cols
    pairs = HEADS // 2
    grad_rows = 2 * ff + 4 * width
    out, dmid, esib, eown, grads, small = pl.pallas_call(
        layer_kernel,
        out_shape=(
            jax.ShapeDtypeStruct((own, width), bf16),
            jax.ShapeDtypeStruct((own, width), f32),
            jax.ShapeDtypeStruct((own, width), bf16),
            jax.ShapeDtypeStruct((own, width), f32),
            jax.ShapeDtypeStruct((grad_rows, width), f32),
            jax.ShapeDtypeStruct((8, width), f32),
        ),
        in_specs=[vmem] * 16,
        out_specs=(vmem,) * 6,
        scratch_shapes=[
            pltpu.VMEM((rows, width), bf16),
            pltpu.VMEM((pairs, width, cols), bf16),
            pltpu.VMEM((pairs, rows, width), bf16),
            pltpu.VMEM((pairs, rows, width), bf16),
            pltpu.VMEM((width, rows), bf16),
            pltpu.VMEM((pairs, width // 2 + 16, rows), bf16),
            pltpu.VMEM((pairs, rows, cols), bf16),
            pltpu.VMEM((rows, TILE), f32),
            pltpu.VMEM((pairs, width // 2, cols), f32),
            pltpu.VMEM((pairs, 1, cols), f32),
            pltpu.VMEM((width, own), bf16),
            pltpu.VMEM((own, width), bf16),
            pltpu.VMEM((own, width), bf16),
            pltpu.VMEM((own, ff), bf16),
            pltpu.VMEM((own, ff), bf16),
            pltpu.VMEM((own, width), bf16),
            pltpu.VMEM((pairs, width, cols), bf16),
            pltpu.VMEM((width, own), bf16),
            pltpu.VMEM((rows, width), bf16),
            pltpu.VMEM((rows, width), bf16),
        ],
        compiler_params=pltpu.CompilerParams(vmem_limit_bytes=62 * 2**20),
        name="layer",
    )(x_all, keep, cot_own, vec(attn_gain), vec(attn_shift), w_query, w_key, w_value, w_out, vec(out_bias),
      vec(mlp_gain), vec(mlp_shift), w_up, vec(up_bias), w_down, vec(down_bias))
    result = gather(out)
    esib = lax.ppermute(esib, "ctx", siblings)
    back, gains = pl.pallas_call(
        final_kernel,
        out_shape=(jax.ShapeDtypeStruct((own, width), bf16), jax.ShapeDtypeStruct((8, width), f32)),
        in_specs=[vmem] * 5,
        out_specs=(vmem, vmem),
        compiler_params=pltpu.CompilerParams(vmem_limit_bytes=32 * 2**20),
        name="input_grad",
    )(x_own, eown, esib, dmid, vec(attn_gain))
    input_grad = cotangent + gather(back).astype(f32)
    grads, small = all_sum(grads, jnp.concatenate([small, gains]), nctx, seqs)
    up_rows = ff // width
    return (
        result, input_grad, small[8], small[9],
        grads[2 * ff + width:2 * ff + 2 * width], grads[2 * ff + 2 * width:2 * ff + 3 * width],
        grads[2 * ff + 3 * width:2 * ff + 4 * width], grads[2 * ff:2 * ff + width],
        small[1], small[2], small[3], grads[ff:2 * ff].T, small[4:4 + up_rows].reshape(ff),
        grads[0:ff], small[0],
    )


def solution(mesh):
    tokens = P("ctx", "seq", None)
    return jax.shard_map(
        partial(body, mesh.shape["ctx"], mesh.shape["seq"]),
        mesh=mesh,
        in_specs=(tokens, P("ctx", None)) + (P(),) * 13 + (tokens,),
        out_specs=(tokens, tokens) + (P(),) * 13,
        check_vma=False,
    )
```

time: 596 us -> 205 us (0.34)
  the two profiles are of different devices: /device:TPU:0 before, /device:TPU:11 now
where the time goes in v1:
time: 205 us
  Pallas kernels  126 us (61%)
  waiting for transfers between devices  33.5 us (16%)
  starting transfers between devices  21.8 us (11%)
  local copies, waits for them, and re-layouts  15.2 us (7%)
  other arithmetic  7.66 us (4%)
    pallas_call x1, Pallas kernels, body(): pl.pallas_call(layer_kernel, out_shape=(jax.ShapeDtypeStruct((own, width)...  73.8 us
    pallas_call x1, Pallas kernels, all_sum(): pl.pallas_call(partial(reduce_kernel, nbits, seqs), out_shape=(jax.ShapeD...  49.7 us
    ppermute x4, waiting for transfers between devices, gather(): lax.ppermute(held[k * tok:(k + 1) * tok], ('ctx', 'seq'), back)  19 us
    ppermute x4, waiting for transfers between devices, scatter(): parts.append(lax.ppermute(block, ('ctx', 'seq'), go(k)))  14.5 us
    ppermute x4, starting transfers between devices, gather(): lax.ppermute(held[k * tok:(k + 1) * tok], ('ctx', 'seq'), back)  10.4 us
    ppermute x4, starting transfers between devices, scatter(): parts.append(lax.ppermute(block, ('ctx', 'seq'), go(k)))  10.1 us
  transfers between devices with their start and end apart: 11, of which 5 were waited for; matrix products, arithmetic and copies ran while one was open for 9% of the time, Pallas kernels for 0%

profile of v1, /device:TPU:11, one launch (start us, length us, event | category | flops | bytes accessed | tf_op | source)
XLA Modules:
  0.0 204.8 jit_solution(15001407282500397795)
XLA Ops:
  1.4 1.4 convert_element_type.6
  2.9 4.2 %collective-permute-start.4 = (bf16[552,256]{1,0:T(8,128)(2,1)S(1)}, bf16[552,256]{1,0:T(8,128)(2,1)S(1)}, u32[]{:S(2)}, u32[]{:S(2)}) collective-permute-start(bf16[552,256]{1,0:T(8,128)(2,1)S(1)} %get-tuple-element.75), channel_id=1, source_target_pairs={{0,0},{1,1},{2,4},{3,5},{4,2},{5,3},{6,6},{7,7},{8,8},{9,9},{10,12... | collective-permute-start | bytes 847880 | tf_op jit(solution)/shard_map/ppermute | solution.py:370
  7.3 1.7 collective-permute-start.1
  9.0 4.1 %collective-permute-start = (bf16[552,256]{1,0:T(8,128)(2,1)S(1)}, bf16[552,256]{1,0:T(8,128)(2,1)S(1)}, u32[]{:S(2)}, u32[]{:S(2)}) collective-permute-start(bf16[552,256]{1,0:T(8,128)(2,1)S(1)} %get-tuple-element.78), channel_id=1, source_target_pairs={{0,0},{1,1},{2,4},{3,5},{4,2},{5,3},{6,6},{7,7},{8,8},{9,9},{10,12... | collective-permute-start | bytes 847880 | tf_op jit(solution)/shard_map/ppermute | solution.py:370
  17.3 14.5 %collective-permute-done = bf16[552,256]{1,0:T(8,128)(2,1)S(1)} collective-permute-done((bf16[552,256]{1,0:T(8,128)(2,1)S(1)}, bf16[552,256]{1,0:T(8,128)(2,1)S(1)}, u32[]{:S(2)}, u32[]{:S(2)}) %collective-permute-start) | collective-permute-done | bytes 282656 | tf_op jit(solution)/shard_map/ppermute | solution.py:370
  32.7 1.4 select_n.93.keep_ref
  34.1 0.8 pad_maximum_fusion.1.cot_ref
  34.9 1.1 pad_maximum_fusion.x_ref
  36.0 73.8 %layer.1 = (bf16[1104,256]{1,0:T(8,128)(2,1)}, f32[1104,256]{1,0:T(8,128)}, bf16[1104,256]{1,0:T(8,128)(2,1)}, f32[1104,256]{1,0:T(8,128)}, f32[3072,256]{1,0:T(8,128)}, /*index=5*/f32[8,256]{1,0:T(8,128)}) custom-call(bf16[2208,256]{1,0:T(8,128)(2,1)} %pad_maximum_fusion.x_ref, f32[2208,1]{1,0:T(8,128)} %select_n.93.keep_ref, ...), custom_call_target="tpu_custom_call" | custom-call | tf_op jit(solution)/shard_map/layer/pallas_call | solution.py:397
  110.3 1.9 fusion.5
  112.2 5.3 %collective-permute-start.6 = (bf16[552,256]{1,0:T(8,128)(2,1)}, bf16[552,256]{1,0:T(8,128)(2,1)S(1)}, u32[]{:S(2)}, u32[]{:S(2)}) collective-permute-start(bf16[552,256]{1,0:T(8,128)(2,1)} %get-tuple-element.73), channel_id=1, source_target_pairs={{0,0},{1,1},{4,2},{5,3},{2,4},{3,5},{6,6},{7,7},{8,8},{9,9},{12,10... | collective-permute-start | bytes 847880 | tf_op jit(solution)/shard_map/ppermute | solution.py:377
  117.6 8.6 %collective-permute-done.6 = bf16[552,256]{1,0:T(8,128)(2,1)S(1)} collective-permute-done((bf16[552,256]{1,0:T(8,128)(2,1)}, bf16[552,256]{1,0:T(8,128)(2,1)S(1)}, u32[]{:S(2)}, u32[]{:S(2)}) %collective-permute-start.6) | collective-permute-done | bytes 282656 | tf_op jit(solution)/shard_map/ppermute | solution.py:377
  126.2 4.4 %collective-permute-done.7 = bf16[552,256]{1,0:T(8,128)(2,1)} collective-permute-done((bf16[552,256]{1,0:T(8,128)(2,1)S(1)}, bf16[552,256]{1,0:T(8,128)(2,1)}, u32[]{:S(2)}, u32[]{:S(2)}) %collective-permute-start.7) | collective-permute-done | bytes 282656 | tf_op jit(solution)/shard_map/ppermute | solution.py:377
  130.6 1.9 maximum_select_fusion
  132.6 2.1 %input_grad.1 = (bf16[1104,256]{1,0:T(8,128)(2,1)S(1)}, f32[8,256]{1,0:T(8,128)S(1)}) custom-call(bf16[1104,256]{1,0:T(8,128)(2,1)S(1)} %constant_dynamic-update-slice_fusion.x_ref, f32[1104,256]{1,0:T(8,128)S(1)} %copy-done.2, bf16[1104,256]{1,0:T(8,128)(2,1)} %collective-permute-done.8.esib_ref, f32[1104,256]{1,0:T(8,128)S(1)} %copy-done.1, ...), custom_call_target="tpu_custom_call" | custom-call | tf_op jit(solution)/shard_map/input_grad/pallas_call | solution.py:437
  134.8 0.9 fusion.4
  135.6 49.7 %sum_grads.1 = (f32[3072,256]{1,0:T(8,128)S(1)}, f32[16,256]{1,0:T(8,128)S(1)}) custom-call(f32[3072,256]{1,0:T(8,128)S(1)} %copy-done, f32[16,256]{1,0:T(8,128)S(1)} %pad_maximum_fusion.2.small_ref), custom_call_target="tpu_custom_call" | custom-call | tf_op jit(solution)/shard_map/sum_grads/pallas_call | solution.py:332
  186.0 5.0 %collective-permute-start.9 = (bf16[552,256]{1,0:T(8,128)(2,1)}, bf16[552,256]{1,0:T(8,128)(2,1)S(1)}, u32[]{:S(2)}, u32[]{:S(2)}) collective-permute-start(bf16[552,256]{1,0:T(8,128)(2,1)} %get-tuple-element.71), channel_id=1, source_target_pairs={{0,0},{1,1},{4,2},{5,3},{2,4},{3,5},{6,6},{7,7},{8,8},{9,9},{12,10... | collective-permute-start | bytes 847880 | tf_op jit(solution)/shard_map/ppermute | solution.py:377
  191.1 1.5 fusion.2
  193.1 2.5 %copy.33 = f32[256,1024]{1,0:T(8,128)} copy(f32[256,1024]{0,1:T(8,128)} %get-tuple-element.66) | data formatting | bytes 2097152
  195.7 1.0 fusion.3
  196.6 1.6 collective-permute-done.9
  198.2 4.4 %collective-permute-done.10 = bf16[552,256]{1,0:T(8,128)(2,1)} collective-permute-done((bf16[552,256]{1,0:T(8,128)(2,1)}, bf16[552,256]{1,0:T(8,128)(2,1)}, u32[]{:S(2)}, u32[]{:S(2)}) %collective-permute-start.10) | collective-permute-done | bytes 282656 | tf_op jit(solution)/shard_map/ppermute | solution.py:377
  202.6 2.2 %convert_add_fusion = f32[2,552,256]{2,1,0:T(8,128)} fusion(f32[2,552,256]{2,1,0:T(8,128)S(1)} %copy-done.4, bf16[1,552,256]{2,1,0:T(8,128)(2,1)} %bitcast.14, bf16[1,552,256]{2,1,0:T(8,128)(2,1)S(1)} %bitcast.31, pred[]{:T(512)S(6)} %eq.23), kind=kLoop, calls=%fused_computation.2 | loop fusion | flops 1413120 | bytes 2826241 | tf_op jit(solution)/shard_map/add | solution.py:445
  (66 shorter events, 7.8 us)
Async XLA Ops:
  0.6 16.6 %collective-permute-start.3 = (s32[2,2208]{1,0:T(2,128)}, s32[2,2208]{1,0:T(2,128)S(1)}, u32[]{:S(2)}, u32[]{:S(2)}) collective-permute-start(s32[2,2208]{1,0:T(2,128)} %param.17), channel_id=1, source_target_pairs={{0,4},{4,0},{8,12},{12,8},{16,20},{20,16},{24,28},{28,24},{1,5},{5... | collective-permute-start | bytes 53000 | tf_op jit(solution)/shard_map/ppermute | solution.py:381
  1.4 5.8 %copy-start.5 = (bf16[2,552,256]{2,1,0:T(8,128)(2,1)S(1)}, bf16[2,552,256]{2,1,0:T(8,128)(2,1)}, u32[]{:S(2)}) copy-start(bf16[2,552,256]{2,1,0:T(8,128)(2,1)} %param.16) | copy-start | bytes 1695748
  2.8 10.5 %copy-start.9 = (bf16[256]{0:T(256)(128)(2,1)S(1)}, bf16[256]{0:T(256)(128)(2,1)}, u32[]{:S(2)}) copy-start(bf16[256]{0:T(256)(128)(2,1)} %param.18) | copy-start | bytes 1540
  2.8 11.0 %copy-start.10 = (bf16[256]{0:T(256)(128)(2,1)S(1)}, bf16[256]{0:T(256)(128)(2,1)}, u32[]{:S(2)}) copy-start(bf16[256]{0:T(256)(128)(2,1)} %param.19) | copy-start | bytes 1540
  2.8 11.6 %copy-start.11 = (bf16[256]{0:T(256)(128)(2,1)S(1)}, bf16[256]{0:T(256)(128)(2,1)}, u32[]{:S(2)}) copy-start(bf16[256]{0:T(256)(128)(2,1)} %param.24) | copy-start | bytes 1540
  2.8 12.2 %copy-start.12 = (bf16[256]{0:T(256)(128)(2,1)S(1)}, bf16[256]{0:T(256)(128)(2,1)}, u32[]{:S(2)}) copy-start(bf16[256]{0:T(256)(128)(2,1)} %param.25) | copy-start | bytes 1540
  2.8 12.7 %copy-start.13 = (bf16[256]{0:T(256)(128)(2,1)S(1)}, bf16[256]{0:T(256)(128)(2,1)}, u32[]{:S(2)}) copy-start(bf16[256]{0:T(256)(128)(2,1)} %param.26) | copy-start | bytes 1540
  2.8 13.3 %copy-start.14 = (bf16[256]{0:T(256)(128)(2,1)S(1)}, bf16[256]{0:T(256)(128)(2,1)}, u32[]{:S(2)}) copy-start(bf16[256]{0:T(256)(128)(2,1)} %param.30) | copy-start | bytes 1540
  2.8 13.8 %copy-start.8 = (bf16[1024]{0:T(1024)(128)(2,1)S(1)}, bf16[1024]{0:T(1024)(128)(2,1)}, u32[]{:S(2)}) copy-start(bf16[1024]{0:T(1024)(128)(2,1)} %param.28) | copy-start | bytes 6148
  2.9 14.4 %copy-start.6 = (s32[2,2208]{1,0:T(2,128)S(1)}, s32[2,2208]{1,0:T(2,128)}, u32[]{:S(2)}) copy-start(s32[2,2208]{1,0:T(2,128)} %param.17) | copy-start | bytes 52996
  2.9 31.2 %collective-permute-start.4 = (bf16[552,256]{1,0:T(8,128)(2,1)S(1)}, bf16[552,256]{1,0:T(8,128)(2,1)S(1)}, u32[]{:S(2)}, u32[]{:S(2)}) collective-permute-start(bf16[552,256]{1,0:T(8,128)(2,1)S(1)} %get-tuple-element.75), channel_id=1, source_target_pairs={{0,0},{1,1},{2,4},{3,5},{4,2},{5,3},{6,6},{7,7},{8,8},{9,9},{10,12... | collective-permute-start | bytes 847880 | tf_op jit(solution)/shard_map/ppermute | solution.py:370
  7.1 27.0 %collective-permute-start.5 = (bf16[552,256]{1,0:T(8,128)(2,1)S(1)}, bf16[552,256]{1,0:T(8,128)(2,1)S(1)}, u32[]{:S(2)}, u32[]{:S(2)}) collective-permute-start(bf16[552,256]{1,0:T(8,128)(2,1)S(1)} %get-tuple-element.76), channel_id=1, source_target_pairs={{0,1},{1,0},{2,5},{3,4},{4,3},{5,2},{6,7},{7,6},{8,9},{9,8},{10,13... | collective-permute-start | bytes 847880 | tf_op jit(solution)/shard_map/ppermute | solution.py:370
  7.3 24.6 %collective-permute-start.1 = (bf16[552,256]{1,0:T(8,128)(2,1)S(1)}, bf16[552,256]{1,0:T(8,128)(2,1)S(1)}, u32[]{:S(2)}, u32[]{:S(2)}) collective-permute-start(bf16[552,256]{1,0:T(8,128)(2,1)S(1)} %get-tuple-element.77), channel_id=1, source_target_pairs={{0,1},{1,0},{2,5},{3,4},{4,3},{5,2},{6,7},{7,6},{8,9},{9,8},{10,13... | collective-permute-start | bytes 847880 | tf_op jit(solution)/shard_map/ppermute | solution.py:370
  9.0 22.8 %collective-permute-start = (bf16[552,256]{1,0:T(8,128)(2,1)S(1)}, bf16[552,256]{1,0:T(8,128)(2,1)S(1)}, u32[]{:S(2)}, u32[]{:S(2)}) collective-permute-start(bf16[552,256]{1,0:T(8,128)(2,1)S(1)} %get-tuple-element.78), channel_id=1, source_target_pairs={{0,0},{1,1},{2,4},{3,5},{4,2},{5,3},{6,6},{7,7},{8,8},{9,9},{10,12... | collective-permute-start | bytes 847880 | tf_op jit(solution)/shard_map/ppermute | solution.py:370
  31.9 3.1 %collective-permute-start.2 = (bf16[1104,256]{1,0:T(8,128)(2,1)S(1)}, bf16[1104,256]{1,0:T(8,128)(2,1)S(1)}, u32[]{:S(2)}, u32[]{:S(2)}) collective-permute-start(bf16[1104,256]{1,0:T(8,128)(2,1)S(1)} %constant_dynamic-update-slice_fusion.x_ref), channel_id=1, source_target_pairs={{0,4},{4,0},{8,12},{12,8},{16,20},{20,16},{24,28},{28,24},{1,5},{5... | collective-permute-start | bytes 1695752 | tf_op jit(solution)/shard_map/ppermute | solution.py:382
  109.8 22.8 %collective-permute-start.8 = (bf16[1104,256]{1,0:T(8,128)(2,1)}, bf16[1104,256]{1,0:T(8,128)(2,1)}, u32[]{:S(2)}, u32[]{:S(2)}) collective-permute-start(bf16[1104,256]{1,0:T(8,128)(2,1)} %get-tuple-element.27), channel_id=1, source_target_pairs={{0,4},{4,0},{8,12},{12,8},{16,20},{20,16},{24,28},{28,24},{1,5},{5... | collective-permute-start | bytes 1695752 | tf_op jit(solution)/shard_map/ppermute | solution.py:436
  110.3 22.3 %copy-start.1 = (f32[1104,256]{1,0:T(8,128)S(1)}, f32[1104,256]{1,0:T(8,128)}, u32[]{:S(2)}) copy-start(f32[1104,256]{1,0:T(8,128)} %get-tuple-element.28.dmid_ref) | copy-start | bytes 3391492
  110.3 22.3 %copy-start.2 = (f32[1104,256]{1,0:T(8,128)S(1)}, f32[1104,256]{1,0:T(8,128)}, u32[]{:S(2)}) copy-start(f32[1104,256]{1,0:T(8,128)} %get-tuple-element.26.eown_ref) | copy-start | bytes 3391492
  110.3 22.3 %copy-start.3 = (bf16[1,256]{1,0:T(2,128)(2,1)S(1)}, bf16[1,256]{1,0:T(2,128)(2,1)}, u32[]{:S(2)}) copy-start(bf16[1,256]{1,0:T(2,128)(2,1)} %reshape.245.ag_ref) | copy-start | bytes 1540
  112.2 14.0 %collective-permute-start.6 = (bf16[552,256]{1,0:T(8,128)(2,1)}, bf16[552,256]{1,0:T(8,128)(2,1)S(1)}, u32[]{:S(2)}, u32[]{:S(2)}) collective-permute-start(bf16[552,256]{1,0:T(8,128)(2,1)} %get-tuple-element.73), channel_id=1, source_target_pairs={{0,0},{1,1},{4,2},{5,3},{2,4},{3,5},{6,6},{7,7},{8,8},{9,9},{12,10... | collective-permute-start | bytes 847880 | tf_op jit(solution)/shard_map/ppermute | solution.py:377
  117.5 13.1 %collective-permute-start.7 = (bf16[552,256]{1,0:T(8,128)(2,1)S(1)}, bf16[552,256]{1,0:T(8,128)(2,1)}, u32[]{:S(2)}, u32[]{:S(2)}) collective-permute-start(bf16[552,256]{1,0:T(8,128)(2,1)S(1)} %get-tuple-element.74), channel_id=1, source_target_pairs={{1,0},{0,1},{5,2},{4,3},{3,4},{2,5},{7,6},{6,7},{9,8},{8,9},{13,10... | collective-permute-start | bytes 847880 | tf_op jit(solution)/shard_map/ppermute | solution.py:377
  186.0 12.3 %collective-permute-start.9 = (bf16[552,256]{1,0:T(8,128)(2,1)}, bf16[552,256]{1,0:T(8,128)(2,1)S(1)}, u32[]{:S(2)}, u32[]{:S(2)}) collective-permute-start(bf16[552,256]{1,0:T(8,128)(2,1)} %get-tuple-element.71), channel_id=1, source_target_pairs={{0,0},{1,1},{4,2},{5,3},{2,4},{3,5},{6,6},{7,7},{8,8},{9,9},{12,10... | collective-permute-start | bytes 847880 | tf_op jit(solution)/shard_map/ppermute | solution.py:377
  191.0 11.6 %collective-permute-start.10 = (bf16[552,256]{1,0:T(8,128)(2,1)}, bf16[552,256]{1,0:T(8,128)(2,1)}, u32[]{:S(2)}, u32[]{:S(2)}) collective-permute-start(bf16[552,256]{1,0:T(8,128)(2,1)} %get-tuple-element.72), channel_id=1, source_target_pairs={{1,0},{0,1},{5,2},{4,3},{3,4},{2,5},{7,6},{6,7},{9,8},{8,9},{13,10... | collective-permute-start | bytes 847880 | tf_op jit(solution)/shard_map/ppermute | solution.py:377
  195.7 6.9 %copy-start.4 = (f32[2,552,256]{2,1,0:T(8,128)S(1)}, f32[2,552,256]{2,1,0:T(8,128)}, u32[]{:S(2)}) copy-start(f32[2,552,256]{2,1,0:T(8,128)} %param.31) | copy-start | bytes 3391492
  (2 other events, 3.9 us)

commit v2 on v1

--- a/solution.py
+++ b/solution.py
@@ -58,12 +58,18 @@
     x_ref, keep_ref, cot_ref,
     ag_ref, as_ref, wq_ref, wk_ref, wv_ref, wo_ref, ob_ref,
     mg_ref, ms_ref, wu_ref, ub_ref, wd_ref, db_ref,
-    out_ref, dmid_ref, esib_ref, eown_ref, grads_ref, small_ref,
+    out_ref, back_ref, grads_ref, small_ref,
+    erecv_ref, esend_sem, erecv_sem,
     n_ref, qaug, kaug, vaug, kt, vtaug, prob, s_ref, ot_ref, rl_ref,
-    att_t, att, nt_ref, act_ref, gh_ref, gml_ref, gaug, gatt_t, dk_ref, dv_ref,
+    att_t, att, act_ref, gh_ref, gml_ref, gaug,
 ):
     rows, width = x_ref.shape
     own = rows // 2
+    ctx = lax.axis_index("ctx")
+    sibling = (ctx + 1 - 2 * lax.rem(ctx, 2), lax.axis_index("seq"))
+    barrier = pltpu.get_barrier_semaphore()
+    pl.semaphore_signal(barrier, inc=1, device_id=sibling, device_id_type=MESH)
+    pl.semaphore_wait(barrier, 1)
     hd = width // HEADS
     pairs = HEADS // 2
     pw = 2 * hd
@@ -75,8 +81,8 @@
     ff = wu_ref.shape[1]
     chunk = own // 3
 
-    gain = ag_ref[...].astype(f32)
-    shift = as_ref[...].astype(f32)
+    gain = ag_ref[...].astype(f32).reshape(1, -1)
+    shift = as_ref[...].astype(f32).reshape(1, -1)
 
     def norm_rows(i, carry):
         at = pl.ds(pl.multiple_of(i * chunk, 16), chunk)
@@ -92,7 +98,10 @@
 
     lax.fori_loop(0, rows // chunk, norm_rows, 0)
     lane = lax.broadcasted_iota(jnp.int32, (rows, pw), 1)
-    bias = jnp.where(lane == 0, keep_ref[...], 0.0).astype(bf16)
+    sub = lax.broadcasted_iota(jnp.int32, (16, rows), 0)
+    marks = jnp.where(sub == 0, keep_ref[...], 0.0).astype(bf16)
+    unit = jnp.where(lax.broadcasted_iota(jnp.int32, (16, pw), 0) == lax.broadcasted_iota(jnp.int32, (16, pw), 1), 1.0, 0.0)
+    bias = mm(marks, unit.astype(bf16), TN).astype(bf16)
     ones = jnp.where(lane < 2, 1.0, 0.0).astype(bf16)
     for p in range(pairs):
         kaug[p, :, pw:2 * pw] = bias
@@ -132,11 +141,11 @@
             ].astype(bf16)
     att[...] = jnp.transpose(att_t[...])
 
-    gain2 = mg_ref[...].astype(f32)
-    shift2 = ms_ref[...].astype(f32)
-    out_bias = ob_ref[...].astype(f32)
-    up_bias = ub_ref[...].astype(f32)
-    down_bias = db_ref[...].astype(f32)
+    gain2 = mg_ref[...].astype(f32).reshape(1, -1)
+    shift2 = ms_ref[...].astype(f32).reshape(1, -1)
+    out_bias = ob_ref[...].astype(f32).reshape(1, -1)
+    up_bias = ub_ref[...].astype(f32).reshape(1, -1)
+    down_bias = db_ref[...].astype(f32).reshape(1, -1)
 
     def mlp(i, carry):
         g_up, g_down, g_out, g_gain, g_shift = carry
@@ -144,7 +153,7 @@
         middle = x_ref[at, :].astype(f32) + (mm(att[at, :], wo_ref[...]) + out_bias)
         n, rstd = norm_parts(middle)
         low = (n * gain2 + shift2).astype(bf16)
-        nt_ref[at, :] = low
+        att[at, :] = low
         hidden = mm(low, wu_ref[...]) + up_bias
         dist, dens = normal_parts(hidden)
         act = (hidden * dist).astype(bf16)
@@ -155,7 +164,7 @@
         gh_ref[at, :] = gh
         e = mm(gh, wu_ref[...], NT)
         back = norm_back(e * gain2, n, rstd)
-        dmid_ref[at, :] = back
+        s_ref[at, :] = back
         cot = cot.astype(f32)
         gml = (cot + back).astype(bf16)
         gml_ref[at, :] = gml
@@ -173,15 +182,14 @@
     for j in range(ff // width):
         small_ref[4 + j:5 + j, :] = sums[0][:, j * width:(j + 1) * width]
     grads_ref[0:ff, :] = mm(act_ref[...], cot_ref[...], TN)
-    grads_ref[ff:2 * ff, :] = mm(gh_ref[...], nt_ref[...], TN)
+    grads_ref[ff:2 * ff, :] = mm(gh_ref[...], att[...], TN)
     grads_ref[2 * ff:2 * ff + width, :] = mm(att_t[...], gml_ref[...])
 
-    gatt_t[...] = mm(wo_ref[...], gml_ref[...], NT).astype(bf16)
     sub = lax.broadcasted_iota(jnp.int32, (16, own), 0)
     for p in range(pairs):
         for h in range(2):
             lanes = slice(h * head_cols, h * head_cols + own)
-            g = gatt_t[p * pw + h * hd:p * pw + (h + 1) * hd, :].astype(f32)
+            g = mm(wo_ref[p * pw + h * hd:p * pw + (h + 1) * hd, :], gml_ref[...], NT).astype(bf16).astype(f32)
             g = (g * rl_ref[p, :, lanes]).astype(bf16)
             gaug[p, h * hd:(h + 1) * hd, lanes] = g
             delta = -colsum(g.astype(f32) * ot_ref[p, h * hd:(h + 1) * hd, lanes])
@@ -190,7 +198,9 @@
             gaug[p, pw:pw + 16, lanes] = jnp.where(sub == 0, coarse, jnp.where(sub == 1, fine, 0.0)).astype(bf16)
 
     for p in range(pairs):
-        dv_ref[:, p * pw:(p + 1) * pw] = mm(prob[p], gaug[p, 0:pw, :], NT).astype(bf16)
+        for half in range(2):
+            lanes = slice(half * width + p * pw, half * width + (p + 1) * pw)
+            act_ref[:, lanes] = mm(prob[p, half * own:(half + 1) * own, :], gaug[p, 0:pw, :], NT).astype(bf16)
 
     def backward(i, carry):
         p = i // tiles
@@ -203,30 +213,55 @@
 
     lax.fori_loop(0, pairs * tiles, backward, 0)
     for p in range(pairs):
-        dk_ref[:, p * pw:(p + 1) * pw] = (mm(prob[p], qaug[p, 0:pw, :], NT) * scale).astype(bf16)
-
+        for half in range(2):
+            lanes = slice(half * width + p * pw, half * width + (p + 1) * pw)
+            gh_ref[:, lanes] = (mm(prob[p, half * own:(half + 1) * own, :], qaug[p, 0:pw, :], NT) * scale).astype(bf16)
+
+    dv_own, dv_sib = act_ref.at[:, 0:width], act_ref.at[:, width:2 * width]
+    dk_own, dk_sib = gh_ref.at[:, 0:width], gh_ref.at[:, width:2 * width]
+
+    def other_rows(i, carry):
+        at = pl.ds(pl.multiple_of(i * chunk, 16), chunk)
+        gml_ref[at, :] = (mm(dk_sib[at, :], wk_ref[...], NT) + mm(dv_sib[at, :], wv_ref[...], NT)).astype(bf16)
+        return carry
+
+    lax.fori_loop(0, 3, other_rows, 0)
+    copy = pltpu.make_async_remote_copy(
+        src_ref=gml_ref, dst_ref=erecv_ref, send_sem=esend_sem, recv_sem=erecv_sem,
+        device_id=sibling, device_id_type=MESH)
+    copy.start()
     for p in range(pairs):
         for h in range(2):
             att_t[p * pw + h * hd:p * pw + (h + 1) * hd, :] = ot_ref[
                 p, h * hd:(h + 1) * hd, h * head_cols:h * head_cols + own
             ].astype(bf16)
-    dq = jnp.transpose(att_t[...])
+    att[...] = jnp.transpose(att_t[...])
     base = 2 * ff + width
-    grads_ref[base:base + width, :] = mm(n_ref[0:own, :], dq, TN)
-    grads_ref[base + width:base + 2 * width, :] = mm(n_ref[...], dk_ref[...], TN)
-    grads_ref[base + 2 * width:base + 3 * width, :] = mm(n_ref[...], dv_ref[...], TN)
-    esib_ref[...] = (mm(dk_ref[own:rows, :], wk_ref[...], NT) + mm(dv_ref[own:rows, :], wv_ref[...], NT)).astype(bf16)
-    eown_ref[...] = (
-        mm(dq, wq_ref[...], NT) + mm(dk_ref[0:own, :], wk_ref[...], NT) + mm(dv_ref[0:own, :], wv_ref[...], NT)
-    )
-
-
-def final_kernel(x_ref, eown_ref, esib_ref, dmid_ref, ag_ref, res_ref, small_ref):
-    n, rstd = norm_parts(x_ref[...].astype(f32))
-    e = eown_ref[...] + esib_ref[...].astype(f32)
-    small_ref[0:1, :] = colsum(e * n)
-    small_ref[1:2, :] = colsum(e)
-    res_ref[...] = (dmid_ref[...] + norm_back(e * ag_ref[...].astype(f32), n, rstd)).astype(bf16)
+    grads_ref[base:base + width, :] = mm(n_ref[0:own, :], att[...], TN)
+    grads_ref[base + width:base + 2 * width, :] = mm(n_ref[0:own, :], dk_own[...], TN) + mm(n_ref[own:rows, :], dk_sib[...], TN)
+    grads_ref[base + 2 * width:base + 3 * width, :] = mm(n_ref[0:own, :], dv_own[...], TN) + mm(n_ref[own:rows, :], dv_sib[...], TN)
+
+    def own_rows(i, carry):
+        at = pl.ds(pl.multiple_of(i * chunk, 16), chunk)
+        s_ref[pl.ds(pl.multiple_of(own + i * chunk, 16), chunk), :] = (
+            mm(att[at, :], wq_ref[...], NT) + mm(dk_own[at, :], wk_ref[...], NT) + mm(dv_own[at, :], wv_ref[...], NT)
+        )
+        return carry
+
+    lax.fori_loop(0, 3, own_rows, 0)
+    copy.wait()
+
+    def last_rows(i, carry):
+        at = pl.ds(pl.multiple_of(i * chunk, 16), chunk)
+        n, rstd = norm_parts(x_ref[at, :].astype(f32))
+        e = s_ref[pl.ds(pl.multiple_of(own + i * chunk, 16), chunk), :] + erecv_ref[at, :].astype(f32)
+        back_ref[at, :] = (s_ref[at, :] + norm_back(e * gain, n, rstd)).astype(bf16)
+        return carry[0] + colsum(e * n), carry[1] + colsum(e)
+
+    sums = lax.fori_loop(0, 3, last_rows, (zero, zero))
+    ups = 4 + ff // width
+    small_ref[ups:ups + 1, :] = sums[0]
+    small_ref[ups + 1:ups + 2, :] = sums[1]
 
 
 def reduce_kernel(nbits, seqs, g_ref, small_ref, res_ref, sres_ref, acc, send, recv, gat, ssend, srecv, ssem, rsem):
@@ -386,27 +421,27 @@
     row = lax.dynamic_index_in_dim(row, s % 2, 0, keepdims=False).reshape(seqs, tok)
     first = s % 2
     order = jnp.stack([2 * cc + first, 2 * cc + 1 - first, 2 * (1 - cc) + first, 2 * (1 - cc) + 1 - first])
-    keep = jnp.where(row[order].reshape(rows, 1), 0.0, MASKED).astype(f32)
-
-    vec = lambda v: v.reshape(1, -1)
+    keep = jnp.where(row[order].reshape(1, rows), 0.0, MASKED).astype(f32)
+
     vmem = pl.BlockSpec(memory_space=pltpu.VMEM)
     head_cols = -(-own // 128) * 128
     cols = 2 * head_cols
     pairs = HEADS // 2
     grad_rows = 2 * ff + 4 * width
-    out, dmid, esib, eown, grads, small = pl.pallas_call(
+    out, back, grads, small = pl.pallas_call(
         layer_kernel,
         out_shape=(
             jax.ShapeDtypeStruct((own, width), bf16),
-            jax.ShapeDtypeStruct((own, width), f32),
             jax.ShapeDtypeStruct((own, width), bf16),
-            jax.ShapeDtypeStruct((own, width), f32),
             jax.ShapeDtypeStruct((grad_rows, width), f32),
-            jax.ShapeDtypeStruct((8, width), f32),
+            jax.ShapeDtypeStruct((16, width), f32),
         ),
         in_specs=[vmem] * 16,
-        out_specs=(vmem,) * 6,
+        out_specs=(vmem,) * 4,
         scratch_shapes=[
+            pltpu.VMEM((own, width), bf16),
+            pltpu.SemaphoreType.DMA,
+            pltpu.SemaphoreType.DMA,
             pltpu.VMEM((rows, width), bf16),
             pltpu.VMEM((pairs, width, cols), bf16),
             pltpu.VMEM((pairs, rows, width), bf16),
@@ -419,31 +454,18 @@
             pltpu.VMEM((pairs, 1, cols), f32),
             pltpu.VMEM((width, own), bf16),
             pltpu.VMEM((own, width), bf16),
-            pltpu.VMEM((own, width), bf16),
             pltpu.VMEM((own, ff), bf16),
             pltpu.VMEM((own, ff), bf16),
             pltpu.VMEM((own, width), bf16),
             pltpu.VMEM((pairs, width, cols), bf16),
-            pltpu.VMEM((width, own), bf16),
-            pltpu.VMEM((rows, width), bf16),
-            pltpu.VMEM((rows, width), bf16),
         ],
-        compiler_params=pltpu.CompilerParams(vmem_limit_bytes=62 * 2**20),
+        compiler_params=pltpu.CompilerParams(collective_id=2, has_side_effects=True, vmem_limit_bytes=62 * 2**20),
         name="layer",
-    )(x_all, keep, cot_own, vec(attn_gain), vec(attn_shift), w_query, w_key, w_value, w_out, vec(out_bias),
-      vec(mlp_gain), vec(mlp_shift), w_up, vec(up_bias), w_down, vec(down_bias))
+    )(x_all, keep, cot_own, attn_gain, attn_shift, w_query, w_key, w_value, w_out, out_bias,
+      mlp_gain, mlp_shift, w_up, up_bias, w_down, down_bias)
     result = gather(out)
-    esib = lax.ppermute(esib, "ctx", siblings)
-    back, gains = pl.pallas_call(
-        final_kernel,
-        out_shape=(jax.ShapeDtypeStruct((own, width), bf16), jax.ShapeDtypeStruct((8, width), f32)),
-        in_specs=[vmem] * 5,
-        out_specs=(vmem, vmem),
-        compiler_params=pltpu.CompilerParams(vmem_limit_bytes=32 * 2**20),
-        name="input_grad",
-    )(x_own, eown, esib, dmid, vec(attn_gain))
     input_grad = cotangent + gather(back).astype(f32)
-    grads, small = all_sum(grads, jnp.concatenate([small, gains]), nctx, seqs)
+    grads, small = all_sum(grads, small, nctx, seqs)
     up_rows = ff // width
     return (
         result, input_grad, small[8], small[9],

time: 205 us -> 199 us (0.971)
  the two profiles are of different devices: /device:TPU:11 before, /device:TPU:18 now
where the time goes in v2:
time: 199 us; the launch traced here: 198 us
  Pallas kernels  124 us (62%)
  waiting for transfers between devices  36.9 us (19%)
  starting transfers between devices  19.9 us (10%)
  local copies, waits for them, and re-layouts  10 us (5%)
  other arithmetic  6.84 us (3%)
    pallas_call x1, Pallas kernels, body(): pl.pallas_call(layer_kernel, out_shape=(jax.ShapeDtypeStruct((own, width)...  76.4 us
    pallas_call x1, Pallas kernels, all_sum(): pl.pallas_call(partial(reduce_kernel, nbits, seqs), out_shape=(jax.ShapeD...  47.5 us
    ppermute x4, waiting for transfers between devices, scatter(): parts.append(lax.ppermute(block, ('ctx', 'seq'), go(k)))  19.6 us
    ppermute x4, waiting for transfers between devices, gather(): lax.ppermute(held[k * tok:(k + 1) * tok], ('ctx', 'seq'), back)  16.2 us
    ppermute x4, starting transfers between devices, gather(): lax.ppermute(held[k * tok:(k + 1) * tok], ('ctx', 'seq'), back)  10.6 us
    ppermute x4, starting transfers between devices, scatter(): parts.append(lax.ppermute(block, ('ctx', 'seq'), go(k)))  9.2 us
    unnamed x17, local copies, waits for them, and re-layouts  4.93 us
  transfers between devices with their start and end apart: 10, of which 5 were waited for; matrix products, arithmetic and copies ran while one was open for 4% of the time, Pallas kernels for 0%

profile of v2, /device:TPU:18, one launch (start us, length us, event | category | flops | bytes accessed | tf_op | source)
XLA Modules:
  0.0 198.4 jit_solution(1940099639528306059)
XLA Ops:
  0.7 1.4 convert_element_type.6
  2.2 1.9 collective-permute-start.4
  4.1 2.8 %collective-permute-start.5 = (bf16[552,256]{1,0:T(8,128)(2,1)S(1)}, bf16[552,256]{1,0:T(8,128)(2,1)S(1)}, u32[]{:S(2)}, u32[]{:S(2)}) collective-permute-start(bf16[552,256]{1,0:T(8,128)(2,1)S(1)} %get-tuple-element.53), channel_id=1, source_target_pairs={{0,1},{1,0},{2,5},{3,4},{4,3},{5,2},{6,7},{7,6},{8,9},{9,8},{10,13... | collective-permute-start | bytes 847880 | tf_op jit(solution)/shard_map/ppermute | solution.py:405
  6.9 2.8 %collective-permute-start = (bf16[552,256]{1,0:T(8,128)(2,1)S(1)}, bf16[552,256]{1,0:T(8,128)(2,1)S(1)}, u32[]{:S(2)}, u32[]{:S(2)}) collective-permute-start(bf16[552,256]{1,0:T(8,128)(2,1)S(1)} %get-tuple-element.54), channel_id=1, source_target_pairs={{0,0},{1,1},{2,4},{3,5},{4,2},{5,3},{6,6},{7,7},{8,8},{9,9},{10,12... | collective-permute-start | bytes 847880 | tf_op jit(solution)/shard_map/ppermute | solution.py:405
  9.8 1.7 collective-permute-start.1
  11.6 1.1 collective-permute-done.3
  12.7 13.7 %collective-permute-done = bf16[552,256]{1,0:T(8,128)(2,1)S(1)} collective-permute-done((bf16[552,256]{1,0:T(8,128)(2,1)S(1)}, bf16[552,256]{1,0:T(8,128)(2,1)S(1)}, u32[]{:S(2)}, u32[]{:S(2)}) %collective-permute-start) | collective-permute-done | bytes 282656 | tf_op jit(solution)/shard_map/ppermute | solution.py:405
  26.4 5.9 %collective-permute-done.1 = bf16[552,256]{1,0:T(8,128)(2,1)S(1)} collective-permute-done((bf16[552,256]{1,0:T(8,128)(2,1)S(1)}, bf16[552,256]{1,0:T(8,128)(2,1)S(1)}, u32[]{:S(2)}, u32[]{:S(2)}) %collective-permute-start.1) | collective-permute-done | bytes 282656 | tf_op jit(solution)/shard_map/ppermute | solution.py:405
  33.8 0.8 pad_maximum_fusion.2.cot_ref
  34.7 1.1 pad_maximum_fusion.x_ref
  35.7 76.4 %layer.1 = (bf16[1104,256]{1,0:T(8,128)(2,1)}, bf16[1104,256]{1,0:T(8,128)(2,1)}, f32[3072,256]{1,0:T(8,128)}, f32[16,256]{1,0:T(8,128)}) custom-call(bf16[2208,256]{1,0:T(8,128)(2,1)} %pad_maximum_fusion.x_ref, f32[1,2208]{1,0:T(1,128)} %select_n.90.keep_ref, bf16[1104,256]{1,0:T(8,128)(2,1)} %pad_maximum_fusion.2.cot_ref, bf16[256]{0:T(256)(128)(2,1)} %ag_ref.1, ...), custom_call_target="tpu_custom_call" | custom-call | tf_op jit(solution)/shard_map/layer/pallas_call | solution.py:431
  112.2 1.9 copy-done
  114.8 47.5 %sum_grads.1 = (f32[3072,256]{1,0:T(8,128)S(1)}, f32[16,256]{1,0:T(8,128)S(1)}) custom-call(f32[3072,256]{1,0:T(8,128)S(1)} %copy-done, f32[16,256]{1,0:T(8,128)S(1)} %copy-done.1), custom_call_target="tpu_custom_call" | custom-call | tf_op jit(solution)/shard_map/sum_grads/pallas_call | solution.py:367
  162.3 1.1 fusion.2
  163.4 1.0 fusion.3
  164.9 3.4 %collective-permute-start.8 = (bf16[552,256]{1,0:T(8,128)(2,1)S(1)}, bf16[552,256]{1,0:T(8,128)(2,1)S(1)}, u32[]{:S(2)}, u32[]{:S(2)}) collective-permute-start(bf16[552,256]{1,0:T(8,128)(2,1)S(1)} %get-tuple-element.48), channel_id=1, source_target_pairs={{0,0},{1,1},{4,2},{5,3},{2,4},{3,5},{6,6},{7,7},{8,8},{9,9},{12,10... | collective-permute-start | bytes 847880 | tf_op jit(solution)/shard_map/ppermute | solution.py:412
  168.3 4.3 %collective-permute-start.9 = (bf16[552,256]{1,0:T(8,128)(2,1)S(1)}, bf16[552,256]{1,0:T(8,128)(2,1)S(1)}, u32[]{:S(2)}, u32[]{:S(2)}) collective-permute-start(bf16[552,256]{1,0:T(8,128)(2,1)S(1)} %get-tuple-element.49), channel_id=1, source_target_pairs={{1,0},{0,1},{5,2},{4,3},{3,4},{2,5},{7,6},{6,7},{9,8},{8,9},{13,10... | collective-permute-start | bytes 847880 | tf_op jit(solution)/shard_map/ppermute | solution.py:412
  172.6 0.8 fusion.5
  174.1 2.8 %collective-permute-start.6 = (bf16[552,256]{1,0:T(8,128)(2,1)}, bf16[552,256]{1,0:T(8,128)(2,1)}, u32[]{:S(2)}, u32[]{:S(2)}) collective-permute-start(bf16[552,256]{1,0:T(8,128)(2,1)} %get-tuple-element.50), channel_id=1, source_target_pairs={{0,0},{1,1},{4,2},{5,3},{2,4},{3,5},{6,6},{7,7},{8,8},{9,9},{12,10... | collective-permute-start | bytes 847880 | tf_op jit(solution)/shard_map/ppermute | solution.py:412
  177.0 1.3 copy.31
  178.9 11.2 %collective-permute-done.9 = bf16[552,256]{1,0:T(8,128)(2,1)S(1)} collective-permute-done((bf16[552,256]{1,0:T(8,128)(2,1)S(1)}, bf16[552,256]{1,0:T(8,128)(2,1)S(1)}, u32[]{:S(2)}, u32[]{:S(2)}) %collective-permute-start.9) | collective-permute-done | bytes 282656 | tf_op jit(solution)/shard_map/ppermute | solution.py:412
  190.1 1.2 convert_add_fusion
  191.3 5.0 %collective-permute-done.7 = bf16[552,256]{1,0:T(8,128)(2,1)} collective-permute-done((bf16[552,256]{1,0:T(8,128)(2,1)}, bf16[552,256]{1,0:T(8,128)(2,1)}, u32[]{:S(2)}, u32[]{:S(2)}) %collective-permute-start.7) | collective-permute-done | bytes 282656 | tf_op jit(solution)/shard_map/ppermute | solution.py:412
  196.3 2.1 %maximum_select_fusion = bf16[2,552,256]{2,1,0:T(8,128)(2,1)} fusion(bf16[1,552,256]{2,1,0:T(8,128)(2,1)} %bitcast.12, bf16[1,552,256]{2,1,0:T(8,128)(2,1)} %bitcast.11, pred[]{:T(512)S(6)} %eq.23), kind=kLoop, calls=%fused_computation.6 | loop fusion | flops 847872 | bytes 1130497 | tf_op jit(solution)/shard_map/jit(_where)/select_n | solution.py:413
  (38 shorter events, 4.3 us)
Async XLA Ops:
  0.7 6.2 %copy-start.3 = (bf16[2,552,256]{2,1,0:T(8,128)(2,1)S(1)}, bf16[2,552,256]{2,1,0:T(8,128)(2,1)}, u32[]{:S(2)}) copy-start(bf16[2,552,256]{2,1,0:T(8,128)(2,1)} %param.16) | copy-start | bytes 1695748
  2.1 9.4 %copy-start.6 = (s32[2,2208]{1,0:T(2,128)S(1)}, s32[2,2208]{1,0:T(2,128)}, u32[]{:S(2)}) copy-start(s32[2,2208]{1,0:T(2,128)} %param.17) | copy-start | bytes 52996
  2.2 31.7 %collective-permute-start.4 = (bf16[552,256]{1,0:T(8,128)(2,1)S(1)}, bf16[552,256]{1,0:T(8,128)(2,1)S(1)}, u32[]{:S(2)}, u32[]{:S(2)}) collective-permute-start(bf16[552,256]{1,0:T(8,128)(2,1)S(1)} %get-tuple-element.52), channel_id=1, source_target_pairs={{0,0},{1,1},{2,4},{3,5},{4,2},{5,3},{6,6},{7,7},{8,8},{9,9},{10,12... | collective-permute-start | bytes 847880 | tf_op jit(solution)/shard_map/ppermute | solution.py:405
  4.1 29.7 %collective-permute-start.5 = (bf16[552,256]{1,0:T(8,128)(2,1)S(1)}, bf16[552,256]{1,0:T(8,128)(2,1)S(1)}, u32[]{:S(2)}, u32[]{:S(2)}) collective-permute-start(bf16[552,256]{1,0:T(8,128)(2,1)S(1)} %get-tuple-element.53), channel_id=1, source_target_pairs={{0,1},{1,0},{2,5},{3,4},{4,3},{5,2},{6,7},{7,6},{8,9},{9,8},{10,13... | collective-permute-start | bytes 847880 | tf_op jit(solution)/shard_map/ppermute | solution.py:405
  6.9 19.4 %collective-permute-start = (bf16[552,256]{1,0:T(8,128)(2,1)S(1)}, bf16[552,256]{1,0:T(8,128)(2,1)S(1)}, u32[]{:S(2)}, u32[]{:S(2)}) collective-permute-start(bf16[552,256]{1,0:T(8,128)(2,1)S(1)} %get-tuple-element.54), channel_id=1, source_target_pairs={{0,0},{1,1},{2,4},{3,5},{4,2},{5,3},{6,6},{7,7},{8,8},{9,9},{10,12... | collective-permute-start | bytes 847880 | tf_op jit(solution)/shard_map/ppermute | solution.py:405
  9.8 22.5 %collective-permute-start.1 = (bf16[552,256]{1,0:T(8,128)(2,1)S(1)}, bf16[552,256]{1,0:T(8,128)(2,1)S(1)}, u32[]{:S(2)}, u32[]{:S(2)}) collective-permute-start(bf16[552,256]{1,0:T(8,128)(2,1)S(1)} %get-tuple-element.55), channel_id=1, source_target_pairs={{0,1},{1,0},{2,5},{3,4},{4,3},{5,2},{6,7},{7,6},{8,9},{9,8},{10,13... | collective-permute-start | bytes 847880 | tf_op jit(solution)/shard_map/ppermute | solution.py:405
  11.5 1.2 collective-permute-start.3
  32.3 2.4 %collective-permute-start.2 = (bf16[1104,256]{1,0:T(8,128)(2,1)S(1)}, bf16[1104,256]{1,0:T(8,128)(2,1)S(1)}, u32[]{:S(2)}, u32[]{:S(2)}) collective-permute-start(bf16[1104,256]{1,0:T(8,128)(2,1)S(1)} %pad_maximum_fusion.1), channel_id=1, source_target_pairs={{0,4},{4,0},{8,12},{12,8},{16,20},{20,16},{24,28},{28,24},{1,5},{5... | collective-permute-start | bytes 1695752 | tf_op jit(solution)/shard_map/ppermute | solution.py:417
  112.2 1.9 copy-start
  114.1 0.7 copy-start.1
  163.4 1.4 copy-start.5
  163.4 9.2 %copy-start.4 = (bf16[1104,256]{1,0:T(8,128)(2,1)S(1)}, bf16[1104,256]{1,0:T(8,128)(2,1)}, u32[]{:S(2)}) copy-start(bf16[1104,256]{1,0:T(8,128)(2,1)} %get-tuple-element.21) | copy-start | bytes 1695748
  164.9 14.0 %collective-permute-start.8 = (bf16[552,256]{1,0:T(8,128)(2,1)S(1)}, bf16[552,256]{1,0:T(8,128)(2,1)S(1)}, u32[]{:S(2)}, u32[]{:S(2)}) collective-permute-start(bf16[552,256]{1,0:T(8,128)(2,1)S(1)} %get-tuple-element.48), channel_id=1, source_target_pairs={{0,0},{1,1},{4,2},{5,3},{2,4},{3,5},{6,6},{7,7},{8,8},{9,9},{12,10... | collective-permute-start | bytes 847880 | tf_op jit(solution)/shard_map/ppermute | solution.py:412
  168.3 21.8 %collective-permute-start.9 = (bf16[552,256]{1,0:T(8,128)(2,1)S(1)}, bf16[552,256]{1,0:T(8,128)(2,1)S(1)}, u32[]{:S(2)}, u32[]{:S(2)}) collective-permute-start(bf16[552,256]{1,0:T(8,128)(2,1)S(1)} %get-tuple-element.49), channel_id=1, source_target_pairs={{1,0},{0,1},{5,2},{4,3},{3,4},{2,5},{7,6},{6,7},{9,8},{8,9},{13,10... | collective-permute-start | bytes 847880 | tf_op jit(solution)/shard_map/ppermute | solution.py:412
  173.5 16.6 %copy-start.2 = (f32[2,552,256]{2,1,0:T(8,128)S(1)}, f32[2,552,256]{2,1,0:T(8,128)}, u32[]{:S(2)}) copy-start(f32[2,552,256]{2,1,0:T(8,128)} %param.31) | copy-start | bytes 3391492
  174.1 17.2 %collective-permute-start.6 = (bf16[552,256]{1,0:T(8,128)(2,1)}, bf16[552,256]{1,0:T(8,128)(2,1)}, u32[]{:S(2)}, u32[]{:S(2)}) collective-permute-start(bf16[552,256]{1,0:T(8,128)(2,1)} %get-tuple-element.50), channel_id=1, source_target_pairs={{0,0},{1,1},{4,2},{5,3},{2,4},{3,5},{6,6},{7,7},{8,8},{9,9},{12,10... | collective-permute-start | bytes 847880 | tf_op jit(solution)/shard_map/ppermute | solution.py:412
  176.9 19.4 %collective-permute-start.7 = (bf16[552,256]{1,0:T(8,128)(2,1)}, bf16[552,256]{1,0:T(8,128)(2,1)}, u32[]{:S(2)}, u32[]{:S(2)}) collective-permute-start(bf16[552,256]{1,0:T(8,128)(2,1)} %get-tuple-element.51), channel_id=1, source_target_pairs={{1,0},{0,1},{5,2},{4,3},{3,4},{2,5},{7,6},{6,7},{9,8},{8,9},{13,10... | collective-permute-start | bytes 847880 | tf_op jit(solution)/shard_map/ppermute | solution.py:412

commit v3 on v2

v3 whole, which is shorter than its diff:
```python
import math
from functools import partial

import jax
import jax.numpy as jnp
from jax import lax
from jax.experimental import pallas as pl
from jax.experimental.pallas import tpu as pltpu
from jax.sharding import PartitionSpec as P

bf16 = jnp.bfloat16
f32 = jnp.float32
HEADS = 4
CLS = 8
TILE = 256
MASKED = -8.0e9
NN = (((1,), (0,)), ((), ()))
NT = (((1,), (1,)), ((), ()))
TN = (((0,), (0,)), ((), ()))
TT = (((0,), (1,)), ((), ()))
MESH = pl.DeviceIdType.MESH


def mm(a, b, dims=NN):
    return lax.dot_general(a, b, dims, preferred_element_type=f32)


def norm_parts(z):
    average = jnp.mean(z, axis=-1, keepdims=True)
    centred = z - average
    spread = jnp.mean(centred * centred, axis=-1, keepdims=True)
    rstd = lax.rsqrt(spread + 1e-05)
    return centred * rstd, rstd


def norm_back(f, n, rstd):
    mean_f = jnp.mean(f, axis=-1, keepdims=True)
    mean_fn = jnp.mean(f * n, axis=-1, keepdims=True)
    return rstd * (f - mean_f - n * mean_fn)


def normal_parts(u):
    bell = jnp.exp2(u * u * (-0.5 * math.log2(math.e)))
    t = 1.0 / (1.0 + (0.3275911 / math.sqrt(2.0)) * jnp.abs(u))
    poly = 1.061405429 * t - 1.453152027
    poly = poly * t + 1.421413741
    poly = poly * t - 0.284496736
    poly = (poly * t + 0.254829592) * t
    tail = 0.5 * poly * bell
    return jnp.where(u < 0, tail, 1.0 - tail), bell * (1.0 / math.sqrt(2.0 * math.pi))


def colsum(z):
    return jnp.sum(z, axis=0, keepdims=True)


def row_vec(ref):
    return ref[...].astype(f32).reshape(1, -1)


def up16(n):
    return -(-n // 16) * 16


class Sems:
    def __init__(self, send, recv):
        self.send, self.recv, self.used = send, recv, 0

    def copy(self, src, dst, device):
        k = self.used
        self.used += 1
        return pltpu.make_async_remote_copy(
            src_ref=src, dst_ref=dst, send_sem=self.send.at[k], recv_sem=self.recv.at[k],
            device_id=device, device_id_type=MESH)


def reduce_steps(sems, ctx, seq, order, seqs, rows, acc, acc0, send, send0, recv, recv0, gat, gat0):
    half = rows // 2
    mine = lax.rem(ctx, 2)
    base = mine * half
    off = base
    size = half
    into = recv0
    out = send0
    path = []
    for step, bit in enumerate(order):
        peer = (ctx + (1 - 2 * lax.rem(ctx // (1 << bit), 2)) * (1 << bit), seq)
        if step == 0:
            path.append((peer, off, size))
            cp = sems.copy(send.at[pl.ds(out, size)], recv.at[pl.ds(into, size)], peer)
            kept = off
        elif size % (32 * seqs) == 0:
            size = size // 2
            mine = lax.rem(ctx // (1 << bit), 2)
            kept = off + mine * size
            away = off + (1 - mine) * size
            send[pl.ds(out, size), :] = acc[pl.ds(pl.multiple_of(acc0 + away - base, 16), size), :].astype(bf16)
            path.append((peer, kept, size))
            cp = sems.copy(send.at[pl.ds(out, size)], recv.at[pl.ds(into, size)], peer)
        else:
            send[pl.ds(out, size), :] = acc[pl.ds(pl.multiple_of(acc0 + off - base, 16), size), :].astype(bf16)
            cp = sems.copy(send.at[pl.ds(out, size)], recv.at[pl.ds(into, size)], peer)
            kept = off
        cp.start()
        yield
        cp.wait()
        at = pl.ds(pl.multiple_of(acc0 + kept - base, 16), size)
        acc[at, :] = acc[at, :] + recv[pl.ds(into, size), :].astype(f32)
        off = kept
        into += size
    piece = size // seqs
    send[pl.ds(out, size), :] = acc[pl.ds(pl.multiple_of(acc0 + off - base, 16), size), :].astype(bf16)
    cps = []
    for d in range(1, seqs):
        t = lax.rem(seq + d, seqs)
        cps.append(sems.copy(
            send.at[pl.ds(pl.multiple_of(out + t * piece, 16), piece)],
            recv.at[pl.ds(into + (d - 1) * piece, piece)], (ctx, t)))
    for cp in cps:
        cp.start()
    yield
    for cp in cps:
        cp.wait()
    total = acc[pl.ds(pl.multiple_of(acc0 + off - base + seq * piece, 16), piece), :]
    for d in range(1, seqs):
        total += recv[pl.ds(into + (d - 1) * piece, piece), :].astype(f32)
    at = pl.ds(pl.multiple_of(gat0 + off + seq * piece, 16), piece)
    gat[at, :] = total.astype(bf16)
    cps = []
    for d in range(1, seqs):
        cps.append(sems.copy(gat.at[at], gat.at[at], (ctx, lax.rem(seq + d, seqs))))
    for cp in cps:
        cp.start()
    yield
    for cp in cps:
        cp.wait()
    for peer, kept, size in reversed(path):
        at = pl.ds(pl.multiple_of(gat0 + kept, 16), size)
        cp = sems.copy(gat.at[at], gat.at[at], peer)
        cp.start()
        yield
        cp.wait()


def landing_rows(rows, nbits, seqs):
    size = rows // 2
    count = size
    for _ in range(nbits - 1):
        if size % (32 * seqs) == 0:
            size //= 2
        count += size
    return count + size // seqs * (seqs - 1)


def landing_rows(rows, nbits, seqs):
    size = rows // 2
    count = size
    for _ in range(nbits - 1):
        if size % (32 * seqs) == 0:
            size //= 2
        count += size
    return count + size // seqs * (seqs - 1)


def small_steps(sems, ctx, seq, nbits, seqs, small, send, recv):
    for b in range(nbits):
        send[b] = small[...].astype(bf16)
        peer = (ctx + (1 - 2 * lax.rem(ctx // (1 << b), 2)) * (1 << b), seq)
        cp = sems.copy(send.at[b], recv.at[b], peer)
        cp.start()
        yield
        cp.wait()
        small[...] = send[b].astype(f32) + recv[b].astype(f32)
    send[nbits] = small[...].astype(bf16)
    cps = []
    for d in range(1, seqs):
        cps.append(sems.copy(send.at[nbits], recv.at[nbits + d - 1], (ctx, lax.rem(seq + d, seqs))))
    for cp in cps:
        cp.start()
    yield
    for cp in cps:
        cp.wait()
    shares = [send[nbits].astype(f32)] + [recv[nbits + d - 1].astype(f32) for d in range(1, seqs)]
    total = jnp.zeros_like(shares[0])
    for o in range(seqs):
        which = lax.rem(seq - o + seqs, seqs)
        for d in range(seqs):
            total += jnp.where(which == d, shares[d], 0.0)
    small[...] = total


def layer_kernel(
    nbits, seqs,
    xin, kept_ref, cot_hbm,
    ag_ref, as_ref, wq_ref, wk_ref, wv_ref, wo_ref, ob_ref,
    mg_ref, ms_ref, wu_ref, ub_ref, wd_ref, db_ref,
    outr, backr, gat, small_ref,
    stage, xall, cotr, marks, n_ref, qaug, kaug, vaug, kt, vtaug, prob, s_ref, ot_ref, rl_ref,
    att_t, att, act_ref, gh_ref, gml_ref, gaug, dext, erecv, acc, recv, ssend, srecv,
    local_sem, send_sems, recv_sems, ret_send, ret_recv,
):
    copies, tok, width = xin.shape
    tokp = xall.shape[1]
    own = 2 * tokp
    rows = 2 * own
    ctx = lax.axis_index("ctx")
    seq = lax.axis_index("seq")
    cc = lax.rem(ctx, 2)
    group = ctx - cc
    sems = Sems(send_sems, recv_sems)
    hd = width // HEADS
    pairs = HEADS // 2
    pw = 2 * hd
    head_cols = qaug.shape[2] // 2
    cols = 2 * head_cols
    tiles = cols // TILE
    scale = 1.0 / math.sqrt(hd)
    expo = scale * math.log2(math.e)
    ff = wu_ref.shape[1]
    chunk = tokp
    nchunk = own // chunk
    sibling = (group + 1 - cc, seq)
    stay = seq // 2 == cc

    cot_in = pltpu.make_async_copy(cot_hbm, s_ref.at[pl.ds(0, 2 * tok)], local_sem)
    cot_in.start()

    barrier = pltpu.get_barrier_semaphore()
    for dc in range(2):
        for d in range(seqs):
            if dc or d:
                pl.semaphore_signal(
                    barrier, inc=1, device_id=(group + lax.rem(cc + dc, 2), lax.rem(seq + d, seqs)), device_id_type=MESH)
    for b in range(1, nbits):
        pl.semaphore_signal(
            barrier, inc=1, device_id=(ctx + (1 - 2 * lax.rem(ctx // (1 << b), 2)) * (1 << b), seq), device_id_type=MESH)

    lane = lax.broadcasted_iota(jnp.int32, (1, seqs * tok), 1)
    usable = jnp.where(jnp.logical_or(kept_ref[...] == 1, lane < CLS), 0.0, MASKED)
    usable = jnp.where(lax.rem(seq, 2) == 0, usable[0:1, :], usable[1:2, :])
    wide = marks.shape[3]
    sub = lax.broadcasted_iota(jnp.int32, (16, wide), 0)
    for sh in range(seqs):
        piece = jnp.concatenate(
            [usable[:, sh * tok:(sh + 1) * tok], jnp.full((1, wide - tok), MASKED, f32)], axis=1)
        marks[0, sh] = jnp.where(sub == 0, piece, 0.0).astype(bf16)
    stage[:, tokp - 16:tokp, :] = jnp.zeros((copies, 16, width), bf16)
    stage[:, 0:tok, :] = xin[...]

    def out_copy(k, dst):
        b = lax.rem(seq + k, 2)
        return sems.copy(stage.at[b], dst.at[k], (group + seq // 2, 2 * cc + b))

    def scatter(dst):
        moves = [out_copy(0, dst), out_copy(1, dst)]
        moves[1].start()

        @pl.when(jnp.logical_not(stay))
        def _():
            moves[0].start()

        @pl.when(stay)
        def _():
            dst[0] = stage[lax.rem(seq, 2)]

        return moves

    def arrived(moves, k):
        if k:
            moves[k].wait_recv()
        else:
            @pl.when(jnp.logical_not(stay))
            def _():
                moves[0].wait_recv()

    def left(moves):
        moves[1].wait_send()

        @pl.when(jnp.logical_not(stay))
        def _():
            moves[0].wait_send()

    pl.semaphore_wait(barrier, 2 * seqs - 1 + nbits - 1)
    moves = scatter(xall)
    marks_copy = sems.copy(marks.at[0], marks.at[1], sibling)
    marks_copy.start()

    gain = row_vec(ag_ref)
    shift = row_vec(as_ref)

    def project(pos):
        at = slice(pos * tokp, (pos + 1) * tokp)
        n, _ = norm_parts(xall[pos].astype(f32))
        low = (n * gain + shift).astype(bf16)
        n_ref[at, :] = low
        k = mm(low, wk_ref[...]).astype(bf16)
        v = mm(low, wv_ref[...]).astype(bf16)
        for p in range(pairs):
            kaug[p, at, 0:pw] = k[:, p * pw:(p + 1) * pw]
            vaug[p, at, 0:pw] = v[:, p * pw:(p + 1) * pw]

    forwards = []
    for k in range(2):
        arrived(moves, k)
        forwards.append(sems.copy(xall.at[k], xall.at[2 + k], sibling))
        forwards[k].start()
    for k in range(2):
        project(k)
    left(moves)
    cot_in.wait()
    for b in range(2):
        stage[b, 0:tok, :] = s_ref[b * tok:(b + 1) * tok, :].astype(bf16)
    cot_moves = scatter(cotr)
    marks_copy.wait()
    held = jnp.where(stay, 0, 1)
    unit = jnp.where(
        lax.broadcasted_iota(jnp.int32, (16, pw), 0) == lax.broadcasted_iota(jnp.int32, (16, pw), 1), 1.0, 0.0
    ).astype(bf16)
    lane = lax.broadcasted_iota(jnp.int32, (rows, pw), 1)
    ones = jnp.where(lane < 2, 1.0, 0.0).astype(bf16)
    for p in range(pairs):
        vaug[p, :, pw:2 * pw] = ones
    for pos in range(4):
        side = cc if pos < 2 else 1 - cc
        mark = marks[held, 2 * side + lax.rem(seq + pos, 2)]
        bias = mm(mark, unit, TN).astype(bf16)[0:tokp, :]
        for p in range(pairs):
            kaug[p, pos * tokp:(pos + 1) * tokp, pw:2 * pw] = bias
    qt = mm(wq_ref[...], n_ref[0:own, :], TT).astype(bf16)
    qaug[...] = jnp.zeros_like(qaug)
    gaug[...] = jnp.zeros_like(gaug)
    dext[...] = jnp.zeros_like(dext)
    for p in range(pairs):
        for h in range(2):
            qaug[p, h * hd:(h + 1) * hd, h * head_cols:h * head_cols + own] = qt[p * pw + h * hd:p * pw + (h + 1) * hd, :]
    for k in range(2):
        forwards[k].wait()
        project(2 + k)
    kt[...] = mm(wk_ref[...], n_ref[...], TT).astype(bf16)
    vt = mm(wv_ref[...], n_ref[...], TT).astype(bf16)
    sub = lax.broadcasted_iota(jnp.int32, (16, rows), 0)
    for p in range(pairs):
        vtaug[p, 0:pw, :] = vt[p * pw:(p + 1) * pw, :]
        vtaug[p, pw:pw + 16, :] = jnp.where(sub == 0, 1.0, 0.0).astype(bf16)

    first = jnp.where(lax.broadcasted_iota(jnp.int32, (pw, TILE), 0) == 0, 1.0, 0.0).astype(bf16)

    def forward(i, carry):
        p = i // tiles
        at = pl.ds(pl.multiple_of((i % tiles) * TILE, TILE), TILE)
        s_ref[...] = mm(kaug[p], jnp.concatenate([qaug[p, :, at], first], axis=0))
        top = jnp.max(s_ref[...], axis=0, keepdims=True)
        prob[p, :, at] = jnp.exp2((s_ref[...] - top) * expo).astype(bf16)
        o = mm(vtaug[p], prob[p, :, at])
        rl = 1.0 / o[pw:pw + 1]
        ot_ref[p, :, at] = o[0:pw] * rl
        rl_ref[p, :, at] = rl
        return carry

    lax.fori_loop(0, pairs * tiles, forward, 0)
    for p in range(pairs):
        for h in range(2):
            att_t[p * pw + h * hd:p * pw + (h + 1) * hd, :] = ot_ref[
                p, h * hd:(h + 1) * hd, h * head_cols:h * head_cols + own
            ].astype(bf16)
    att[...] = jnp.transpose(att_t[...])

    gain2 = row_vec(mg_ref)
    shift2 = row_vec(ms_ref)
    out_bias = row_vec(ob_ref)
    up_bias = row_vec(ub_ref)
    down_bias = row_vec(db_ref)
    arrived(cot_moves, 0)
    arrived(cot_moves, 1)
    left(cot_moves)

    def mlp(i, carry):
        g_up, g_down, g_out, g_gain, g_shift = carry
        at = pl.ds(pl.multiple_of(i * chunk, 16), chunk)
        middle = xall[i].astype(f32) + (mm(att[at, :], wo_ref[...]) + out_bias)
        n, rstd = norm_parts(middle)
        low = (n * gain2 + shift2).astype(bf16)
        att[at, :] = low
        hidden = mm(low, wu_ref[...]) + up_bias
        dist, dens = normal_parts(hidden)
        act = (hidden * dist).astype(bf16)
        act_ref[at, :] = act
        stage[i] = (middle + (mm(act, wd_ref[...]) + down_bias)).astype(bf16)
        cot = cotr[i]
        gh = ((dist + hidden * dens) * mm(cot, wd_ref[...], NT)).astype(bf16)
        gh_ref[at, :] = gh
        e = mm(gh, wu_ref[...], NT)
        back = norm_back(e * gain2, n, rstd)
        s_ref[at, :] = back
        cot = cot.astype(f32)
        gml = (cot + back).astype(bf16)
        gml_ref[at, :] = gml
        return (
            g_up + colsum(gh.astype(f32)), g_down + colsum(cot), g_out + colsum(gml.astype(f32)),
            g_gain + colsum(e * n), g_shift + colsum(e),
        )

    zero = jnp.zeros((1, width), f32)
    sums = lax.fori_loop(0, nchunk, mlp, (jnp.zeros((1, ff), f32), zero, zero, zero, zero))
    small_ref[0:1, :] = sums[1]
    small_ref[1:2, :] = sums[2]
    small_ref[2:3, :] = sums[3]
    small_ref[3:4, :] = sums[4]
    ups = 4 + ff // width
    for j in range(ff // width):
        small_ref[4 + j:5 + j, :] = sums[0][:, j * width:(j + 1) * width]

    def back_copy(k, dst, sem):
        b = lax.rem(seq, 2)
        return pltpu.make_async_remote_copy(
            src_ref=stage.at[k], dst_ref=dst.at[b], send_sem=ret_send.at[2 * sem + k], recv_sem=ret_recv.at[2 * sem + b],
            device_id=(group + seq // 2, 2 * cc + lax.rem(seq + k, 2)), device_id_type=MESH)

    def send_home(dst, sem):
        moves = [back_copy(0, dst, sem), back_copy(1, dst, sem)]
        moves[1].start()

        @pl.when(jnp.logical_not(stay))
        def _():
            moves[0].start()

        @pl.when(stay)
        def _():
            dst[lax.rem(seq, 2)] = stage[0]

        return moves

    def home_again(dst, sem):
        for b in range(2):
            here = jnp.logical_and(stay, lax.rem(seq, 2) == b)

            @pl.when(jnp.logical_not(here))
            def _():
                pltpu.make_async_remote_copy(
                    src_ref=stage.at[b], dst_ref=dst.at[b], send_sem=ret_send.at[2 * sem + b],
                    recv_sem=ret_recv.at[2 * sem + b], device_id=sibling, device_id_type=MESH).wait_recv()

    out_moves = send_home(outr, 0)

    spare = own

    def split(value, count, acc0, send, send0, at=0):
        s_ref[spare:spare + count, :] = value
        half = count // 2
        acc[acc0:acc0 + half, :] = s_ref[pl.ds(pl.multiple_of(spare + cc * half, 16), half), :]
        send[pl.ds(send0, half), :] = s_ref[pl.ds(pl.multiple_of(spare + (1 - cc) * half, 16), half), :].astype(bf16)

    sets = (ff, ff, 2 * width, 2 * width)
    starts = [sum(sets[:j]) for j in range(4)]
    lands = [landing_rows(sets[j], nbits, seqs) for j in range(4)]
    lands = [sum(lands[:j]) for j in range(4)]
    lands = [landing_rows(sets[j], nbits, seqs) for j in range(4)]
    lands = [sum(lands[:j]) for j in range(4)]
    send_a = act_ref.at[:, 2 * width:3 * width]
    send_b = act_ref.at[:, 3 * width:4 * width]
    send_c = gh_ref.at[:, 2 * width:3 * width]
    send_d = gh_ref.at[:, 3 * width:4 * width]
    sends = (send_a, send_b, send_c, send_d)
    bits = list(range(nbits))
    turned = bits[:1] + bits[:0:-1]
    orders = (bits, turned, turned, bits)
    steps = [
        reduce_steps(sems, ctx, seq, orders[j], seqs, sets[j], acc, starts[j] // 2, sends[j], 0, recv, lands[j], gat, starts[j])
        for j in range(4)
    ]
    running = []

    def turn():
        for g in list(running):
            if next(g, "done") == "done":
                running.remove(g)

    split(mm(act_ref[...], cotr[...].reshape(own, width), TN), ff, starts[0] // 2, send_a, 0)
    up = mm(att[...], gh_ref[...], TN)
    up = jnp.concatenate([up[:, j * width:(j + 1) * width] for j in range(ff // width)], axis=0)
    split(up, ff, starts[1] // 2, send_b, 0)
    running += [steps[0], steps[1]]
    turn()
    split(mm(att_t[...], gml_ref[...]), width, starts[2] // 2, send_c, 0)

    sub = lax.broadcasted_iota(jnp.int32, (16, own), 0)
    for p in range(pairs):
        for h in range(2):
            lanes = slice(h * head_cols, h * head_cols + own)
            g = mm(wo_ref[p * pw + h * hd:p * pw + (h + 1) * hd, :], gml_ref[...], NT).astype(bf16).astype(f32)
            g = (g * rl_ref[p, :, lanes]).astype(bf16)
            gaug[p, h * hd:(h + 1) * hd, lanes] = g
            delta = -colsum(g.astype(f32) * ot_ref[p, h * hd:(h + 1) * hd, lanes])
            coarse = delta.astype(bf16).astype(f32)
            dext[p, :, lanes] = jnp.where(sub == 0, coarse, jnp.where(sub == 1, delta - coarse, 0.0)).astype(bf16)

    for p in range(pairs):
        for half in range(2):
            lanes = slice(half * width + p * pw, half * width + (p + 1) * pw)
            act_ref[:, lanes] = mm(prob[p, half * own:(half + 1) * own, :], gaug[p], NT).astype(bf16)
        turn()
    dv_own, dv_sib = act_ref.at[:, 0:width], act_ref.at[:, width:2 * width]
    dk_own, dk_sib = gh_ref.at[:, 0:width], gh_ref.at[:, width:2 * width]
    split(mm(n_ref[0:own, :], dv_own[...], TN) + mm(n_ref[own:rows, :], dv_sib[...], TN),
          width, (starts[2] + width) // 2, send_c, width // 2)
    running.append(steps[2])
    turn()
    nothing = jnp.zeros((pw - 16, TILE), bf16)

    def backward(i, carry):
        p = i // tiles
        at = pl.ds(pl.multiple_of((i % tiles) * TILE, TILE), TILE)
        right = jnp.concatenate([gaug[p, :, at], dext[p, :, at], nothing], axis=0)
        ds = prob[p, :, at] * mm(vaug[p], right).astype(bf16)
        prob[p, :, at] = ds
        dq = mm(kt[pl.ds(pl.multiple_of(p * pw, pw), pw), :], ds)
        ot_ref[p, :, at] = dq * scale
        return carry

    for p in range(pairs):
        for part in range(3):
            lax.fori_loop(p * tiles + part * tiles // 3, p * tiles + (part + 1) * tiles // 3, backward, 0)
            turn()
    for p in range(pairs):
        for half in range(2):
            lanes = slice(half * width + p * pw, half * width + (p + 1) * pw)
            gh_ref[:, lanes] = (mm(prob[p, half * own:(half + 1) * own, :], qaug[p], NT) * scale).astype(bf16)
        turn()
    left(out_moves)

    def other_rows(i, carry):
        at = pl.ds(pl.multiple_of(i * chunk, 16), chunk)
        gml_ref[at, :] = (mm(dk_sib[at, :], wk_ref[...], NT) + mm(dv_sib[at, :], wv_ref[...], NT)).astype(bf16)
        return carry

    lax.fori_loop(0, nchunk, other_rows, 0)
    e_copy = sems.copy(gml_ref, erecv, sibling)
    e_copy.start()
    turn()
    for p in range(pairs):
        for h in range(2):
            att_t[p * pw + h * hd:p * pw + (h + 1) * hd, :] = ot_ref[
                p, h * hd:(h + 1) * hd, h * head_cols:h * head_cols + own
            ].astype(bf16)
    att[...] = jnp.transpose(att_t[...])
    split(mm(n_ref[0:own, :], att[...], TN), width, starts[3] // 2, send_d, 0)
    split(mm(n_ref[0:own, :], dk_own[...], TN) + mm(n_ref[own:rows, :], dk_sib[...], TN),
          width, (starts[3] + width) // 2, send_d, width // 2)
    running.append(steps[3])
    turn()

    def own_rows(i, carry):
        at = pl.ds(pl.multiple_of(i * chunk, 16), chunk)
        s_ref[pl.ds(pl.multiple_of(own + i * chunk, 16), chunk), :] = (
            mm(att[at, :], wq_ref[...], NT) + mm(dk_own[at, :], wk_ref[...], NT) + mm(dv_own[at, :], wv_ref[...], NT)
        )
        return carry

    lax.fori_loop(0, nchunk, own_rows, 0)
    turn()
    e_copy.wait()

    def last_rows(i, carry):
        at = pl.ds(pl.multiple_of(i * chunk, 16), chunk)
        n, rstd = norm_parts(xall[i].astype(f32))
        e = s_ref[pl.ds(pl.multiple_of(own + i * chunk, 16), chunk), :] + erecv[at, :].astype(f32)
        stage[i] = (s_ref[at, :] + norm_back(e * gain, n, rstd)).astype(bf16)
        return carry[0] + colsum(e * n), carry[1] + colsum(e)

    sums = lax.fori_loop(0, nchunk, last_rows, (zero, zero))
    small_ref[ups:ups + 1, :] = sums[0]
    small_ref[ups + 1:ups + 2, :] = sums[1]
    small_ref[ups + 2:, :] = jnp.zeros((small_ref.shape[0] - ups - 2, width), f32)
    back_moves = send_home(backr, 1)
    running.append(small_steps(sems, ctx, seq, nbits, seqs, small_ref, ssend, srecv))
    while running:
        turn()
    left(back_moves)
    home_again(outr, 0)
    home_again(backr, 1)


def unpack_kernel(cot_ref, outr, backr, gat, small, *outs):
    copies, tok, width = cot_ref.shape
    (out, xg, ag, as_, wq, wk, wv, wo, ob, mg, ms, wu, ub, wd, db) = outs
    ff = wd.shape[0]
    out[...] = outr[:, 0:tok, :]
    xg[...] = cot_ref[...] + backr[:, 0:tok, :].astype(f32)
    wd[...] = gat[0:ff, :].astype(f32)
    for j in range(ff // width):
        wu[:, j * width:(j + 1) * width] = gat[ff + j * width:ff + (j + 1) * width, :].astype(f32)
        ub[0:1, j * width:(j + 1) * width] = small[4 + j:5 + j, :]
    half = width // 2
    for j, ref in enumerate((wo, wv, wq, wk)):
        at = 2 * ff + j // 2 * 2 * width + j % 2 * half
        ref[0:half, :] = gat[at:at + half, :].astype(f32)
        ref[half:width, :] = gat[at + width:at + width + half, :].astype(f32)
    ups = 4 + ff // width
    for j, ref in ((0, db), (1, ob), (2, mg), (3, ms), (ups, ag), (ups + 1, as_)):
        ref[...] = small[j:j + 1, :]


def body(nctx, seqs, layer_input, gene_kept, attn_gain, attn_shift, w_query, w_key, w_value, w_out, out_bias,
         mlp_gain, mlp_shift, w_up, up_bias, w_down, down_bias, cotangent):
    copies, tok, width = layer_input.shape
    tokp = up16(tok)
    own = 2 * tokp
    rows = 2 * own
    ff = w_up.shape[1]
    nbits = nctx.bit_length() - 1
    vmem = pl.BlockSpec(memory_space=pltpu.VMEM)
    hbm = pl.BlockSpec(memory_space=pl.ANY)
    head_cols = -(-own // 128) * 128
    cols = 2 * head_cols
    pairs = HEADS // 2
    pw = width // 2
    grad_rows = 2 * ff + 4 * width
    landing = 2 * landing_rows(ff, nbits, seqs) + 2 * landing_rows(2 * width, nbits, seqs)
    landing = 2 * landing_rows(ff, nbits, seqs) + 2 * landing_rows(2 * width, nbits, seqs)
    ncopy = 2 + 1 + 2 + 2 + 1 + 4 * (2 * nbits + 2 * (seqs - 1)) + nbits + seqs - 1
    home = jax.ShapeDtypeStruct((copies, tokp, width), bf16)
    outr, backr, gat, small = pl.pallas_call(
        partial(layer_kernel, nbits, seqs),
        out_shape=(
            home, home,
            jax.ShapeDtypeStruct((grad_rows, width), bf16),
            jax.ShapeDtypeStruct((16, width), f32),
        ),
        in_specs=[vmem, vmem, hbm] + [vmem] * 13,
        out_specs=(vmem,) * 4,
        scratch_shapes=[
            pltpu.VMEM((copies, tokp, width), bf16),
            pltpu.VMEM((4, tokp, width), bf16),
            pltpu.VMEM((copies, tokp, width), bf16),
            pltpu.VMEM((2, seqs, 16, -(-tokp // 128) * 128), bf16),
            pltpu.VMEM((rows, width), bf16),
            pltpu.VMEM((pairs, pw, cols), bf16),
            pltpu.VMEM((pairs, rows, width), bf16),
            pltpu.VMEM((pairs, rows, width), bf16),
            pltpu.VMEM((width, rows), bf16),
            pltpu.VMEM((pairs, pw + 16, rows), bf16),
            pltpu.VMEM((pairs, rows, cols), bf16),
            pltpu.VMEM((rows, TILE), f32),
            pltpu.VMEM((pairs, pw, cols), f32),
            pltpu.VMEM((pairs, 1, cols), f32),
            pltpu.VMEM((width, own), bf16),
            pltpu.VMEM((own, width), bf16),
            pltpu.VMEM((own, ff), bf16),
            pltpu.VMEM((own, ff), bf16),
            pltpu.VMEM((own, width), bf16),
            pltpu.VMEM((pairs, pw, cols), bf16),
            pltpu.VMEM((pairs, 16, cols), bf16),
            pltpu.VMEM((own, width), bf16),
            pltpu.VMEM((grad_rows // 2, width), f32),
            pltpu.VMEM((landing, width), bf16),
            pltpu.VMEM((nbits + 1, 16, width), bf16),
            pltpu.VMEM((nbits + seqs, 16, width), bf16),
            pltpu.SemaphoreType.DMA,
            pltpu.SemaphoreType.DMA((ncopy,)),
            pltpu.SemaphoreType.DMA((ncopy,)),
            pltpu.SemaphoreType.DMA((4,)),
            pltpu.SemaphoreType.DMA((4,)),
        ],
        compiler_params=pltpu.CompilerParams(collective_id=1, has_side_effects=True, vmem_limit_bytes=63 * 2**20),
        name="layer",
    )(layer_input, gene_kept, cotangent.reshape(copies * tok, width), attn_gain, attn_shift, w_query, w_key, w_value,
      w_out, out_bias, mlp_gain, mlp_shift, w_up, up_bias, w_down, down_bias)
    line = jax.ShapeDtypeStruct((1, width), f32)
    square = jax.ShapeDtypeStruct((width, width), f32)
    outs = pl.pallas_call(
        unpack_kernel,
        out_shape=(
            jax.ShapeDtypeStruct((copies, tok, width), bf16), jax.ShapeDtypeStruct((copies, tok, width), f32),
            line, line, square, square, square, square, line, line, line,
            jax.ShapeDtypeStruct((width, ff), f32), jax.ShapeDtypeStruct((1, ff), f32),
            jax.ShapeDtypeStruct((ff, width), f32), line,
        ),
        in_specs=[vmem] * 5,
        out_specs=(vmem,) * 15,
        compiler_params=pltpu.CompilerParams(vmem_limit_bytes=32 * 2**20),
        name="unpack",
    )(cotangent, outr, backr, gat, small)
    return tuple(o.reshape(-1) if o.shape[0] == 1 else o for o in outs)


def solution(mesh):
    tokens = P("ctx", "seq", None)
    return jax.shard_map(
        partial(body, mesh.shape["ctx"], mesh.shape["seq"]),
        mesh=mesh,
        in_specs=(tokens, P("ctx", None)) + (P(),) * 13 + (tokens,),
        out_specs=(tokens, tokens) + (P(),) * 13,
        check_vma=False,
    )
```

time: 199 us -> 143 us (0.72)
  the two profiles are of different devices: /device:TPU:18 before, /device:TPU:0 now
where the time goes in v3:
time: 143 us; the launch traced here: 142 us
  Pallas kernels  136 us (95%)
  local copies, waits for them, and re-layouts  5.49 us (4%)
    pallas_call x1, Pallas kernels, body(): pl.pallas_call(partial(layer_kernel, nbits, seqs), out_shape=(home, home,...  134 us
    unnamed x10, local copies, waits for them, and re-layouts  5.49 us

profile of v3, /device:TPU:0, one launch (start us, length us, event | category | flops | bytes accessed | tf_op | source)
XLA Modules:
  0.0 142.5 jit_solution(16230783300456632819)
XLA Ops:
  0.7 133.6 %layer.1 = (bf16[2,560,256]{2,1,0:T(8,128)(2,1)}, bf16[2,560,256]{2,1,0:T(8,128)(2,1)}, bf16[3072,256]{1,0:T(8,128)(2,1)}, f32[16,256]{1,0:T(8,128)}) custom-call(bf16[2,552,256]{2,1,0:T(8,128)(2,1)} %xin.1, s32[2,2208]{1,0:T(2,128)} %kept_ref.1, f32[1104,256]{1,0:T(8,128)} %bitcast.8, bf16[256]{0:T(256)(128)(2,1)} %ag_ref.1, bf16[256]{0:T(256)(128)(2,1)} %as_ref.1, ...), custom_call_target="tpu_custom_call" | custom-call | tf_op jit(solution)/shard_map/layer/pallas_call | solution.py:622
  134.2 0.0 copy-start
  134.2 1.2 copy-done
  135.5 0.0 copy-start.1
  135.5 1.4 copy-done.1
  136.9 0.0 copy-start.2
  136.9 1.1 copy-done.2
  138.0 0.0 copy-start.3
  138.0 1.1 copy-done.3
  139.0 0.0 copy-start.4
  139.0 0.7 copy-done.4
  139.7 2.6 %unpack.1 = (bf16[2,552,256]{2,1,0:T(8,128)(2,1)}, f32[2,552,256]{2,1,0:T(8,128)}, f32[1,256]{1,0:T(1,128)}, f32[1,256]{1,0:T(1,128)}, f32[256,256]{1,0:T(8,128)...) custom-call(f32[2,552,256]{2,1,0:T(8,128)S(1)} %copy-done, ...), custom_call_target="tpu_custom_call" | custom-call | tf_op jit(solution)/shard_map/unpack/pallas_call | solution.py:670
Async XLA Ops:
  134.2 1.3 copy-start
  135.5 1.4 copy-start.1
  136.9 1.1 copy-start.2
  138.0 1.1 copy-start.3
  139.0 0.7 copy-start.4

commit v4 on v3

--- a/solution.py
+++ b/solution.py
@@ -74,119 +74,106 @@
             device_id=device, device_id_type=MESH)
 
 
-def reduce_steps(sems, ctx, seq, order, seqs, rows, acc, acc0, send, send0, recv, recv0, gat, gat0):
-    half = rows // 2
-    mine = lax.rem(ctx, 2)
-    base = mine * half
+def spread(ctx, seq, nbits, seqs):
+    stages = []
+    groups = [(0,)] + [tuple(range(b, min(b + 2, nbits))) for b in range(1, nbits, 2)]
+    for bits in groups:
+        place = [lax.rem(ctx // (1 << b), 2) for b in bits]
+        others = []
+        for r in range(1, 1 << len(bits)):
+            device, index = ctx, 0
+            for k, b in enumerate(bits):
+                there = lax.rem(place[k] + (r >> k) % 2, 2)
+                device = device + (there - place[k]) * (1 << b)
+                index = index + there * (1 << k)
+            others.append(((device, seq), index))
+        mine = sum(p * (1 << k) for k, p in enumerate(place))
+        stages.append((mine, others, 0))
+    stages.append((seq, [((ctx, lax.rem(seq + d, seqs)), lax.rem(seq + d, seqs)) for d in range(1, seqs)], seqs // 2 - 1))
+    return stages
+
+
+def add_in_pairs(own, got, pair):
+    if len(got) == 1:
+        return own + got[0]
+    rest = [g for n, g in enumerate(got) if n != pair]
+    return (own + got[pair]) + (rest[0] + rest[1])
+
+
+def reduce_steps(sems, stages, rows, acc, acc0, send, recv, recv0, gat, gat0):
+    size = rows // 2
+    mine, others, _ = stages[0]
+    base = mine * size
     off = base
-    size = half
     into = recv0
-    out = send0
-    path = []
-    for step, bit in enumerate(order):
-        peer = (ctx + (1 - 2 * lax.rem(ctx // (1 << bit), 2)) * (1 << bit), seq)
-        if step == 0:
-            path.append((peer, off, size))
-            cp = sems.copy(send.at[pl.ds(out, size)], recv.at[pl.ds(into, size)], peer)
-            kept = off
-        elif size % (32 * seqs) == 0:
-            size = size // 2
-            mine = lax.rem(ctx // (1 << bit), 2)
-            kept = off + mine * size
-            away = off + (1 - mine) * size
-            send[pl.ds(out, size), :] = acc[pl.ds(pl.multiple_of(acc0 + away - base, 16), size), :].astype(bf16)
-            path.append((peer, kept, size))
-            cp = sems.copy(send.at[pl.ds(out, size)], recv.at[pl.ds(into, size)], peer)
+
+    def held(at, count):
+        return pl.ds(pl.multiple_of(acc0 + at - base, 16), count)
+
+    cp = sems.copy(send.at[pl.ds(0, size)], recv.at[pl.ds(into, size)], others[0][0])
+    cp.start()
+    yield
+    cp.wait()
+    acc[held(off, size), :] = acc[held(off, size), :] + recv[pl.ds(into, size), :].astype(f32)
+    into += size
+    path = [(others, off, size)]
+    for mine, others, pair in stages[1:]:
+        ways = len(others) + 1
+        split = size % (16 * ways) == 0
+        piece = size // ways if split else size
+        send[pl.ds(0, size), :] = acc[held(off, size), :].astype(bf16)
+        cps = []
+        for n, (device, index) in enumerate(others):
+            start = pl.multiple_of(index * piece, 16) if split else 0
+            cps.append(sems.copy(send.at[pl.ds(start, piece)], recv.at[pl.ds(into + n * piece, piece)], device))
+        for cp in cps:
+            cp.start()
+        yield
+        for cp in cps:
+            cp.wait()
+        got = [recv[pl.ds(into + n * piece, piece), :].astype(f32) for n in range(ways - 1)]
+        into += (ways - 1) * piece
+        if split:
+            off = off + mine * piece
+            size = piece
+            acc[held(off, size), :] = acc[held(off, size), :] + sum(got[1:], got[0])
+            path.append((others, off, size))
         else:
-            send[pl.ds(out, size), :] = acc[pl.ds(pl.multiple_of(acc0 + off - base, 16), size), :].astype(bf16)
-            cp = sems.copy(send.at[pl.ds(out, size)], recv.at[pl.ds(into, size)], peer)
-            kept = off
-        cp.start()
+            acc[held(off, size), :] = add_in_pairs(send[pl.ds(0, size), :].astype(f32), got, pair)
+    gat[pl.ds(pl.multiple_of(gat0 + off, 16), size), :] = acc[held(off, size), :].astype(bf16)
+    for others, off, size in reversed(path):
+        at = pl.ds(pl.multiple_of(gat0 + off, 16), size)
+        cps = [sems.copy(gat.at[at], gat.at[at], device) for device, _ in others]
+        for cp in cps:
+            cp.start()
         yield
-        cp.wait()
-        at = pl.ds(pl.multiple_of(acc0 + kept - base, 16), size)
-        acc[at, :] = acc[at, :] + recv[pl.ds(into, size), :].astype(f32)
-        off = kept
-        into += size
-    piece = size // seqs
-    send[pl.ds(out, size), :] = acc[pl.ds(pl.multiple_of(acc0 + off - base, 16), size), :].astype(bf16)
-    cps = []
-    for d in range(1, seqs):
-        t = lax.rem(seq + d, seqs)
-        cps.append(sems.copy(
-            send.at[pl.ds(pl.multiple_of(out + t * piece, 16), piece)],
-            recv.at[pl.ds(into + (d - 1) * piece, piece)], (ctx, t)))
-    for cp in cps:
-        cp.start()
-    yield
-    for cp in cps:
-        cp.wait()
-    total = acc[pl.ds(pl.multiple_of(acc0 + off - base + seq * piece, 16), piece), :]
-    for d in range(1, seqs):
-        total += recv[pl.ds(into + (d - 1) * piece, piece), :].astype(f32)
-    at = pl.ds(pl.multiple_of(gat0 + off + seq * piece, 16), piece)
-    gat[at, :] = total.astype(bf16)
-    cps = []
-    for d in range(1, seqs):
-        cps.append(sems.copy(gat.at[at], gat.at[at], (ctx, lax.rem(seq + d, seqs))))
-    for cp in cps:
-        cp.start()
-    yield
-    for cp in cps:
-        cp.wait()
-    for peer, kept, size in reversed(path):
-        at = pl.ds(pl.multiple_of(gat0 + kept, 16), size)
-        cp = sems.copy(gat.at[at], gat.at[at], peer)
-        cp.start()
-        yield
-        cp.wait()
+        for cp in cps:
+            cp.wait()
 
 
 def landing_rows(rows, nbits, seqs):
     size = rows // 2
     count = size
-    for _ in range(nbits - 1):
-        if size % (32 * seqs) == 0:
-            size //= 2
-        count += size
-    return count + size // seqs * (seqs - 1)
-
-
-def landing_rows(rows, nbits, seqs):
-    size = rows // 2
-    count = size
-    for _ in range(nbits - 1):
-        if size % (32 * seqs) == 0:
-            size //= 2
-        count += size
-    return count + size // seqs * (seqs - 1)
-
-
-def small_steps(sems, ctx, seq, nbits, seqs, small, send, recv):
-    for b in range(nbits):
-        send[b] = small[...].astype(bf16)
-        peer = (ctx + (1 - 2 * lax.rem(ctx // (1 << b), 2)) * (1 << b), seq)
-        cp = sems.copy(send.at[b], recv.at[b], peer)
-        cp.start()
+    for ways in [1 << len(range(b, min(b + 2, nbits))) for b in range(1, nbits, 2)] + [seqs]:
+        if size % (16 * ways) == 0:
+            size //= ways
+        count += (ways - 1) * size
+    return count
+
+
+def small_steps(sems, stages, small, send, recv):
+    into = 0
+    for k, (_, others, pair) in enumerate(stages):
+        send[k] = small[...].astype(bf16)
+        cps = [sems.copy(send.at[k], recv.at[into + n], device) for n, (device, _) in enumerate(others)]
+        for cp in cps:
+            cp.start()
         yield
-        cp.wait()
-        small[...] = send[b].astype(f32) + recv[b].astype(f32)
-    send[nbits] = small[...].astype(bf16)
-    cps = []
-    for d in range(1, seqs):
-        cps.append(sems.copy(send.at[nbits], recv.at[nbits + d - 1], (ctx, lax.rem(seq + d, seqs))))
-    for cp in cps:
-        cp.start()
-    yield
-    for cp in cps:
-        cp.wait()
-    shares = [send[nbits].astype(f32)] + [recv[nbits + d - 1].astype(f32) for d in range(1, seqs)]
-    total = jnp.zeros_like(shares[0])
-    for o in range(seqs):
-        which = lax.rem(seq - o + seqs, seqs)
-        for d in range(seqs):
-            total += jnp.where(which == d, shares[d], 0.0)
-    small[...] = total
+        for cp in cps:
+            cp.wait()
+        got = [recv[into + n].astype(f32) for n in range(len(others))]
+        into += len(others)
+        small[...] = add_in_pairs(send[k].astype(f32), got, pair)
 
 
 def layer_kernel(
@@ -196,7 +183,7 @@
     mg_ref, ms_ref, wu_ref, ub_ref, wd_ref, db_ref,
     outr, backr, gat, small_ref,
     stage, xall, cotr, marks, n_ref, qaug, kaug, vaug, kt, vtaug, prob, s_ref, ot_ref, rl_ref,
-    att_t, att, act_ref, gh_ref, gml_ref, gaug, dext, erecv, acc, recv, ssend, srecv,
+    att_t, att, act_ref, gh_ref, gml_ref, gaug, dext, erecv, s_more, acc, recv, ssend, srecv,
     local_sem, send_sems, recv_sems, ret_send, ret_recv,
 ):
     copies, tok, width = xin.shape
@@ -231,9 +218,12 @@
             if dc or d:
                 pl.semaphore_signal(
                     barrier, inc=1, device_id=(group + lax.rem(cc + dc, 2), lax.rem(seq + d, seqs)), device_id_type=MESH)
-    for b in range(1, nbits):
-        pl.semaphore_signal(
-            barrier, inc=1, device_id=(ctx + (1 - 2 * lax.rem(ctx // (1 << b), 2)) * (1 << b), seq), device_id_type=MESH)
+    stages = spread(ctx, seq, nbits, seqs)
+    greeted = 2 * seqs - 1
+    for _, others, _ in stages[1:-1]:
+        greeted += len(others)
+        for device, _ in others:
+            pl.semaphore_signal(barrier, inc=1, device_id=device, device_id_type=MESH)
 
     lane = lax.broadcasted_iota(jnp.int32, (1, seqs * tok), 1)
     usable = jnp.where(jnp.logical_or(kept_ref[...] == 1, lane < CLS), 0.0, MASKED)
@@ -280,7 +270,7 @@
         def _():
             moves[0].wait_send()
 
-    pl.semaphore_wait(barrier, 2 * seqs - 1 + nbits - 1)
+    pl.semaphore_wait(barrier, greeted)
     moves = scatter(xall)
     marks_copy = sems.copy(marks.at[0], marks.at[1], sibling)
     marks_copy.start()
@@ -345,19 +335,44 @@
 
     first = jnp.where(lax.broadcasted_iota(jnp.int32, (pw, TILE), 0) == 0, 1.0, 0.0).astype(bf16)
 
-    def forward(i, carry):
-        p = i // tiles
-        at = pl.ds(pl.multiple_of((i % tiles) * TILE, TILE), TILE)
-        s_ref[...] = mm(kaug[p], jnp.concatenate([qaug[p, :, at], first], axis=0))
-        top = jnp.max(s_ref[...], axis=0, keepdims=True)
-        prob[p, :, at] = jnp.exp2((s_ref[...] - top) * expo).astype(bf16)
-        o = mm(vtaug[p], prob[p, :, at])
-        rl = 1.0 / o[pw:pw + 1]
-        ot_ref[p, :, at] = o[0:pw] * rl
+    cut = acc.shape[0] // 2
+    bounds = ((0, cut), (cut, 2 * cut), (2 * cut, rows))
+    even = [s_ref.at[a:b] for a, b in bounds]
+    odd = [acc.at[0:cut], acc.at[cut:2 * cut], s_more]
+    count = pairs * tiles
+
+    def place(t):
+        return t // tiles, pl.ds(pl.multiple_of((t % tiles) * TILE, TILE), TILE)
+
+    def score(t, into, c):
+        p, at = place(t)
+        a, b = bounds[c]
+        value = mm(kaug[p, a:b, :], jnp.concatenate([qaug[p, :, at], first], axis=0))
+        into[c][...] = value
+        return jnp.max(value.reshape((b - a) // 8, 8, TILE), axis=0)
+
+    def weigh(t, scores, top, ahead):
+        p, at = place(t)
+        top = jnp.max(top, axis=0, keepdims=True)
+        tops = []
+        total = None
+        for c, (a, b) in enumerate(bounds):
+            if ahead is not None:
+                tops.append(score(lax.rem(t + 1, count), ahead, c))
+            weights = jnp.exp2((scores[c][...] - top) * expo).astype(bf16)
+            prob[p, a:b, at] = weights
+            part = mm(vtaug[p, :, a:b], weights)
+            total = part if total is None else total + part
+        rl = 1.0 / total[pw:pw + 1]
+        ot_ref[p, :, at] = total[0:pw] * rl
         rl_ref[p, :, at] = rl
-        return carry
-
-    lax.fori_loop(0, pairs * tiles, forward, 0)
+        return jnp.maximum(jnp.maximum(tops[0], tops[1]), tops[2])
+
+    def forward(i, top):
+        return weigh(2 * i + 1, odd, weigh(2 * i, even, top, odd), even)
+
+    tops = [score(0, even, c) for c in range(3)]
+    lax.fori_loop(0, count // 2, forward, jnp.maximum(jnp.maximum(tops[0], tops[1]), tops[2]))
     for p in range(pairs):
         for h in range(2):
             att_t[p * pw + h * hd:p * pw + (h + 1) * hd, :] = ot_ref[
@@ -450,38 +465,29 @@
         acc[acc0:acc0 + half, :] = s_ref[pl.ds(pl.multiple_of(spare + cc * half, 16), half), :]
         send[pl.ds(send0, half), :] = s_ref[pl.ds(pl.multiple_of(spare + (1 - cc) * half, 16), half), :].astype(bf16)
 
-    sets = (ff, ff, 2 * width, 2 * width)
-    starts = [sum(sets[:j]) for j in range(4)]
-    lands = [landing_rows(sets[j], nbits, seqs) for j in range(4)]
-    lands = [sum(lands[:j]) for j in range(4)]
-    lands = [landing_rows(sets[j], nbits, seqs) for j in range(4)]
-    lands = [sum(lands[:j]) for j in range(4)]
-    send_a = act_ref.at[:, 2 * width:3 * width]
-    send_b = act_ref.at[:, 3 * width:4 * width]
-    send_c = gh_ref.at[:, 2 * width:3 * width]
-    send_d = gh_ref.at[:, 3 * width:4 * width]
-    sends = (send_a, send_b, send_c, send_d)
-    bits = list(range(nbits))
-    turned = bits[:1] + bits[:0:-1]
-    orders = (bits, turned, turned, bits)
+    sets = (ff, ff, 2 * width, width, width)
+    starts = [sum(sets[:j]) for j in range(5)]
+    lands = [landing_rows(rows_of, nbits, seqs) for rows_of in sets]
+    lands = [sum(lands[:j]) for j in range(5)]
+    sends = (
+        act_ref.at[:, 2 * width:3 * width], act_ref.at[:, 3 * width:4 * width],
+        gh_ref.at[:, 2 * width:3 * width], gh_ref.at[0:own // 2, 3 * width:4 * width], gh_ref.at[own // 2:own, 3 * width:4 * width])
     steps = [
-        reduce_steps(sems, ctx, seq, orders[j], seqs, sets[j], acc, starts[j] // 2, sends[j], 0, recv, lands[j], gat, starts[j])
-        for j in range(4)
+        reduce_steps(sems, stages, sets[j], acc, starts[j] // 2, sends[j], recv, lands[j], gat, starts[j])
+        for j in range(5)
     ]
-    running = []
-
-    def turn():
-        for g in list(running):
-            if next(g, "done") == "done":
-                running.remove(g)
-
-    split(mm(act_ref[...], cotr[...].reshape(own, width), TN), ff, starts[0] // 2, send_a, 0)
+
+    def turn(*which):
+        for j in which:
+            next(steps[j], None)
+
+    split(mm(act_ref[...], cotr[...].reshape(own, width), TN), ff, starts[0] // 2, sends[0], 0)
+    turn(0)
     up = mm(att[...], gh_ref[...], TN)
     up = jnp.concatenate([up[:, j * width:(j + 1) * width] for j in range(ff // width)], axis=0)
-    split(up, ff, starts[1] // 2, send_b, 0)
-    running += [steps[0], steps[1]]
-    turn()
-    split(mm(att_t[...], gml_ref[...]), width, starts[2] // 2, send_c, 0)
+    split(up, ff, starts[1] // 2, sends[1], 0)
+    turn(1)
+    split(mm(att_t[...], gml_ref[...]), width, starts[2] // 2, sends[2], 0)
 
     sub = lax.broadcasted_iota(jnp.int32, (16, own), 0)
     for p in range(pairs):
@@ -494,60 +500,67 @@
             coarse = delta.astype(bf16).astype(f32)
             dext[p, :, lanes] = jnp.where(sub == 0, coarse, jnp.where(sub == 1, delta - coarse, 0.0)).astype(bf16)
 
+    turn(0, 1)
     for p in range(pairs):
         for half in range(2):
             lanes = slice(half * width + p * pw, half * width + (p + 1) * pw)
             act_ref[:, lanes] = mm(prob[p, half * own:(half + 1) * own, :], gaug[p], NT).astype(bf16)
-        turn()
     dv_own, dv_sib = act_ref.at[:, 0:width], act_ref.at[:, width:2 * width]
     dk_own, dk_sib = gh_ref.at[:, 0:width], gh_ref.at[:, width:2 * width]
     split(mm(n_ref[0:own, :], dv_own[...], TN) + mm(n_ref[own:rows, :], dv_sib[...], TN),
-          width, (starts[2] + width) // 2, send_c, width // 2)
-    running.append(steps[2])
-    turn()
-    nothing = jnp.zeros((pw - 16, TILE), bf16)
+          width, (starts[2] + width) // 2, sends[2], width // 2)
+    turn(0, 1, 2)
+    wide = 3 * TILE
+    nothing = jnp.zeros((pw - 16, wide), bf16)
 
     def backward(i, carry):
-        p = i // tiles
-        at = pl.ds(pl.multiple_of((i % tiles) * TILE, TILE), TILE)
+        p = i // 3
+        at = pl.ds(pl.multiple_of((i % 3) * wide, TILE), wide)
         right = jnp.concatenate([gaug[p, :, at], dext[p, :, at], nothing], axis=0)
-        ds = prob[p, :, at] * mm(vaug[p], right).astype(bf16)
-        prob[p, :, at] = ds
-        dq = mm(kt[pl.ds(pl.multiple_of(p * pw, pw), pw), :], ds)
-        ot_ref[p, :, at] = dq * scale
+        total = None
+        for a, b in bounds:
+            ds = prob[p, a:b, at] * mm(vaug[p, a:b, :], right).astype(bf16)
+            prob[p, a:b, at] = ds
+            part = mm(kt[pl.ds(pl.multiple_of(p * pw, pw), pw), a:b], ds)
+            total = part if total is None else total + part
+        ot_ref[p, :, at] = total * scale
         return carry
 
-    for p in range(pairs):
-        for part in range(3):
-            lax.fori_loop(p * tiles + part * tiles // 3, p * tiles + (part + 1) * tiles // 3, backward, 0)
-            turn()
-    for p in range(pairs):
-        for half in range(2):
-            lanes = slice(half * width + p * pw, half * width + (p + 1) * pw)
-            gh_ref[:, lanes] = (mm(prob[p, half * own:(half + 1) * own, :], qaug[p], NT) * scale).astype(bf16)
-        turn()
-    left(out_moves)
-
-    def other_rows(i, carry):
-        at = pl.ds(pl.multiple_of(i * chunk, 16), chunk)
-        gml_ref[at, :] = (mm(dk_sib[at, :], wk_ref[...], NT) + mm(dv_sib[at, :], wv_ref[...], NT)).astype(bf16)
-        return carry
-
-    lax.fori_loop(0, nchunk, other_rows, 0)
-    e_copy = sems.copy(gml_ref, erecv, sibling)
-    e_copy.start()
-    turn()
+    lax.fori_loop(0, 3, backward, 0)
+    turn(0, 1, 2)
+    lax.fori_loop(3, 6, backward, 0)
+    turn(0, 1, 2)
     for p in range(pairs):
         for h in range(2):
             att_t[p * pw + h * hd:p * pw + (h + 1) * hd, :] = ot_ref[
                 p, h * hd:(h + 1) * hd, h * head_cols:h * head_cols + own
             ].astype(bf16)
     att[...] = jnp.transpose(att_t[...])
-    split(mm(n_ref[0:own, :], att[...], TN), width, starts[3] // 2, send_d, 0)
+    split(mm(n_ref[0:own, :], att[...], TN), width, starts[3] // 2, sends[3], 0)
+    turn(3)
+
+    def key_grads(half):
+        for p in range(pairs):
+            lanes = slice(half * width + p * pw, half * width + (p + 1) * pw)
+            gh_ref[:, lanes] = (mm(prob[p, half * own:(half + 1) * own, :], qaug[p], NT) * scale).astype(bf16)
+
+    key_grads(1)
+    left(out_moves)
+
+    def other_rows(i, carry):
+        at = pl.ds(pl.multiple_of(i * chunk, 16), chunk)
+        gml_ref[at, :] = (mm(dk_sib[at, :], wk_ref[...], NT) + mm(dv_sib[at, :], wv_ref[...], NT)).astype(bf16)
+        return carry
+
+    lax.fori_loop(0, nchunk, other_rows, 0)
+    e_copy = sems.copy(gml_ref, erecv, sibling)
+    e_copy.start()
+    turn(2, 3)
+    key_grads(0)
+    turn(0, 1, 2, 3)
     split(mm(n_ref[0:own, :], dk_own[...], TN) + mm(n_ref[own:rows, :], dk_sib[...], TN),
-          width, (starts[3] + width) // 2, send_d, width // 2)
-    running.append(steps[3])
-    turn()
+          width, starts[4] // 2, sends[4], 0)
+    turn(4)
 
     def own_rows(i, carry):
         at = pl.ds(pl.multiple_of(i * chunk, 16), chunk)
@@ -557,44 +570,70 @@
         return carry
 
     lax.fori_loop(0, nchunk, own_rows, 0)
-    turn()
+    turn(4)
     e_copy.wait()
 
-    def last_rows(i, carry):
-        at = pl.ds(pl.multiple_of(i * chunk, 16), chunk)
-        n, rstd = norm_parts(xall[i].astype(f32))
-        e = s_ref[pl.ds(pl.multiple_of(own + i * chunk, 16), chunk), :] + erecv[at, :].astype(f32)
-        stage[i] = (s_ref[at, :] + norm_back(e * gain, n, rstd)).astype(bf16)
-        return carry[0] + colsum(e * n), carry[1] + colsum(e)
-
-    sums = lax.fori_loop(0, nchunk, last_rows, (zero, zero))
+    moves = [back_copy(0, backr, 1), back_copy(1, backr, 1)]
+    sums = (zero, zero)
+    for k in range(2):
+        at = slice(k * chunk, (k + 1) * chunk)
+        n, rstd = norm_parts(xall[k].astype(f32))
+        e = s_ref[own + k * chunk:own + (k + 1) * chunk, :] + erecv[at, :].astype(f32)
+        stage[k] = (s_ref[at, :] + norm_back(e * gain, n, rstd)).astype(bf16)
+        sums = (sums[0] + colsum(e * n), sums[1] + colsum(e))
+        if k:
+            moves[1].start()
+        else:
+            @pl.when(jnp.logical_not(stay))
+            def _():
+                moves[0].start()
+
+            @pl.when(stay)
+            def _():
+                backr[lax.rem(seq, 2)] = stage[0]
     small_ref[ups:ups + 1, :] = sums[0]
     small_ref[ups + 1:ups + 2, :] = sums[1]
     small_ref[ups + 2:, :] = jnp.zeros((small_ref.shape[0] - ups - 2, width), f32)
-    back_moves = send_home(backr, 1)
-    running.append(small_steps(sems, ctx, seq, nbits, seqs, small_ref, ssend, srecv))
-    while running:
-        turn()
-    left(back_moves)
+    steps.append(small_steps(sems, stages, small_ref, ssend, srecv))
+    for _ in range(len(stages) * 2):
+        turn(5, 0, 1, 2, 3, 4)
+    left(moves)
     home_again(outr, 0)
     home_again(backr, 1)
 
 
-def unpack_kernel(cot_ref, outr, backr, gat, small, *outs):
-    copies, tok, width = cot_ref.shape
+def unpack_kernel(cot_hbm, outr_hbm, backr_hbm, gat_hbm, small_hbm, *refs):
+    outs, (cot_ref, outr, backr, gat, small, sems) = refs[:15], refs[15:]
     (out, xg, ag, as_, wq, wk, wv, wo, ob, mg, ms, wu, ub, wd, db) = outs
+    copies = [
+        pltpu.make_async_copy(src, dst, sems.at[k])
+        for k, (src, dst) in enumerate(
+            ((gat_hbm, gat), (outr_hbm, outr), (backr_hbm, backr), (cot_hbm, cot_ref), (small_hbm, small)))
+    ]
+    for cp in copies:
+        cp.start()
+    _, tok, width = cot_ref.shape
     ff = wd.shape[0]
-    out[...] = outr[:, 0:tok, :]
-    xg[...] = cot_ref[...] + backr[:, 0:tok, :].astype(f32)
+    half = width // 2
+    copies[0].wait()
     wd[...] = gat[0:ff, :].astype(f32)
     for j in range(ff // width):
         wu[:, j * width:(j + 1) * width] = gat[ff + j * width:ff + (j + 1) * width, :].astype(f32)
-        ub[0:1, j * width:(j + 1) * width] = small[4 + j:5 + j, :]
-    half = width // 2
-    for j, ref in enumerate((wo, wv, wq, wk)):
-        at = 2 * ff + j // 2 * 2 * width + j % 2 * half
+    for j, ref in enumerate((wo, wv)):
+        at = 2 * ff + j * half
         ref[0:half, :] = gat[at:at + half, :].astype(f32)
         ref[half:width, :] = gat[at + width:at + width + half, :].astype(f32)
+    for j, ref in enumerate((wq, wk)):
+        at = 2 * ff + (2 + j) * width
+        ref[...] = gat[at:at + width, :].astype(f32)
+    copies[1].wait()
+    out[...] = outr[:, 0:tok, :]
+    copies[2].wait()
+    copies[3].wait()
+    xg[...] = cot_ref[...] + backr[:, 0:tok, :].astype(f32)
+    copies[4].wait()
+    for j in range(ff // width):
+        ub[0:1, j * width:(j + 1) * width] = small[4 + j:5 + j, :]
     ups = 4 + ff // width
     for j, ref in ((0, db), (1, ob), (2, mg), (3, ms), (ups, ag), (ups + 1, as_)):
         ref[...] = small[j:j + 1, :]
@@ -615,9 +654,13 @@
     pairs = HEADS // 2
     pw = width // 2
     grad_rows = 2 * ff + 4 * width
-    landing = 2 * landing_rows(ff, nbits, seqs) + 2 * landing_rows(2 * width, nbits, seqs)
-    landing = 2 * landing_rows(ff, nbits, seqs) + 2 * landing_rows(2 * width, nbits, seqs)
-    ncopy = 2 + 1 + 2 + 2 + 1 + 4 * (2 * nbits + 2 * (seqs - 1)) + nbits + seqs - 1
+    sets = (ff, ff, 2 * width, width, width)
+    landing = sum(landing_rows(r, nbits, seqs) for r in sets)
+    peers = 1 + sum((1 << len(range(b, min(b + 2, nbits)))) - 1 for b in range(1, nbits, 2)) + seqs - 1
+    sets = (ff, ff, 2 * width, width, width)
+    landing = sum(landing_rows(r, nbits, seqs) for r in sets)
+    peers = 1 + sum((1 << len(range(b, min(b + 2, nbits)))) - 1 for b in range(1, nbits, 2)) + seqs - 1
+    ncopy = 8 + (2 * len(sets) + 1) * peers
     home = jax.ShapeDtypeStruct((copies, tokp, width), bf16)
     outr, backr, gat, small = pl.pallas_call(
         partial(layer_kernel, nbits, seqs),
@@ -651,10 +694,11 @@
             pltpu.VMEM((pairs, pw, cols), bf16),
             pltpu.VMEM((pairs, 16, cols), bf16),
             pltpu.VMEM((own, width), bf16),
+            pltpu.VMEM((rows - grad_rows // 2, TILE), f32),
             pltpu.VMEM((grad_rows // 2, width), f32),
             pltpu.VMEM((landing, width), bf16),
             pltpu.VMEM((nbits + 1, 16, width), bf16),
-            pltpu.VMEM((nbits + seqs, 16, width), bf16),
+            pltpu.VMEM((peers, 16, width), bf16),
             pltpu.SemaphoreType.DMA,
             pltpu.SemaphoreType.DMA((ncopy,)),
             pltpu.SemaphoreType.DMA((ncopy,)),
@@ -675,9 +719,13 @@
             jax.ShapeDtypeStruct((width, ff), f32), jax.ShapeDtypeStruct((1, ff), f32),
             jax.ShapeDtypeStruct((ff, width), f32), line,
         ),
-        in_specs=[vmem] * 5,
+        in_specs=[hbm] * 5,
         out_specs=(vmem,) * 15,
-        compiler_params=pltpu.CompilerParams(vmem_limit_bytes=32 * 2**20),
+        scratch_shapes=[
+            pltpu.VMEM(cotangent.shape, f32), pltpu.VMEM(home.shape, bf16), pltpu.VMEM(home.shape, bf16),
+            pltpu.VMEM((grad_rows, width), bf16), pltpu.VMEM((16, width), f32), pltpu.SemaphoreType.DMA((5,)),
+        ],
+        compiler_params=pltpu.CompilerParams(vmem_limit_bytes=63 * 2**20),
         name="unpack",
     )(cotangent, outr, backr, gat, small)
     return tuple(o.reshape(-1) if o.shape[0] == 1 else o for o in outs)

time: 143 us -> 109 us (0.76)
  Pallas kernels: 136 us -> 108 us
  local copies, waits for them, and re-layouts: 5.49 us -> 0 us
    pallas_call x1, Pallas kernels: 134 us -> 104 us  [body(): pl.pallas_call(partial(layer_kernel, nbits, seqs), out_shape=(home, home,...]
    unnamed x10 -> x0, local copies, waits for them, and re-layouts: 5.49 us -> none
    pallas_call x1, Pallas kernels: 2.56 us -> 4.45 us  [body(): pl.pallas_call(unpack_kernel, out_shape=(jax.ShapeDtypeStruct((copies, to...]
where the time goes in v4:
time: 109 us
  Pallas kernels  108 us (99%)
    pallas_call x1, Pallas kernels, body(): pl.pallas_call(partial(layer_kernel, nbits, seqs), out_shape=(home, home,...  104 us
    pallas_call x1, Pallas kernels, body(): pl.pallas_call(unpack_kernel, out_shape=(jax.ShapeDtypeStruct((copies, to...  4.45 us

profile of v4, /device:TPU:0, one launch (start us, length us, event | category | flops | bytes accessed | tf_op | source)
XLA Modules:
  0.0 109.3 jit_solution(4698501629446828818)
XLA Ops:
  0.7 104.0 %layer.1 = (bf16[2,560,256]{2,1,0:T(8,128)(2,1)}, bf16[2,560,256]{2,1,0:T(8,128)(2,1)}, bf16[3072,256]{1,0:T(8,128)(2,1)}, f32[16,256]{1,0:T(8,128)}) custom-call(bf16[2,552,256]{2,1,0:T(8,128)(2,1)} %xin.1, s32[2,2208]{1,0:T(2,128)} %kept_ref.1, f32[1104,256]{1,0:T(8,128)} %bitcast.8, bf16[256]{0:T(256)(128)(2,1)} %ag_ref.1, bf16[256]{0:T(256)(128)(2,1)} %as_ref.1, ...), custom_call_target="tpu_custom_call" | custom-call | tf_op jit(solution)/shard_map/layer/pallas_call | solution.py:665
  104.6 4.4 %unpack.1 = (bf16[2,552,256]{2,1,0:T(8,128)(2,1)}, f32[2,552,256]{2,1,0:T(8,128)}, f32[1,256]{1,0:T(1,128)}, f32[1,256]{1,0:T(1,128)}, f32[256,256]{1,0:T(8,128)...) custom-call(f32[2,552,256]{2,1,0:T(8,128)} %cot_hbm.1, ...), custom_call_target="tpu_custom_call" | custom-call | tf_op jit(solution)/shard_map/unpack/pallas_call | solution.py:714

commit v5 on v4

--- a/solution.py
+++ b/solution.py
@@ -74,10 +74,13 @@
             device_id=device, device_id_type=MESH)
 
 
-def spread(ctx, seq, nbits, seqs):
+def bit_groups(nbits, first):
+    return [tuple(range(first))] + [tuple(range(b, min(b + 2, nbits))) for b in range(first, nbits, 2)]
+
+
+def spread(ctx, seq, nbits, seqs, first):
     stages = []
-    groups = [(0,)] + [tuple(range(b, min(b + 2, nbits))) for b in range(1, nbits, 2)]
-    for bits in groups:
+    for bits in bit_groups(nbits, first):
         place = [lax.rem(ctx // (1 << b), 2) for b in bits]
         others = []
         for r in range(1, 1 << len(bits)):
@@ -88,36 +91,46 @@
                 index = index + there * (1 << k)
             others.append(((device, seq), index))
         mine = sum(p * (1 << k) for k, p in enumerate(place))
-        stages.append((mine, others, 0))
-    stages.append((seq, [((ctx, lax.rem(seq + d, seqs)), lax.rem(seq + d, seqs)) for d in range(1, seqs)], seqs // 2 - 1))
+        stages.append((mine, others, list(range(len(others) + 1))))
+    half = seqs // 2
+    stages.append((
+        seq, [((ctx, lax.rem(seq + d, seqs)), lax.rem(seq + d, seqs)) for d in range(1, seqs)],
+        [n // 2 + n % 2 * half for n in range(seqs)]))
     return stages
 
 
-def add_in_pairs(own, got, pair):
-    if len(got) == 1:
-        return own + got[0]
-    rest = [g for n, g in enumerate(got) if n != pair]
-    return (own + got[pair]) + (rest[0] + rest[1])
-
-
-def reduce_steps(sems, stages, rows, acc, acc0, send, recv, recv0, gat, gat0):
-    size = rows // 2
-    mine, others, _ = stages[0]
-    base = mine * size
-    off = base
+def add_in_pairs(values, order):
+    values = [values[n] for n in order]
+    while len(values) > 1:
+        values = [a + b for a, b in zip(values[::2], values[1::2])]
+    return values[0]
+
+
+def reduce_steps(sems, stages, rows, acc, acc0, send, recv, recv0, gat, gat0, split_first, done):
     into = recv0
+    path = []
+    if split_first:
+        size = rows // 2
+        mine, others, _ = stages[0]
+        off = mine * size
+    else:
+        size = rows
+        off = 0
+    base = off
 
     def held(at, count):
         return pl.ds(pl.multiple_of(acc0 + at - base, 16), count)
 
-    cp = sems.copy(send.at[pl.ds(0, size)], recv.at[pl.ds(into, size)], others[0][0])
-    cp.start()
-    yield
-    cp.wait()
-    acc[held(off, size), :] = acc[held(off, size), :] + recv[pl.ds(into, size), :].astype(f32)
-    into += size
-    path = [(others, off, size)]
-    for mine, others, pair in stages[1:]:
+    if split_first:
+        cp = sems.copy(send.at[pl.ds(0, size)], recv.at[pl.ds(into, size)], others[0][0])
+        cp.start()
+        yield
+        cp.wait()
+        acc[held(off, size), :] = acc[held(off, size), :] + recv[pl.ds(into, size), :].astype(f32)
+        into += size
+        path.append((others, off, size))
+        stages = stages[1:]
+    for mine, others, order in stages:
         ways = len(others) + 1
         split = size % (16 * ways) == 0
         piece = size // ways if split else size
@@ -139,7 +152,7 @@
             acc[held(off, size), :] = acc[held(off, size), :] + sum(got[1:], got[0])
             path.append((others, off, size))
         else:
-            acc[held(off, size), :] = add_in_pairs(send[pl.ds(0, size), :].astype(f32), got, pair)
+            acc[held(off, size), :] = add_in_pairs([send[pl.ds(0, size), :].astype(f32)] + got, order)
     gat[pl.ds(pl.multiple_of(gat0 + off, 16), size), :] = acc[held(off, size), :].astype(bf16)
     for others, off, size in reversed(path):
         at = pl.ds(pl.multiple_of(gat0 + off, 16), size)
@@ -149,21 +162,26 @@
         yield
         for cp in cps:
             cp.wait()
-
-
-def landing_rows(rows, nbits, seqs):
-    size = rows // 2
-    count = size
-    for ways in [1 << len(range(b, min(b + 2, nbits))) for b in range(1, nbits, 2)] + [seqs]:
+    done()
+
+
+def landing_rows(rows, nbits, seqs, split_first):
+    ways_of = [1 << len(bits) for bits in bit_groups(nbits, 1 if split_first else 3)] + [seqs]
+    count = 0
+    size = rows
+    if split_first:
+        size = count = rows // 2
+        ways_of = ways_of[1:]
+    for ways in ways_of:
         if size % (16 * ways) == 0:
             size //= ways
         count += (ways - 1) * size
     return count
 
 
-def small_steps(sems, stages, small, send, recv):
+def small_steps(sems, stages, small, send, recv, done):
     into = 0
-    for k, (_, others, pair) in enumerate(stages):
+    for k, (_, others, order) in enumerate(stages):
         send[k] = small[...].astype(bf16)
         cps = [sems.copy(send.at[k], recv.at[into + n], device) for n, (device, _) in enumerate(others)]
         for cp in cps:
@@ -173,20 +191,21 @@
             cp.wait()
         got = [recv[into + n].astype(f32) for n in range(len(others))]
         into += len(others)
-        small[...] = add_in_pairs(send[k].astype(f32), got, pair)
+        small[...] = add_in_pairs([send[k].astype(f32)] + got, order)
+    done()
 
 
 def layer_kernel(
     nbits, seqs,
-    xin, kept_ref, cot_hbm,
+    xin_hbm, kept_ref, cot_hbm,
     ag_ref, as_ref, wq_ref, wk_ref, wv_ref, wo_ref, ob_ref,
     mg_ref, ms_ref, wu_ref, ub_ref, wd_ref, db_ref,
-    outr, backr, gat, small_ref,
-    stage, xall, cotr, marks, n_ref, qaug, kaug, vaug, kt, vtaug, prob, s_ref, ot_ref, rl_ref,
+    outr, backr, gat_hbm, small_hbm,
+    gat, small_ref, xin, stage, xall, cotr, marks, n_ref, qaug, kaug, vaug, kt, vtaug, prob, s_ref, ot_ref, rl_ref,
     att_t, att, act_ref, gh_ref, gml_ref, gaug, dext, erecv, s_more, acc, recv, ssend, srecv,
-    local_sem, send_sems, recv_sems, ret_send, ret_recv,
+    local_sems, send_sems, recv_sems, ret_send, ret_recv,
 ):
-    copies, tok, width = xin.shape
+    copies, tok, width = xin_hbm.shape
     tokp = xall.shape[1]
     own = 2 * tokp
     rows = 2 * own
@@ -209,7 +228,9 @@
     sibling = (group + 1 - cc, seq)
     stay = seq // 2 == cc
 
-    cot_in = pltpu.make_async_copy(cot_hbm, s_ref.at[pl.ds(0, 2 * tok)], local_sem)
+    keep_in = pltpu.make_async_copy(xin_hbm, xin, local_sems.at[0])
+    keep_in.start()
+    cot_in = pltpu.make_async_copy(cot_hbm, s_ref.at[pl.ds(0, 2 * tok)], local_sems.at[1])
     cot_in.start()
 
     barrier = pltpu.get_barrier_semaphore()
@@ -218,12 +239,13 @@
             if dc or d:
                 pl.semaphore_signal(
                     barrier, inc=1, device_id=(group + lax.rem(cc + dc, 2), lax.rem(seq + d, seqs)), device_id_type=MESH)
-    stages = spread(ctx, seq, nbits, seqs)
-    greeted = 2 * seqs - 1
-    for _, others, _ in stages[1:-1]:
-        greeted += len(others)
-        for device, _ in others:
-            pl.semaphore_signal(barrier, inc=1, device_id=device, device_id_type=MESH)
+    stages = spread(ctx, seq, nbits, seqs, 1)
+    stages_flat = spread(ctx, seq, nbits, seqs, min(nbits, 3))
+    met = [device for device, _ in stages_flat[0][1][1:]]
+    met += [device for _, others, _ in stages_flat[1:-1] for device, _ in others]
+    for device in met:
+        pl.semaphore_signal(barrier, inc=1, device_id=device, device_id_type=MESH)
+    greeted = 2 * seqs - 1 + len(met)
 
     lane = lax.broadcasted_iota(jnp.int32, (1, seqs * tok), 1)
     usable = jnp.where(jnp.logical_or(kept_ref[...] == 1, lane < CLS), 0.0, MASKED)
@@ -235,6 +257,7 @@
             [usable[:, sh * tok:(sh + 1) * tok], jnp.full((1, wide - tok), MASKED, f32)], axis=1)
         marks[0, sh] = jnp.where(sub == 0, piece, 0.0).astype(bf16)
     stage[:, tokp - 16:tokp, :] = jnp.zeros((copies, 16, width), bf16)
+    keep_in.wait()
     stage[:, 0:tok, :] = xin[...]
 
     def out_copy(k, dst):
@@ -270,6 +293,14 @@
         def _():
             moves[0].wait_send()
 
+    qaug[...] = jnp.zeros_like(qaug)
+    gaug[...] = jnp.zeros_like(gaug)
+    dext[...] = jnp.zeros_like(dext)
+    lane = lax.broadcasted_iota(jnp.int32, (rows, pw), 1)
+    sub = lax.broadcasted_iota(jnp.int32, (16, rows), 0)
+    for p in range(pairs):
+        vaug[p, :, pw:2 * pw] = jnp.where(lane < 2, 1.0, 0.0).astype(bf16)
+        vtaug[p, pw:pw + 16, :] = jnp.where(sub == 0, 1.0, 0.0).astype(bf16)
     pl.semaphore_wait(barrier, greeted)
     moves = scatter(xall)
     marks_copy = sems.copy(marks.at[0], marks.at[1], sibling)
@@ -306,10 +337,6 @@
     unit = jnp.where(
         lax.broadcasted_iota(jnp.int32, (16, pw), 0) == lax.broadcasted_iota(jnp.int32, (16, pw), 1), 1.0, 0.0
     ).astype(bf16)
-    lane = lax.broadcasted_iota(jnp.int32, (rows, pw), 1)
-    ones = jnp.where(lane < 2, 1.0, 0.0).astype(bf16)
-    for p in range(pairs):
-        vaug[p, :, pw:2 * pw] = ones
     for pos in range(4):
         side = cc if pos < 2 else 1 - cc
         mark = marks[held, 2 * side + lax.rem(seq + pos, 2)]
@@ -317,9 +344,6 @@
         for p in range(pairs):
             kaug[p, pos * tokp:(pos + 1) * tokp, pw:2 * pw] = bias
     qt = mm(wq_ref[...], n_ref[0:own, :], TT).astype(bf16)
-    qaug[...] = jnp.zeros_like(qaug)
-    gaug[...] = jnp.zeros_like(gaug)
-    dext[...] = jnp.zeros_like(dext)
     for p in range(pairs):
         for h in range(2):
             qaug[p, h * hd:(h + 1) * hd, h * head_cols:h * head_cols + own] = qt[p * pw + h * hd:p * pw + (h + 1) * hd, :]
@@ -328,14 +352,12 @@
         project(2 + k)
     kt[...] = mm(wk_ref[...], n_ref[...], TT).astype(bf16)
     vt = mm(wv_ref[...], n_ref[...], TT).astype(bf16)
-    sub = lax.broadcasted_iota(jnp.int32, (16, rows), 0)
     for p in range(pairs):
         vtaug[p, 0:pw, :] = vt[p * pw:(p + 1) * pw, :]
-        vtaug[p, pw:pw + 16, :] = jnp.where(sub == 0, 1.0, 0.0).astype(bf16)
 
     first = jnp.where(lax.broadcasted_iota(jnp.int32, (pw, TILE), 0) == 0, 1.0, 0.0).astype(bf16)
 
-    cut = acc.shape[0] // 2
+    cut = (rows - s_more.shape[0]) // 2
     bounds = ((0, cut), (cut, 2 * cut), (2 * cut, rows))
     even = [s_ref.at[a:b] for a, b in bounds]
     odd = [acc.at[0:cut], acc.at[cut:2 * cut], s_more]
@@ -431,19 +453,29 @@
             src_ref=stage.at[k], dst_ref=dst.at[b], send_sem=ret_send.at[2 * sem + k], recv_sem=ret_recv.at[2 * sem + b],
             device_id=(group + seq // 2, 2 * cc + lax.rem(seq + k, 2)), device_id_type=MESH)
 
-    def send_home(dst, sem):
-        moves = [back_copy(0, dst, sem), back_copy(1, dst, sem)]
-        moves[1].start()
+    def send_block(move, k, dst, sem):
+        if k:
+            move.start()
+            return
 
         @pl.when(jnp.logical_not(stay))
         def _():
-            moves[0].start()
+            move.start()
 
         @pl.when(stay)
         def _():
-            dst[lax.rem(seq, 2)] = stage[0]
-
-        return moves
+            pltpu.make_async_copy(stage.at[0], dst.at[lax.rem(seq, 2)], local_sems.at[2 + sem]).start()
+
+    def left_home(moves, dst, sem):
+        moves[1].wait_send()
+
+        @pl.when(jnp.logical_not(stay))
+        def _():
+            moves[0].wait_send()
+
+        @pl.when(stay)
+        def _():
+            pltpu.make_async_copy(stage.at[0], dst.at[lax.rem(seq, 2)], local_sems.at[2 + sem]).wait()
 
     def home_again(dst, sem):
         for b in range(2):
@@ -455,25 +487,37 @@
                     src_ref=stage.at[b], dst_ref=dst.at[b], send_sem=ret_send.at[2 * sem + b],
                     recv_sem=ret_recv.at[2 * sem + b], device_id=sibling, device_id_type=MESH).wait_recv()
 
-    out_moves = send_home(outr, 0)
-
-    spare = own
-
-    def split(value, count, acc0, send, send0, at=0):
-        s_ref[spare:spare + count, :] = value
-        half = count // 2
-        acc[acc0:acc0 + half, :] = s_ref[pl.ds(pl.multiple_of(spare + cc * half, 16), half), :]
-        send[pl.ds(send0, half), :] = s_ref[pl.ds(pl.multiple_of(spare + (1 - cc) * half, 16), half), :].astype(bf16)
+    out_moves = [back_copy(0, outr, 0), back_copy(1, outr, 0)]
+    for k in range(2):
+        send_block(out_moves[k], k, outr, 0)
 
     sets = (ff, ff, 2 * width, width, width)
+    halved = (True, True, False, False, False)
     starts = [sum(sets[:j]) for j in range(5)]
-    lands = [landing_rows(rows_of, nbits, seqs) for rows_of in sets]
+    lands = [landing_rows(sets[j], nbits, seqs, halved[j]) for j in range(5)]
     lands = [sum(lands[:j]) for j in range(5)]
+    kept = [sets[j] // 2 if halved[j] else sets[j] for j in range(5)]
+    kept = [sum(kept[:j]) for j in range(5)]
     sends = (
         act_ref.at[:, 2 * width:3 * width], act_ref.at[:, 3 * width:4 * width],
         gh_ref.at[:, 2 * width:3 * width], gh_ref.at[0:own // 2, 3 * width:4 * width], gh_ref.at[own // 2:own, 3 * width:4 * width])
+    written = []
+
+    def write_out(j):
+        at = pl.ds(starts[j], sets[j])
+        copy = pltpu.make_async_copy(gat.at[at], gat_hbm.at[at], local_sems.at[4 + j])
+        copy.start()
+        written.append(copy)
+
+    def write_small():
+        copy = pltpu.make_async_copy(small_ref, small_hbm, local_sems.at[9])
+        copy.start()
+        written.append(copy)
+
     steps = [
-        reduce_steps(sems, stages, sets[j], acc, starts[j] // 2, sends[j], recv, lands[j], gat, starts[j])
+        reduce_steps(
+            sems, stages if halved[j] else stages_flat, sets[j], acc, kept[j], sends[j], recv, lands[j], gat, starts[j],
+            halved[j], partial(write_out, j))
         for j in range(5)
     ]
 
@@ -481,13 +525,22 @@
         for j in which:
             next(steps[j], None)
 
-    split(mm(act_ref[...], cotr[...].reshape(own, width), TN), ff, starts[0] // 2, sends[0], 0)
+    def split(j, make, half):
+        acc[kept[j]:kept[j] + half, :] = make(cc)
+        sends[j][0:half, :] = make(1 - cc).astype(bf16)
+
+    def part(w, count):
+        return pl.ds(pl.multiple_of(w * count, 128), count)
+
+    def up_half(w):
+        value = mm(att[...], gh_ref[:, part(w, ff // 2)], TN)
+        return jnp.concatenate([value[:, j * width:(j + 1) * width] for j in range(ff // width // 2)], axis=0)
+
+    split(0, lambda w: mm(act_ref[:, part(w, ff // 2)], cotr[...].reshape(own, width), TN), ff // 2)
     turn(0)
-    up = mm(att[...], gh_ref[...], TN)
-    up = jnp.concatenate([up[:, j * width:(j + 1) * width] for j in range(ff // width)], axis=0)
-    split(up, ff, starts[1] // 2, sends[1], 0)
+    split(1, up_half, ff // 2)
     turn(1)
-    split(mm(att_t[...], gml_ref[...]), width, starts[2] // 2, sends[2], 0)
+    acc[kept[2]:kept[2] + width, :] = mm(att_t[...], gml_ref[...])
 
     sub = lax.broadcasted_iota(jnp.int32, (16, own), 0)
     for p in range(pairs):
@@ -507,9 +560,8 @@
             act_ref[:, lanes] = mm(prob[p, half * own:(half + 1) * own, :], gaug[p], NT).astype(bf16)
     dv_own, dv_sib = act_ref.at[:, 0:width], act_ref.at[:, width:2 * width]
     dk_own, dk_sib = gh_ref.at[:, 0:width], gh_ref.at[:, width:2 * width]
-    split(mm(n_ref[0:own, :], dv_own[...], TN) + mm(n_ref[own:rows, :], dv_sib[...], TN),
-          width, (starts[2] + width) // 2, sends[2], width // 2)
-    turn(0, 1, 2)
+    acc[kept[2] + width:kept[2] + 2 * width, :] = mm(n_ref[0:own, :], dv_own[...], TN) + mm(n_ref[own:rows, :], dv_sib[...], TN)
+    turn(2)
     wide = 3 * TILE
     nothing = jnp.zeros((pw - 16, wide), bf16)
 
@@ -526,117 +578,121 @@
         ot_ref[p, :, at] = total * scale
         return carry
 
-    lax.fori_loop(0, 3, backward, 0)
-    turn(0, 1, 2)
-    lax.fori_loop(3, 6, backward, 0)
-    turn(0, 1, 2)
+    lax.fori_loop(0, 1, backward, 0)
+    turn(0, 1)
+    lax.fori_loop(1, 4, backward, 0)
+    turn(2)
+    lax.fori_loop(4, 5, backward, 0)
+    turn(0, 1)
+    lax.fori_loop(5, 6, backward, 0)
     for p in range(pairs):
         for h in range(2):
             att_t[p * pw + h * hd:p * pw + (h + 1) * hd, :] = ot_ref[
                 p, h * hd:(h + 1) * hd, h * head_cols:h * head_cols + own
             ].astype(bf16)
     att[...] = jnp.transpose(att_t[...])
-    split(mm(n_ref[0:own, :], att[...], TN), width, starts[3] // 2, sends[3], 0)
-    turn(3)
-
-    def key_grads(half):
+    acc[kept[3]:kept[3] + width, :] = mm(n_ref[0:own, :], att[...], TN)
+    turn(2, 3)
+    left_home(out_moves, outr, 0)
+
+    def key_grads(pos):
+        half, k = pos // 2, pos % 2
         for p in range(pairs):
             lanes = slice(half * width + p * pw, half * width + (p + 1) * pw)
-            gh_ref[:, lanes] = (mm(prob[p, half * own:(half + 1) * own, :], qaug[p], NT) * scale).astype(bf16)
-
-    key_grads(1)
-    left(out_moves)
-
-    def other_rows(i, carry):
-        at = pl.ds(pl.multiple_of(i * chunk, 16), chunk)
-        gml_ref[at, :] = (mm(dk_sib[at, :], wk_ref[...], NT) + mm(dv_sib[at, :], wv_ref[...], NT)).astype(bf16)
-        return carry
-
-    lax.fori_loop(0, nchunk, other_rows, 0)
-    e_copy = sems.copy(gml_ref, erecv, sibling)
-    e_copy.start()
-    turn(2, 3)
-    key_grads(0)
-    turn(0, 1, 2, 3)
-    split(mm(n_ref[0:own, :], dk_own[...], TN) + mm(n_ref[own:rows, :], dk_sib[...], TN),
-          width, starts[4] // 2, sends[4], 0)
-    turn(4)
-
-    def own_rows(i, carry):
-        at = pl.ds(pl.multiple_of(i * chunk, 16), chunk)
-        s_ref[pl.ds(pl.multiple_of(own + i * chunk, 16), chunk), :] = (
-            mm(att[at, :], wq_ref[...], NT) + mm(dk_own[at, :], wk_ref[...], NT) + mm(dv_own[at, :], wv_ref[...], NT)
-        )
-        return carry
-
-    lax.fori_loop(0, nchunk, own_rows, 0)
-    turn(4)
-    e_copy.wait()
-
-    moves = [back_copy(0, backr, 1), back_copy(1, backr, 1)]
+            gh_ref[k * chunk:(k + 1) * chunk, lanes] = (
+                mm(prob[p, pos * chunk:(pos + 1) * chunk, :], qaug[p], NT) * scale).astype(bf16)
+
+    e_copies = []
+    back_moves = [back_copy(0, backr, 1), back_copy(1, backr, 1)]
     sums = (zero, zero)
     for k in range(2):
         at = slice(k * chunk, (k + 1) * chunk)
+        key_grads(2 + k)
+        gml_ref[at, :] = (mm(dk_sib[at, :], wk_ref[...], NT) + mm(dv_sib[at, :], wv_ref[...], NT)).astype(bf16)
+        e_copies.append(sems.copy(gml_ref.at[at], erecv.at[at], sibling))
+        e_copies[k].start()
+        key_grads(k)
+        if k == 0:
+            turn(2, 3)
+        else:
+            acc[kept[4]:kept[4] + width, :] = mm(n_ref[0:own, :], dk_own[...], TN) + mm(n_ref[own:rows, :], dk_sib[...], TN)
+            turn(4, 0, 1, 3)
+        e = mm(att[at, :], wq_ref[...], NT) + mm(dk_own[at, :], wk_ref[...], NT) + mm(dv_own[at, :], wv_ref[...], NT)
         n, rstd = norm_parts(xall[k].astype(f32))
-        e = s_ref[own + k * chunk:own + (k + 1) * chunk, :] + erecv[at, :].astype(f32)
+        e_copies[k].wait()
+        e = e + erecv[at, :].astype(f32)
         stage[k] = (s_ref[at, :] + norm_back(e * gain, n, rstd)).astype(bf16)
         sums = (sums[0] + colsum(e * n), sums[1] + colsum(e))
-        if k:
-            moves[1].start()
-        else:
-            @pl.when(jnp.logical_not(stay))
-            def _():
-                moves[0].start()
-
-            @pl.when(stay)
-            def _():
-                backr[lax.rem(seq, 2)] = stage[0]
+        send_block(back_moves[k], k, backr, 1)
     small_ref[ups:ups + 1, :] = sums[0]
     small_ref[ups + 1:ups + 2, :] = sums[1]
     small_ref[ups + 2:, :] = jnp.zeros((small_ref.shape[0] - ups - 2, width), f32)
-    steps.append(small_steps(sems, stages, small_ref, ssend, srecv))
+    steps.append(small_steps(sems, stages_flat, small_ref, ssend, srecv, write_small))
+    turn(5)
+    turn(4, 5, 3, 2)
+    turn(4, 5, 0, 1)
+    turn(4, 0, 1)
     for _ in range(len(stages) * 2):
-        turn(5, 0, 1, 2, 3, 4)
-    left(moves)
+        turn(5, 4, 0, 1, 2, 3)
+    left_home(back_moves, backr, 1)
     home_again(outr, 0)
     home_again(backr, 1)
+    for copy in written:
+        copy.wait()
 
 
 def unpack_kernel(cot_hbm, outr_hbm, backr_hbm, gat_hbm, small_hbm, *refs):
-    outs, (cot_ref, outr, backr, gat, small, sems) = refs[:15], refs[15:]
-    (out, xg, ag, as_, wq, wk, wv, wo, ob, mg, ms, wu, ub, wd, db) = outs
-    copies = [
-        pltpu.make_async_copy(src, dst, sems.at[k])
+    hbm, vec_hbm, vec = refs[:8], refs[8:15], refs[15:22]
+    cot_ref, outr, backr, gat, small, out, xg, wide, up, sq, in_sems, out_sems = refs[22:]
+    out_hbm, xg_hbm, wq_hbm, wk_hbm, wv_hbm, wo_hbm, wu_hbm, wd_hbm = hbm
+    ag, as_, ob, mg, ms, ub, db = vec
+    _, tok, width = cot_ref.shape
+    ff = wide.shape[0]
+    cuts = ((0, ff), (ff, 2 * ff), (2 * ff, 2 * ff + 4 * width))
+    ins = [
+        pltpu.make_async_copy(src, dst, in_sems.at[k])
         for k, (src, dst) in enumerate(
-            ((gat_hbm, gat), (outr_hbm, outr), (backr_hbm, backr), (cot_hbm, cot_ref), (small_hbm, small)))
+            [(gat_hbm.at[a:b], gat.at[a:b]) for a, b in cuts]
+            + [(outr_hbm, outr), (backr_hbm, backr), (cot_hbm, cot_ref), (small_hbm, small)])
     ]
-    for cp in copies:
+    for cp in ins:
         cp.start()
-    _, tok, width = cot_ref.shape
-    ff = wd.shape[0]
-    half = width // 2
-    copies[0].wait()
-    wd[...] = gat[0:ff, :].astype(f32)
+    outs = []
+
+    def put(src, dst):
+        cp = pltpu.make_async_copy(src, dst, out_sems.at[len(outs)])
+        cp.start()
+        outs.append(cp)
+
+    ins[0].wait()
+    wide[...] = gat[0:ff, :].astype(f32)
+    put(wide, wd_hbm)
+    ins[1].wait()
     for j in range(ff // width):
-        wu[:, j * width:(j + 1) * width] = gat[ff + j * width:ff + (j + 1) * width, :].astype(f32)
-    for j, ref in enumerate((wo, wv)):
-        at = 2 * ff + j * half
-        ref[0:half, :] = gat[at:at + half, :].astype(f32)
-        ref[half:width, :] = gat[at + width:at + width + half, :].astype(f32)
-    for j, ref in enumerate((wq, wk)):
-        at = 2 * ff + (2 + j) * width
-        ref[...] = gat[at:at + width, :].astype(f32)
-    copies[1].wait()
+        up[:, j * width:(j + 1) * width] = gat[ff + j * width:ff + (j + 1) * width, :].astype(f32)
+    put(up, wu_hbm)
+    ins[4].wait()
+    ins[5].wait()
+    xg[...] = cot_ref[...] + backr[:, 0:tok, :].astype(f32)
+    put(xg, xg_hbm)
+    ins[2].wait()
+    for j, dst in enumerate((wo_hbm, wv_hbm, wq_hbm, wk_hbm)):
+        at = 2 * ff + j * width
+        sq[j] = gat[at:at + width, :].astype(f32)
+        put(sq.at[j], dst)
+    ins[3].wait()
     out[...] = outr[:, 0:tok, :]
-    copies[2].wait()
-    copies[3].wait()
-    xg[...] = cot_ref[...] + backr[:, 0:tok, :].astype(f32)
-    copies[4].wait()
+    put(out, out_hbm)
+    ins[6].wait()
     for j in range(ff // width):
         ub[0:1, j * width:(j + 1) * width] = small[4 + j:5 + j, :]
     ups = 4 + ff // width
     for j, ref in ((0, db), (1, ob), (2, mg), (3, ms), (ups, ag), (ups + 1, as_)):
         ref[...] = small[j:j + 1, :]
+    for src, dst in zip(vec, vec_hbm):
+        put(src, dst)
+    for cp in outs:
+        cp.wait()
 
 
 def body(nctx, seqs, layer_input, gene_kept, attn_gain, attn_shift, w_query, w_key, w_value, w_out, out_bias,
@@ -655,11 +711,9 @@
     pw = width // 2
     grad_rows = 2 * ff + 4 * width
     sets = (ff, ff, 2 * width, width, width)
-    landing = sum(landing_rows(r, nbits, seqs) for r in sets)
-    peers = 1 + sum((1 << len(range(b, min(b + 2, nbits)))) - 1 for b in range(1, nbits, 2)) + seqs - 1
-    sets = (ff, ff, 2 * width, width, width)
-    landing = sum(landing_rows(r, nbits, seqs) for r in sets)
-    peers = 1 + sum((1 << len(range(b, min(b + 2, nbits)))) - 1 for b in range(1, nbits, 2)) + seqs - 1
+    halved = (True, True, False, False, False)
+    landing = sum(landing_rows(r, nbits, seqs, h) for r, h in zip(sets, halved))
+    peers = sum((1 << len(bits)) - 1 for bits in bit_groups(nbits, min(nbits, 3))) + seqs - 1
     ncopy = 8 + (2 * len(sets) + 1) * peers
     home = jax.ShapeDtypeStruct((copies, tokp, width), bf16)
     outr, backr, gat, small = pl.pallas_call(
@@ -669,9 +723,12 @@
             jax.ShapeDtypeStruct((grad_rows, width), bf16),
             jax.ShapeDtypeStruct((16, width), f32),
         ),
-        in_specs=[vmem, vmem, hbm] + [vmem] * 13,
-        out_specs=(vmem,) * 4,
+        in_specs=[hbm, vmem, hbm] + [vmem] * 13,
+        out_specs=(hbm,) * 4,
         scratch_shapes=[
+            pltpu.VMEM((grad_rows, width), bf16),
+            pltpu.VMEM((16, width), f32),
+            pltpu.VMEM(layer_input.shape, bf16),
             pltpu.VMEM((copies, tokp, width), bf16),
             pltpu.VMEM((4, tokp, width), bf16),
             pltpu.VMEM((copies, tokp, width), bf16),
@@ -695,11 +752,11 @@
             pltpu.VMEM((pairs, 16, cols), bf16),
             pltpu.VMEM((own, width), bf16),
             pltpu.VMEM((rows - grad_rows // 2, TILE), f32),
-            pltpu.VMEM((grad_rows // 2, width), f32),
+            pltpu.VMEM((grad_rows - ff, width), f32),
             pltpu.VMEM((landing, width), bf16),
             pltpu.VMEM((nbits + 1, 16, width), bf16),
             pltpu.VMEM((peers, 16, width), bf16),
-            pltpu.SemaphoreType.DMA,
+            pltpu.SemaphoreType.DMA((10,)),
             pltpu.SemaphoreType.DMA((ncopy,)),
             pltpu.SemaphoreType.DMA((ncopy,)),
             pltpu.SemaphoreType.DMA((4,)),
@@ -711,24 +768,28 @@
       w_out, out_bias, mlp_gain, mlp_shift, w_up, up_bias, w_down, down_bias)
     line = jax.ShapeDtypeStruct((1, width), f32)
     square = jax.ShapeDtypeStruct((width, width), f32)
-    outs = pl.pallas_call(
+    whole = [
+        jax.ShapeDtypeStruct((copies, tok, width), bf16), jax.ShapeDtypeStruct((copies, tok, width), f32),
+        square, square, square, square, jax.ShapeDtypeStruct((width, ff), f32), jax.ShapeDtypeStruct((ff, width), f32),
+    ]
+    rows_out = [line, line, line, line, line, jax.ShapeDtypeStruct((1, ff), f32), line]
+    out, xg, wq, wk, wv, wo, wu, wd, ag, as_, ob, mg, ms, ub, db = pl.pallas_call(
         unpack_kernel,
-        out_shape=(
-            jax.ShapeDtypeStruct((copies, tok, width), bf16), jax.ShapeDtypeStruct((copies, tok, width), f32),
-            line, line, square, square, square, square, line, line, line,
-            jax.ShapeDtypeStruct((width, ff), f32), jax.ShapeDtypeStruct((1, ff), f32),
-            jax.ShapeDtypeStruct((ff, width), f32), line,
-        ),
+        out_shape=tuple(whole + rows_out),
         in_specs=[hbm] * 5,
-        out_specs=(vmem,) * 15,
-        scratch_shapes=[
+        out_specs=(hbm,) * 15,
+        scratch_shapes=[pltpu.VMEM(v.shape, f32) for v in rows_out] + [
             pltpu.VMEM(cotangent.shape, f32), pltpu.VMEM(home.shape, bf16), pltpu.VMEM(home.shape, bf16),
-            pltpu.VMEM((grad_rows, width), bf16), pltpu.VMEM((16, width), f32), pltpu.SemaphoreType.DMA((5,)),
+            pltpu.VMEM((grad_rows, width), bf16), pltpu.VMEM((16, width), f32),
+            pltpu.VMEM(layer_input.shape, bf16), pltpu.VMEM(cotangent.shape, f32), pltpu.VMEM((ff, width), f32),
+            pltpu.VMEM((width, ff), f32), pltpu.VMEM((4, width, width), f32),
+            pltpu.SemaphoreType.DMA((7,)), pltpu.SemaphoreType.DMA((15,)),
         ],
         compiler_params=pltpu.CompilerParams(vmem_limit_bytes=63 * 2**20),
         name="unpack",
     )(cotangent, outr, backr, gat, small)
-    return tuple(o.reshape(-1) if o.shape[0] == 1 else o for o in outs)
+    ag, as_, ob, mg, ms, ub, db = (v.reshape(-1) for v in (ag, as_, ob, mg, ms, ub, db))
+    return out, xg, ag, as_, wq, wk, wv, wo, ob, mg, ms, wu, ub, wd, db
 
 
 def solution(mesh):

time: 109 us -> 102 us (0.936)
  Pallas kernels: 108 us -> 101 us
    pallas_call x1, Pallas kernels: 104 us -> 96.8 us  [body(): pl.pallas_call(partial(layer_kernel, nbits, seqs), out_shape=(home, home,...]
where the time goes in v5:
time: 102 us
  Pallas kernels  101 us (99%)
    pallas_call x1, Pallas kernels, body(): pl.pallas_call(partial(layer_kernel, nbits, seqs), out_shape=(home, home,...  96.8 us
    pallas_call x1, Pallas kernels, body(): pl.pallas_call(unpack_kernel, out_shape=tuple(whole + rows_out), in_specs...  3.98 us

profile of v5, /device:TPU:0, one launch (start us, length us, event | category | flops | bytes accessed | tf_op | source)
XLA Modules:
  0.0 101.6 jit_solution(13049340358027993643)
XLA Ops:
  0.7 96.8 %layer.1 = (bf16[2,560,256]{2,1,0:T(8,128)(2,1)}, bf16[2,560,256]{2,1,0:T(8,128)(2,1)}, bf16[3072,256]{1,0:T(8,128)(2,1)}, f32[16,256]{1,0:T(8,128)}) custom-call(bf16[2,552,256]{2,1,0:T(8,128)(2,1)} %xin_hbm.1, s32[2,2208]{1,0:T(2,128)} %kept_ref.1, f32[1104,256]{1,0:T(8,128)} %bitcast.8, bf16[256]{0:T(256)(128)(2,1)} %ag_ref.1, bf16[256]{0:T(256)(128)(2,1)} %as_ref.1, ...), custom_call_target="tpu_custom_call" | custom-call | tf_op jit(solution)/shard_map/layer/pallas_call | solution.py:719
  97.5 4.0 %unpack.1 = (bf16[2,552,256]{2,1,0:T(8,128)(2,1)}, f32[2,552,256]{2,1,0:T(8,128)}, f32[256,256]{1,0:T(8,128)}, f32[256,256]{1,0:T(8,128)}, f32[256,256]{1,0:T(8,...) custom-call(f32[2,552,256]{2,1,0:T(8,128)} %cot_hbm.1, ...), custom_call_target="tpu_custom_call" | custom-call | tf_op jit(solution)/shard_map/unpack/pallas_call | solution.py:776

commit v6 on v5

--- a/solution.py
+++ b/solution.py
@@ -106,7 +106,7 @@
     return values[0]
 
 
-def reduce_steps(sems, stages, rows, acc, acc0, send, recv, recv0, gat, gat0, split_first, done):
+def reduce_steps(sems, stages, rows, acc, acc0, send, recv, recv0, gat, gat_hbm, gat0, split_first, write):
     into = recv0
     path = []
     if split_first:
@@ -154,15 +154,17 @@
         else:
             acc[held(off, size), :] = add_in_pairs([send[pl.ds(0, size), :].astype(f32)] + got, order)
     gat[pl.ds(pl.multiple_of(gat0 + off, 16), size), :] = acc[held(off, size), :].astype(bf16)
-    for others, off, size in reversed(path):
+    for k, (others, off, size) in reversed(list(enumerate(path))):
         at = pl.ds(pl.multiple_of(gat0 + off, 16), size)
-        cps = [sems.copy(gat.at[at], gat.at[at], device) for device, _ in others]
+        into = gat if k else gat_hbm
+        cps = [sems.copy(gat.at[at], into.at[at], device) for device, _ in others]
         for cp in cps:
             cp.start()
+        if k == 0:
+            write(gat.at[at], gat_hbm.at[at])
         yield
         for cp in cps:
             cp.wait()
-    done()
 
 
 def landing_rows(rows, nbits, seqs, split_first):
@@ -447,35 +449,47 @@
     for j in range(ff // width):
         small_ref[4 + j:5 + j, :] = sums[0][:, j * width:(j + 1) * width]
 
-    def back_copy(k, dst, sem):
+    cut_at = up16(chunk // 2)
+    spans = ((0, cut_at), (cut_at, chunk - cut_at))
+
+    def back_copy(k, dst, sem, part):
         b = lax.rem(seq, 2)
+        at = pl.ds(*spans[part])
         return pltpu.make_async_remote_copy(
-            src_ref=stage.at[k], dst_ref=dst.at[b], send_sem=ret_send.at[2 * sem + k], recv_sem=ret_recv.at[2 * sem + b],
+            src_ref=stage.at[k, at], dst_ref=dst.at[b, at],
+            send_sem=ret_send.at[4 * sem + 2 * part + k], recv_sem=ret_recv.at[4 * sem + 2 * part + b],
             device_id=(group + seq // 2, 2 * cc + lax.rem(seq + k, 2)), device_id_type=MESH)
 
-    def send_block(move, k, dst, sem):
+    def own_copy(dst, sem):
+        return pltpu.make_async_copy(stage.at[0], dst.at[lax.rem(seq, 2)], local_sems.at[2 + sem])
+
+    def send_block(moves, k, dst, sem, parts=(0, 1)):
         if k:
-            move.start()
+            for part in parts:
+                moves[k][part].start()
             return
 
         @pl.when(jnp.logical_not(stay))
         def _():
-            move.start()
+            for part in parts:
+                moves[k][part].start()
 
         @pl.when(stay)
         def _():
-            pltpu.make_async_copy(stage.at[0], dst.at[lax.rem(seq, 2)], local_sems.at[2 + sem]).start()
+            own_copy(dst, sem).start()
 
     def left_home(moves, dst, sem):
-        moves[1].wait_send()
+        for move in moves[1]:
+            move.wait_send()
 
         @pl.when(jnp.logical_not(stay))
         def _():
-            moves[0].wait_send()
+            for move in moves[0]:
+                move.wait_send()
 
         @pl.when(stay)
         def _():
-            pltpu.make_async_copy(stage.at[0], dst.at[lax.rem(seq, 2)], local_sems.at[2 + sem]).wait()
+            own_copy(dst, sem).wait()
 
     def home_again(dst, sem):
         for b in range(2):
@@ -483,13 +497,15 @@
 
             @pl.when(jnp.logical_not(here))
             def _():
-                pltpu.make_async_remote_copy(
-                    src_ref=stage.at[b], dst_ref=dst.at[b], send_sem=ret_send.at[2 * sem + b],
-                    recv_sem=ret_recv.at[2 * sem + b], device_id=sibling, device_id_type=MESH).wait_recv()
-
-    out_moves = [back_copy(0, outr, 0), back_copy(1, outr, 0)]
+                for part in range(2):
+                    at = pl.ds(*spans[part])
+                    pltpu.make_async_remote_copy(
+                        src_ref=stage.at[b, at], dst_ref=dst.at[b, at], send_sem=ret_send.at[4 * sem + 2 * part + b],
+                        recv_sem=ret_recv.at[4 * sem + 2 * part + b], device_id=sibling, device_id_type=MESH).wait_recv()
+
+    out_moves = [[back_copy(k, outr, 0, part) for part in range(2)] for k in range(2)]
     for k in range(2):
-        send_block(out_moves[k], k, outr, 0)
+        send_block(out_moves, k, outr, 0)
 
     sets = (ff, ff, 2 * width, width, width)
     halved = (True, True, False, False, False)
@@ -503,9 +519,8 @@
         gh_ref.at[:, 2 * width:3 * width], gh_ref.at[0:own // 2, 3 * width:4 * width], gh_ref.at[own // 2:own, 3 * width:4 * width])
     written = []
 
-    def write_out(j):
-        at = pl.ds(starts[j], sets[j])
-        copy = pltpu.make_async_copy(gat.at[at], gat_hbm.at[at], local_sems.at[4 + j])
+    def write_out(j, src, dst):
+        copy = pltpu.make_async_copy(src, dst, local_sems.at[4 + j])
         copy.start()
         written.append(copy)
 
@@ -516,7 +531,7 @@
 
     steps = [
         reduce_steps(
-            sems, stages if halved[j] else stages_flat, sets[j], acc, kept[j], sends[j], recv, lands[j], gat, starts[j],
+            sems, stages if halved[j] else stages_flat, sets[j], acc, kept[j], sends[j], recv, lands[j], gat, gat_hbm, starts[j],
             halved[j], partial(write_out, j))
         for j in range(5)
     ]
@@ -562,29 +577,25 @@
     dk_own, dk_sib = gh_ref.at[:, 0:width], gh_ref.at[:, width:2 * width]
     acc[kept[2] + width:kept[2] + 2 * width, :] = mm(n_ref[0:own, :], dv_own[...], TN) + mm(n_ref[own:rows, :], dv_sib[...], TN)
     turn(2)
-    wide = 3 * TILE
-    nothing = jnp.zeros((pw - 16, wide), bf16)
-
-    def backward(i, carry):
-        p = i // 3
-        at = pl.ds(pl.multiple_of((i % 3) * wide, TILE), wide)
-        right = jnp.concatenate([gaug[p, :, at], dext[p, :, at], nothing], axis=0)
-        total = None
-        for a, b in bounds:
-            ds = prob[p, a:b, at] * mm(vaug[p, a:b, :], right).astype(bf16)
-            prob[p, a:b, at] = ds
-            part = mm(kt[pl.ds(pl.multiple_of(p * pw, pw), pw), a:b], ds)
-            total = part if total is None else total + part
-        ot_ref[p, :, at] = total * scale
-        return carry
-
-    lax.fori_loop(0, 1, backward, 0)
+    nothing = jnp.zeros((pw - 16, cols), bf16)
+
+    def backward(p, c):
+        a, b = bounds[c]
+        right = jnp.concatenate([gaug[p], dext[p], nothing], axis=0)
+        ds = prob[p, a:b, :] * mm(vaug[p, a:b, :], right).astype(bf16)
+        prob[p, a:b, :] = ds
+        part = mm(kt[p * pw:(p + 1) * pw, a:b], ds) * scale
+        ot_ref[p] = ot_ref[p] + part if c else part
+
+    backward(0, 0)
     turn(0, 1)
-    lax.fori_loop(1, 4, backward, 0)
+    backward(0, 1)
+    backward(0, 2)
+    backward(1, 0)
     turn(2)
-    lax.fori_loop(4, 5, backward, 0)
+    backward(1, 1)
     turn(0, 1)
-    lax.fori_loop(5, 6, backward, 0)
+    backward(1, 2)
     for p in range(pairs):
         for h in range(2):
             att_t[p * pw + h * hd:p * pw + (h + 1) * hd, :] = ot_ref[
@@ -602,8 +613,13 @@
             gh_ref[k * chunk:(k + 1) * chunk, lanes] = (
                 mm(prob[p, pos * chunk:(pos + 1) * chunk, :], qaug[p], NT) * scale).astype(bf16)
 
+    def key_weight(k):
+        at = slice(k * chunk, (k + 1) * chunk)
+        beyond = slice(own + k * chunk, own + (k + 1) * chunk)
+        return mm(n_ref[at, :], dk_own[at, :], TN) + mm(n_ref[beyond, :], dk_sib[at, :], TN)
+
     e_copies = []
-    back_moves = [back_copy(0, backr, 1), back_copy(1, backr, 1)]
+    back_moves = [[back_copy(k, backr, 1, part) for part in range(2)] for k in range(2)]
     sums = (zero, zero)
     for k in range(2):
         at = slice(k * chunk, (k + 1) * chunk)
@@ -613,25 +629,28 @@
         e_copies[k].start()
         key_grads(k)
         if k == 0:
-            turn(2, 3)
+            acc[kept[4]:kept[4] + width, :] = key_weight(k)
+            turn(0, 1, 2, 3)
         else:
-            acc[kept[4]:kept[4] + width, :] = mm(n_ref[0:own, :], dk_own[...], TN) + mm(n_ref[own:rows, :], dk_sib[...], TN)
-            turn(4, 0, 1, 3)
+            acc[kept[4]:kept[4] + width, :] += key_weight(k)
+            turn(4, 3)
         e = mm(att[at, :], wq_ref[...], NT) + mm(dk_own[at, :], wk_ref[...], NT) + mm(dv_own[at, :], wv_ref[...], NT)
         n, rstd = norm_parts(xall[k].astype(f32))
         e_copies[k].wait()
         e = e + erecv[at, :].astype(f32)
         stage[k] = (s_ref[at, :] + norm_back(e * gain, n, rstd)).astype(bf16)
         sums = (sums[0] + colsum(e * n), sums[1] + colsum(e))
-        send_block(back_moves[k], k, backr, 1)
+        send_block(back_moves, k, backr, 1, (0,) if k else (0, 1))
     small_ref[ups:ups + 1, :] = sums[0]
     small_ref[ups + 1:ups + 2, :] = sums[1]
     small_ref[ups + 2:, :] = jnp.zeros((small_ref.shape[0] - ups - 2, width), f32)
     steps.append(small_steps(sems, stages_flat, small_ref, ssend, srecv, write_small))
     turn(5)
-    turn(4, 5, 3, 2)
-    turn(4, 5, 0, 1)
-    turn(4, 0, 1)
+    turn(4)
+    send_block(back_moves, 1, backr, 1, (1,))
+    turn(0, 1, 2, 5, 3)
+    turn(4, 0, 1, 5)
+    turn(4)
     for _ in range(len(stages) * 2):
         turn(5, 4, 0, 1, 2, 3)
     left_home(back_moves, backr, 1)
@@ -759,8 +778,8 @@
             pltpu.SemaphoreType.DMA((10,)),
             pltpu.SemaphoreType.DMA((ncopy,)),
             pltpu.SemaphoreType.DMA((ncopy,)),
-            pltpu.SemaphoreType.DMA((4,)),
-            pltpu.SemaphoreType.DMA((4,)),
+            pltpu.SemaphoreType.DMA((8,)),
+            pltpu.SemaphoreType.DMA((8,)),
         ],
         compiler_params=pltpu.CompilerParams(collective_id=1, has_side_effects=True, vmem_limit_bytes=63 * 2**20),
         name="layer",

time: 102 us -> 99.3 us (0.974)
  Pallas kernels: 101 us -> 98.3 us
    pallas_call x1, Pallas kernels: 96.8 us -> 94.3 us  [body(): pl.pallas_call(partial(layer_kernel, nbits, seqs), out_shape=(home, home,...]
where the time goes in v6:
time: 99.3 us; the launch traced here: 99.1 us
  Pallas kernels  98.3 us (99%)
    pallas_call x1, Pallas kernels, body(): pl.pallas_call(partial(layer_kernel, nbits, seqs), out_shape=(home, home,...  94.3 us
    pallas_call x1, Pallas kernels, body(): pl.pallas_call(unpack_kernel, out_shape=tuple(whole + rows_out), in_specs...  3.98 us

profile of v6, /device:TPU:0, one launch (start us, length us, event | category | flops | bytes accessed | tf_op | source)
XLA Modules:
  0.0 99.1 jit_solution(3026922501364335409)
XLA Ops:
  0.7 94.3 %layer.1 = (bf16[2,560,256]{2,1,0:T(8,128)(2,1)}, bf16[2,560,256]{2,1,0:T(8,128)(2,1)}, bf16[3072,256]{1,0:T(8,128)(2,1)}, f32[16,256]{1,0:T(8,128)}) custom-call(bf16[2,552,256]{2,1,0:T(8,128)(2,1)} %xin_hbm.1, s32[2,2208]{1,0:T(2,128)} %kept_ref.1, f32[1104,256]{1,0:T(8,128)} %bitcast.8, bf16[256]{0:T(256)(128)(2,1)} %ag_ref.1, bf16[256]{0:T(256)(128)(2,1)} %as_ref.1, ...), custom_call_target="tpu_custom_call" | custom-call | tf_op jit(solution)/shard_map/layer/pallas_call | solution.py:738
  95.0 4.0 %unpack.1 = (bf16[2,552,256]{2,1,0:T(8,128)(2,1)}, f32[2,552,256]{2,1,0:T(8,128)}, f32[256,256]{1,0:T(8,128)}, f32[256,256]{1,0:T(8,128)}, f32[256,256]{1,0:T(8,...) custom-call(f32[2,552,256]{2,1,0:T(8,128)} %cot_hbm.1, ...), custom_call_target="tpu_custom_call" | custom-call | tf_op jit(solution)/shard_map/unpack/pallas_call | solution.py:795

commit v7 on v6

--- a/solution.py
+++ b/solution.py
@@ -199,15 +199,15 @@
 
 def layer_kernel(
     nbits, seqs,
-    xin_hbm, kept_ref, cot_hbm,
+    xin, kept_ref, cot_hbm,
     ag_ref, as_ref, wq_ref, wk_ref, wv_ref, wo_ref, ob_ref,
     mg_ref, ms_ref, wu_ref, ub_ref, wd_ref, db_ref,
     outr, backr, gat_hbm, small_hbm,
-    gat, small_ref, xin, stage, xall, cotr, marks, n_ref, qaug, kaug, vaug, kt, vtaug, prob, s_ref, ot_ref, rl_ref,
+    gat, small_ref, stage, xall, cotr, marks, n_ref, qaug, kaug, vaug, kt, vtaug, prob, s_ref, ot_ref, rl_ref,
     att_t, att, act_ref, gh_ref, gml_ref, gaug, dext, erecv, s_more, acc, recv, ssend, srecv,
     local_sems, send_sems, recv_sems, ret_send, ret_recv,
 ):
-    copies, tok, width = xin_hbm.shape
+    copies, tok, width = xin.shape
     tokp = xall.shape[1]
     own = 2 * tokp
     rows = 2 * own
@@ -230,8 +230,6 @@
     sibling = (group + 1 - cc, seq)
     stay = seq // 2 == cc
 
-    keep_in = pltpu.make_async_copy(xin_hbm, xin, local_sems.at[0])
-    keep_in.start()
     cot_in = pltpu.make_async_copy(cot_hbm, s_ref.at[pl.ds(0, 2 * tok)], local_sems.at[1])
     cot_in.start()
 
@@ -259,7 +257,6 @@
             [usable[:, sh * tok:(sh + 1) * tok], jnp.full((1, wide - tok), MASKED, f32)], axis=1)
         marks[0, sh] = jnp.where(sub == 0, piece, 0.0).astype(bf16)
     stage[:, tokp - 16:tokp, :] = jnp.zeros((copies, 16, width), bf16)
-    keep_in.wait()
     stage[:, 0:tok, :] = xin[...]
 
     def out_copy(k, dst):
@@ -382,7 +379,7 @@
         total = None
         for c, (a, b) in enumerate(bounds):
             if ahead is not None:
-                tops.append(score(lax.rem(t + 1, count), ahead, c))
+                tops.append(score(t + 1, ahead, c))
             weights = jnp.exp2((scores[c][...] - top) * expo).astype(bf16)
             prob[p, a:b, at] = weights
             part = mm(vtaug[p, :, a:b], weights)
@@ -390,13 +387,15 @@
         rl = 1.0 / total[pw:pw + 1]
         ot_ref[p, :, at] = total[0:pw] * rl
         rl_ref[p, :, at] = rl
-        return jnp.maximum(jnp.maximum(tops[0], tops[1]), tops[2])
+        return jnp.maximum(jnp.maximum(tops[0], tops[1]), tops[2]) if tops else None
 
     def forward(i, top):
         return weigh(2 * i + 1, odd, weigh(2 * i, even, top, odd), even)
 
     tops = [score(0, even, c) for c in range(3)]
-    lax.fori_loop(0, count // 2, forward, jnp.maximum(jnp.maximum(tops[0], tops[1]), tops[2]))
+    top = lax.fori_loop(0, count // 2 - 1, forward, jnp.maximum(jnp.maximum(tops[0], tops[1]), tops[2]))
+    top = weigh(count - 2, even, top, odd)
+    weigh(count - 1, odd, top, None)
     for p in range(pairs):
         for h in range(2):
             att_t[p * pw + h * hd:p * pw + (h + 1) * hd, :] = ot_ref[
@@ -662,8 +661,8 @@
 
 def unpack_kernel(cot_hbm, outr_hbm, backr_hbm, gat_hbm, small_hbm, *refs):
     hbm, vec_hbm, vec = refs[:8], refs[8:15], refs[15:22]
-    cot_ref, outr, backr, gat, small, out, xg, wide, up, sq, in_sems, out_sems = refs[22:]
-    out_hbm, xg_hbm, wq_hbm, wk_hbm, wv_hbm, wo_hbm, wu_hbm, wd_hbm = hbm
+    cot_ref, outr, backr, gat, small, xg, wide, up, sq, in_sems, out_sems = refs[22:]
+    out, xg_hbm, wq_hbm, wk_hbm, wv_hbm, wo_hbm, wu_hbm, wd_hbm = hbm
     ag, as_, ob, mg, ms, ub, db = vec
     _, tok, width = cot_ref.shape
     ff = wide.shape[0]
@@ -701,7 +700,6 @@
         put(sq.at[j], dst)
     ins[3].wait()
     out[...] = outr[:, 0:tok, :]
-    put(out, out_hbm)
     ins[6].wait()
     for j in range(ff // width):
         ub[0:1, j * width:(j + 1) * width] = small[4 + j:5 + j, :]
@@ -742,12 +740,11 @@
             jax.ShapeDtypeStruct((grad_rows, width), bf16),
             jax.ShapeDtypeStruct((16, width), f32),
         ),
-        in_specs=[hbm, vmem, hbm] + [vmem] * 13,
+        in_specs=[vmem, vmem, hbm] + [vmem] * 13,
         out_specs=(hbm,) * 4,
         scratch_shapes=[
             pltpu.VMEM((grad_rows, width), bf16),
             pltpu.VMEM((16, width), f32),
-            pltpu.VMEM(layer_input.shape, bf16),
             pltpu.VMEM((copies, tokp, width), bf16),
             pltpu.VMEM((4, tokp, width), bf16),
             pltpu.VMEM((copies, tokp, width), bf16),
@@ -796,11 +793,11 @@
         unpack_kernel,
         out_shape=tuple(whole + rows_out),
         in_specs=[hbm] * 5,
-        out_specs=(hbm,) * 15,
+        out_specs=(vmem,) + (hbm,) * 14,
         scratch_shapes=[pltpu.VMEM(v.shape, f32) for v in rows_out] + [
             pltpu.VMEM(cotangent.shape, f32), pltpu.VMEM(home.shape, bf16), pltpu.VMEM(home.shape, bf16),
             pltpu.VMEM((grad_rows, width), bf16), pltpu.VMEM((16, width), f32),
-            pltpu.VMEM(layer_input.shape, bf16), pltpu.VMEM(cotangent.shape, f32), pltpu.VMEM((ff, width), f32),
+            pltpu.VMEM(cotangent.shape, f32), pltpu.VMEM((ff, width), f32),
             pltpu.VMEM((width, ff), f32), pltpu.VMEM((4, width, width), f32),
             pltpu.SemaphoreType.DMA((7,)), pltpu.SemaphoreType.DMA((15,)),
         ],

time: 99.3 us -> 96.9 us (0.976)
  Pallas kernels: 98.3 us -> 95.9 us
    pallas_call x1, Pallas kernels: 94.3 us -> 91.3 us  [body(): pl.pallas_call(partial(layer_kernel, nbits, seqs), out_shape=(home, home,...]
where the time goes in v7:
time: 96.9 us; the launch traced here: 96.7 us
  Pallas kernels  95.9 us (99%)
    pallas_call x1, Pallas kernels, body(): pl.pallas_call(partial(layer_kernel, nbits, seqs), out_shape=(home, home,...  91.3 us
    pallas_call x1, Pallas kernels, body(): pl.pallas_call(unpack_kernel, out_shape=tuple(whole + rows_out), in_specs...  4.6 us

profile of v7, /device:TPU:0, one launch (start us, length us, event | category | flops | bytes accessed | tf_op | source)
XLA Modules:
  0.0 96.7 jit_solution(784985200104914141)
XLA Ops:
  0.7 91.3 %layer.1 = (bf16[2,560,256]{2,1,0:T(8,128)(2,1)}, bf16[2,560,256]{2,1,0:T(8,128)(2,1)}, bf16[3072,256]{1,0:T(8,128)(2,1)}, f32[16,256]{1,0:T(8,128)}) custom-call(bf16[2,552,256]{2,1,0:T(8,128)(2,1)} %xin.1, s32[2,2208]{1,0:T(2,128)} %kept_ref.1, f32[1104,256]{1,0:T(8,128)} %bitcast.8, bf16[256]{0:T(256)(128)(2,1)} %ag_ref.1, bf16[256]{0:T(256)(128)(2,1)} %as_ref.1, ...), custom_call_target="tpu_custom_call" | custom-call | tf_op jit(solution)/shard_map/layer/pallas_call | solution.py:736
  91.9 4.6 %unpack.1 = (bf16[2,552,256]{2,1,0:T(8,128)(2,1)}, f32[2,552,256]{2,1,0:T(8,128)}, f32[256,256]{1,0:T(8,128)}, f32[256,256]{1,0:T(8,128)}, f32[256,256]{1,0:T(8,...) custom-call(f32[2,552,256]{2,1,0:T(8,128)} %cot_hbm.1, ...), custom_call_target="tpu_custom_call" | custom-call | tf_op jit(solution)/shard_map/unpack/pallas_call | solution.py:792
